TPU v7x, 256 devices: a whole 4x4x8 slice. The times are simulated.
256 devices in a mesh: slab: 16 (over x, y), cross: 16 (over z, core).
Axes of the slice: x: 4, y: 4, z: 8, core: 2. Of those that a mesh axis runs over, the one named last changes fastest.
Arguments:
- rhs: bfloat16 [16, 16, 32, 128, 128], P('slab', 'cross'), may hold values from -6 to 6
- m_blocks: bfloat16 [16, 16, 72, 3, 128, 128], P('slab', 'cross'), may hold values from -0.3125 to 0.3125
- m_cols: int32 [16, 16, 72, 3], P('slab', 'cross'), may hold values from 0 to 71, as said below
- j_blocks: bfloat16 [16, 16, 32, 3, 128, 128], P('slab', 'cross'), may hold values from -0.3125 to 0.3125
- j_cols: int32 [16, 16, 32, 3], P('slab', 'cross'), may hold values from 0 to 71, as said below
- send_list: int32 [16, 16, 16, 2], P('slab', 'cross'), may hold values from 0 to 31, as said below
- send_count: int32 [16, 16, 16], P('slab', 'cross'), may hold values from 0 to 2, as said below
Outputs:
- second_iterate: bfloat16 [16, 16, 32, 128, 128], P('slab', 'cross')
Inputs may be any that keep to these rules, and one draw needn't show every extreme that they name: `m_cols`: each row's first block column is the row itself; the others differ from it and from each other. `j_cols`: each row's first block column is the row itself; the others differ from it and from each other. `send_list`: the used slots of one list name different block rows. `send_count`: no subdomain lends rows to itself; in every slab index some subdomain receives 2 rows from each other one.
All inputs are finite; a program needn't handle non-finite values.
Results may differ from a plain program's by a relative error of at most 0.0058.
Values may be sent and summed in bfloat16 or wider, within the bound.
No kernel may reach another device: no remote copies, remote signals or barrier semaphores. Data moves between devices by JAX's collectives and lax.ppermute only.
A program may use at most 64 MiB of HBM per device.

v0:
```python
import jax
import jax.numpy as jnp
from jax import lax
from jax.sharding import PartitionSpec as P

OVL = 4


def extended_2(cells, sides, width):
    for axis, dim in sides:
        count = lax.axis_size(axis)
        ends = count - 1
        head = lax.slice_in_dim(cells, 0, width, axis=dim)
        tail = lax.slice_in_dim(cells, cells.shape[dim] - width, cells.shape[dim], axis=dim)
        cells = jnp.concatenate(
            [
                lax.ppermute(tail, axis, [(i, (i + 1) % count) for i in range(ends)]),
                cells,
                lax.ppermute(head, axis, [((i + 1) % count, i) for i in range(ends)]),
            ],
            axis=dim,
        )
    return cells


def route(buffer):
    return lax.all_to_all(buffer, "cross", split_axis=0, concat_axis=0, tiled=True)


def per_device(rhs, m_blocks, m_cols, j_blocks, j_cols, send_list, send_count):
    rhs_own = rhs[0, 0]
    inverse = m_blocks[0, 0]
    inverse_cols = m_cols[0, 0]
    jacobian = j_blocks[0, 0]
    jacobian_cols = j_cols[0, 0]
    targets = send_list[0, 0]
    counts = send_count[0, 0]
    owned = rhs_own.shape[0]
    block_size = rhs_own.shape[1]
    vectors = rhs_own.shape[2]
    peer_count = targets.shape[0]
    slot_count = targets.shape[1]
    valid = jnp.arange(slot_count, dtype=jnp.int32)[None, :] < counts[:, None]
    flat_targets = targets.reshape(-1)
    flat_valid = valid.reshape(-1)
    scatter_table = (
        (flat_targets[None, :] == jnp.arange(owned, dtype=jnp.int32)[:, None]) & flat_valid[None, :]
    ).astype(jnp.bfloat16)

    def extend(field):
        padded = extended_2(field, (("slab", 0),), OVL)
        outgoing = jnp.take(field, flat_targets, axis=0)
        outgoing = jnp.where(flat_valid[:, None, None], outgoing, jnp.zeros((), jnp.bfloat16))
        incoming = route(outgoing.reshape(peer_count, slot_count, block_size, vectors))
        return jnp.concatenate(
            [field, padded[:OVL], padded[owned + OVL :], incoming.reshape(-1, block_size, vectors)],
            axis=0,
        )

    def apply_set(blocks, columns, extended):
        picked = jnp.take(extended, columns, axis=0)
        return lax.dot_general(
            blocks, picked, (((1, 3), (1, 2)), ((0,), (0,))), preferred_element_type=jnp.float32
        )

    def precondition(field):
        extended = extend(field)
        partial_value = apply_set(inverse, inverse_cols, extended).astype(jnp.bfloat16)
        returned_slab = extended_2(partial_value[owned : owned + 2 * OVL], (("slab", 0),), OVL)
        cross_part = partial_value[owned + 2 * OVL :].reshape(
            peer_count, slot_count, block_size, vectors
        )
        returned_cross = route(cross_part).reshape(peer_count * slot_count, block_size * vectors)
        total = partial_value[:owned].astype(jnp.float32)
        total = total.at[:OVL].add(returned_slab[:OVL].astype(jnp.float32))
        total = total.at[owned - OVL :].add(returned_slab[3 * OVL :].astype(jnp.float32))
        added = jnp.dot(scatter_table, returned_cross, preferred_element_type=jnp.float32)
        return total + added.reshape(owned, block_size, vectors)

    first = precondition(rhs_own).astype(jnp.bfloat16)
    image = apply_set(jacobian, jacobian_cols, extend(first))
    residual = (rhs_own.astype(jnp.float32) - image).astype(jnp.bfloat16)
    second = (first.astype(jnp.float32) + precondition(residual)).astype(jnp.bfloat16)
    return second[None, None]


def solution(mesh):
    return jax.shard_map(
        per_device,
        mesh=mesh,
        in_specs=(
            P("slab", "cross", None, None, None),
            P("slab", "cross", None, None, None, None),
            P("slab", "cross", None, None),
            P("slab", "cross", None, None, None, None),
            P("slab", "cross", None, None),
            P("slab", "cross", None, None),
            P("slab", "cross", None),
        ),
        out_specs=P("slab", "cross", None, None, None),
        check_vma=False,
    )
```

profile of v0, /device:TPU:1, one launch (start us, length us, event | category | flops | bytes accessed | tf_op | source)
XLA Modules:
  0.0 261.8 jit_solution(4805908663318409949)
XLA Ops:
  1.1 2.3 copy.20
  4.2 2.9 %gather_fusion.1 = bf16[32,128,128]{1,2,0:T(8,128)(2,1)} fusion(bf16[32,128,128]{1,2,0:T(8,128)(2,1)} %bitcast.101, s32[1024]{0:T(1024)S(1)} %pad_clamp_fusion.2), kind=kCustom, calls=%fused_computation.clone | custom fusion | bytes 2097280 | tf_op jit(solution)/shard_map/jit(_take)/gather | solution.py:52
  7.0 2.4 select_select_fusion.2
  9.4 10.0 %all-to-all-start = ((bf16[16,2,128,128]{2,3,1,0:T(8,128)(2,1)}), bf16[16,2,128,128]{2,3,1,0:T(8,128)(2,1)}, u32[]{:S(2)}, u32[]{:S(2)}) async-start(bf16[16,2,128,128]{2,3,1,0:T(8,128)(2,1)} %bitcast.108), calls=%async_computation | async-start | bytes 2097152 | tf_op jit(solution)/shard_map/all_to_all | solution.py:27
  19.4 1.7 slice_bitcast_fusion.1
  21.1 3.2 %collective-permute-start = (bf16[4,128,128]{1,2,0:T(8,128)(2,1)}, bf16[4,128,128]{1,2,0:T(8,128)(2,1)S(1)}, u32[]{:S(2)}, u32[]{:S(2)}) collective-permute-start(bf16[4,128,128]{1,2,0:T(8,128)(2,1)} %get-tuple-element.67), channel_id=1, source_target_pairs={{0,16},{16,32},{32,48},{48,64},{64,80},{80,96},{96,112},{112,128},... | collective-permute-start | bytes 393224 | tf_op jit(solution)/shard_map/ppermute | solution.py:17
  27.4 3.8 %collective-permute-done.1 = bf16[4,128,128]{1,2,0:T(8,128)(2,1)S(1)} collective-permute-done((bf16[4,128,128]{1,2,0:T(8,128)(2,1)}, bf16[4,128,128]{1,2,0:T(8,128)(2,1)S(1)}, u32[]{:S(2)}, u32[]{:S(2)}) %collective-permute-start.1) | collective-permute-done | bytes 131104 | tf_op jit(solution)/shard_map/ppermute | solution.py:19
  31.2 16.3 %all-to-all-done = bf16[16,2,128,128]{2,3,1,0:T(8,128)(2,1)} async-done(((bf16[16,2,128,128]{2,3,1,0:T(8,128)(2,1)}), bf16[16,2,128,128]{2,3,1,0:T(8,128)(2,1)}, u32[]{:S(2)}, u32[]{:S(2)}) %all-to-all-start) | async-done | bytes 1048608 | tf_op jit(solution)/shard_map/all_to_all | solution.py:27
  47.5 3.3 %pad_maximum_fusion = bf16[72,128,128]{1,2,0:T(8,128)(2,1)} fusion(bf16[32,128,128]{1,2,0:T(8,128)(2,1)} %bitcast.5, bf16[4,128,128]{1,2,0:T(8,128)(2,1)S(1)} %collective-permute-done.1, bf16[4,128,128]{1,2,0:T(8,128)(2,1)S(1)} %collective-permute-done, bf16[32,128,128]{1,2,0:T(8,128)(2,1)} %bitcast.102), kind=kLoop, calls=%fused_computation.24 | loop fusion | flops 3538944 | bytes 4718592 | tf_op jit(solution)/shard_map/concatenate | solution.py:55
  50.8 9.9 %gather_fusion.2 = bf16[216,128,128]{1,2,0:T(8,128)(2,1)} fusion(bf16[72,128,128]{1,2,0:T(8,128)(2,1)} %pad_maximum_fusion, s32[1024]{0:T(1024)S(1)} %pad_clamp_fusion.1), kind=kCustom, calls=%fused_computation.1.clone | custom fusion | bytes 14156640 | tf_op jit(solution)/shard_map/jit(_take)/gather | solution.py:61
  60.7 8.1 %fusion.14 = bf16[72,128,128]{1,2,0:T(8,128)(2,1)S(1)} fusion(bf16[1,1,72,3,128,128]{5,4,3,2,1,0:T(8,128)(2,1)} %param.20, bf16[72,3,128,128]{2,3,1,0:T(8,128)(2,1)} %bitcast.104, pred[72,3]{1,0:T(8,128)(4,1)S(1)} %copy.19), kind=kOutput, calls=%fused_computation.22 | convolution fusion | flops 910688256 | bytes 16515288 | tf_op jit(solution)/shard_map/dot_general | solution.py:62
  68.8 2.1 fusion.54
  71.2 2.3 copy.25
  73.4 4.3 %all-to-all-start.1 = ((bf16[16,2,128,128]{3,2,1,0:T(8,128)(2,1)}), bf16[16,2,128,128]{3,2,1,0:T(8,128)(2,1)}, u32[]{:S(2)}, u32[]{:S(2)}) async-start(bf16[16,2,128,128]{3,2,1,0:T(8,128)(2,1)} %copy.25), calls=%async_computation.1 | async-start | bytes 2097152 | tf_op jit(solution)/shard_map/all_to_all | solution.py:27
  78.7 3.2 %collective-permute-start.2 = (bf16[4,128,128]{1,2,0:T(8,128)(2,1)S(1)}, bf16[4,128,128]{1,2,0:T(8,128)(2,1)S(1)}, u32[]{:S(2)}, u32[]{:S(2)}) collective-permute-start(bf16[4,128,128]{1,2,0:T(8,128)(2,1)S(1)} %get-tuple-element.62), channel_id=1, source_target_pairs={{0,16},{16,32},{32,48},{48,64},{64,80},{80,96},{96,112},{112,128},... | collective-permute-start | bytes 393224 | tf_op jit(solution)/shard_map/ppermute | solution.py:17
  83.2 2.0 collective-permute-done.2
  85.1 1.7 fusion.40
  86.8 2.4 collective-permute-done.3
  89.2 1.7 fusion.39
  90.9 14.1 %all-to-all-done.1 = bf16[16,2,128,128]{3,2,1,0:T(8,128)(2,1)} async-done(((bf16[16,2,128,128]{3,2,1,0:T(8,128)(2,1)}), bf16[16,2,128,128]{3,2,1,0:T(8,128)(2,1)}, u32[]{:S(2)}, u32[]{:S(2)}) %all-to-all-start.1) | async-done | bytes 1048608 | tf_op jit(solution)/shard_map/all_to_all | solution.py:27
  105.0 3.3 %fusion.34 = f32[32,128,128]{2,0,1:T(8,128)} fusion(s32[32]{0:T(128)S(1)} %reshape_squeeze.3, pred[32]{0:T(512)(128)(4,1)S(1)} %lt.63, bf16[4,8,128,128]{3,2,1,0:T(8,128)(2,1)} %bitcast.40), kind=kOutput, calls=%fused_computation.38 | convolution fusion | flops 33556480 | bytes 3145888 | tf_op jit(solution)/shard_map/dot_general | solution.py:77
  108.3 3.0 %copy.27 = f32[32,128,128]{1,2,0:T(8,128)} copy(f32[32,128,128]{2,0,1:T(8,128)} %fusion.34) | data formatting | bytes 4194304 | tf_op jit(solution)/shard_map/dot_general | solution.py:77
  111.3 3.6 %add_convert_fusion.1 = bf16[32,128,128]{1,2,0:T(8,128)(2,1)} fusion(f32[32,128,128]{1,2,0:T(8,128)} %fusion.39, f32[32,128,128]{1,2,0:T(8,128)} %copy.27), kind=kLoop, calls=%fused_computation.30 | loop fusion | flops 1048576 | bytes 5242880 | tf_op jit(solution)/shard_map/convert_element_type | solution.py:80
  114.9 2.9 %gather_fusion.3 = bf16[32,128,128]{1,2,0:T(8,128)(2,1)} fusion(bf16[32,128,128]{1,2,0:T(8,128)(2,1)} %add_convert_fusion.1, s32[1024]{0:T(1024)S(1)} %pad_clamp_fusion.2), kind=kCustom, calls=%fused_computation.2.clone | custom fusion | bytes 2097280 | tf_op jit(solution)/shard_map/jit(_take)/gather | solution.py:52
  117.8 2.4 select_select_fusion.1
  120.2 4.3 %all-to-all-start.2 = ((bf16[16,2,128,128]{2,3,1,0:T(8,128)(2,1)}), bf16[16,2,128,128]{2,3,1,0:T(8,128)(2,1)}, u32[]{:S(2)}, u32[]{:S(2)}) async-start(bf16[16,2,128,128]{2,3,1,0:T(8,128)(2,1)} %bitcast.109), calls=%async_computation.2 | async-start | bytes 2097152 | tf_op jit(solution)/shard_map/all_to_all | solution.py:27
  126.7 3.2 %collective-permute-start.4 = (bf16[4,128,128]{1,2,0:T(8,128)(2,1)}, bf16[4,128,128]{1,2,0:T(8,128)(2,1)S(1)}, u32[]{:S(2)}, u32[]{:S(2)}) collective-permute-start(bf16[4,128,128]{1,2,0:T(8,128)(2,1)} %get-tuple-element.65), channel_id=1, source_target_pairs={{0,16},{16,32},{32,48},{48,64},{64,80},{80,96},{96,112},{112,128},... | collective-permute-start | bytes 393224 | tf_op jit(solution)/shard_map/ppermute | solution.py:17
  137.2 14.5 %all-to-all-done.2 = bf16[16,2,128,128]{2,3,1,0:T(8,128)(2,1)} async-done(((bf16[16,2,128,128]{2,3,1,0:T(8,128)(2,1)}), bf16[16,2,128,128]{2,3,1,0:T(8,128)(2,1)}, u32[]{:S(2)}, u32[]{:S(2)}) %all-to-all-start.2) | async-done | bytes 1048608 | tf_op jit(solution)/shard_map/all_to_all | solution.py:27
  151.7 3.2 %pad_maximum_fusion.1 = bf16[72,128,128]{1,2,0:T(8,128)(2,1)} fusion(bf16[32,128,128]{1,2,0:T(8,128)(2,1)} %bitcast.15, bf16[4,128,128]{1,2,0:T(8,128)(2,1)S(1)} %collective-permute-done.5, bf16[4,128,128]{1,2,0:T(8,128)(2,1)S(1)} %collective-permute-done.4, bf16[32,128,128]{1,2,0:T(8,128)(2,1)} %add_convert_fusion.1), kind=kLoop, calls=%fused_computation.25 | loop fusion | flops 3538944 | bytes 4718592 | tf_op jit(solution)/shard_map/concatenate | solution.py:55
  155.0 4.3 %gather_fusion = bf16[96,128,128]{1,2,0:T(8,128)(2,1)} fusion(bf16[72,128,128]{1,2,0:T(8,128)(2,1)} %pad_maximum_fusion.1, s32[1024]{0:T(1024)S(1)} %pad_clamp_fusion), kind=kCustom, calls=%fused_computation.5 | custom fusion | bytes 6291840 | tf_op jit(solution)/shard_map/jit(_take)/gather | solution.py:61
  159.3 4.6 %fusion.16 = bf16[32,128,128]{1,2,0:T(8,128)(2,1)} fusion(bf16[1,1,32,3,128,128]{5,4,3,2,1,0:T(8,128)(2,1)S(1)} %copy-done, bf16[32,3,128,128]{2,3,1,0:T(8,128)(2,1)} %bitcast.111, pred[32,3]{1,0:T(8,128)(4,1)S(1)} %copy-done.13, bf16[1,1,32,128,128]{3,4,2,1,0:T(8,128)(2,1)} %copy.20), kind=kOutput, calls=%fused_computation.28 | convolution fusion | flops 405798912 | bytes 8388704 | tf_op jit(solution)/shard_map/dot_general | solution.py:62
  164.0 2.0 gather_fusion.4
  167.1 3.5 %all-to-all-start.3 = ((bf16[16,2,128,128]{2,3,1,0:T(8,128)(2,1)}), bf16[16,2,128,128]{2,3,1,0:T(8,128)(2,1)S(1)}, u32[]{:S(2)}, u32[]{:S(2)}) async-start(bf16[16,2,128,128]{2,3,1,0:T(8,128)(2,1)} %bitcast.22), calls=%async_computation.3 | async-start | bytes 2097152 | tf_op jit(solution)/shard_map/all_to_all | solution.py:27
  171.7 3.2 %collective-permute-start.6 = (bf16[4,128,128]{1,2,0:T(8,128)(2,1)S(1)}, bf16[4,128,128]{1,2,0:T(8,128)(2,1)S(1)}, u32[]{:S(2)}, u32[]{:S(2)}) collective-permute-start(bf16[4,128,128]{1,2,0:T(8,128)(2,1)S(1)} %get-tuple-element.63), channel_id=1, source_target_pairs={{0,16},{16,32},{32,48},{48,64},{64,80},{80,96},{96,112},{112,128},... | collective-permute-start | bytes 393224 | tf_op jit(solution)/shard_map/ppermute | solution.py:17
  177.7 3.8 %collective-permute-done.7 = bf16[4,128,128]{1,2,0:T(8,128)(2,1)S(1)} collective-permute-done((bf16[4,128,128]{1,2,0:T(8,128)(2,1)S(1)}, bf16[4,128,128]{1,2,0:T(8,128)(2,1)S(1)}, u32[]{:S(2)}, u32[]{:S(2)}) %collective-permute-start.7) | collective-permute-done | bytes 131104 | tf_op jit(solution)/shard_map/ppermute | solution.py:19
  181.5 17.1 %all-to-all-done.3 = bf16[16,2,128,128]{2,3,1,0:T(8,128)(2,1)S(1)} async-done(((bf16[16,2,128,128]{2,3,1,0:T(8,128)(2,1)}), bf16[16,2,128,128]{2,3,1,0:T(8,128)(2,1)S(1)}, u32[]{:S(2)}, u32[]{:S(2)}) %all-to-all-start.3) | async-done | bytes 1048608 | tf_op jit(solution)/shard_map/all_to_all | solution.py:27
  199.6 1.8 pad_maximum_fusion.2
  201.4 8.3 %gather_fusion.5 = bf16[216,128,128]{1,2,0:T(8,128)(2,1)} fusion(bf16[72,128,128]{1,2,0:T(8,128)(2,1)S(1)} %pad_maximum_fusion.2, s32[1024]{0:T(1024)S(1)} %pad_clamp_fusion.1), kind=kCustom, calls=%fused_computation.4.clone | custom fusion | bytes 14156640 | tf_op jit(solution)/shard_map/jit(_take)/gather | solution.py:61
  209.7 8.1 %fusion.15 = bf16[72,128,128]{1,2,0:T(8,128)(2,1)S(1)} fusion(bf16[1,1,72,3,128,128]{5,4,3,2,1,0:T(8,128)(2,1)} %param.20, bf16[72,3,128,128]{2,3,1,0:T(8,128)(2,1)} %bitcast.103, pred[72,3]{1,0:T(8,128)(4,1)S(1)} %copy-done.6), kind=kOutput, calls=%fused_computation.23 | convolution fusion | flops 910688256 | bytes 16515288 | tf_op jit(solution)/shard_map/dot_general | solution.py:62
  217.8 1.8 fusion.52
  221.1 3.7 %all-to-all-start.4 = ((bf16[16,2,128,128]{3,2,1,0:T(8,128)(2,1)}), bf16[16,2,128,128]{3,2,1,0:T(8,128)(2,1)S(1)}, u32[]{:S(2)}, u32[]{:S(2)}) async-start(bf16[16,2,128,128]{3,2,1,0:T(8,128)(2,1)} %copy.32), calls=%async_computation.4 | async-start | bytes 2097152 | tf_op jit(solution)/shard_map/all_to_all | solution.py:27
  225.8 3.2 %collective-permute-start.8 = (bf16[4,128,128]{1,2,0:T(8,128)(2,1)S(1)}, bf16[4,128,128]{1,2,0:T(8,128)(2,1)S(1)}, u32[]{:S(2)}, u32[]{:S(2)}) collective-permute-start(bf16[4,128,128]{1,2,0:T(8,128)(2,1)S(1)} %get-tuple-element.58), channel_id=1, source_target_pairs={{0,16},{16,32},{32,48},{48,64},{64,80},{80,96},{96,112},{112,128},... | collective-permute-start | bytes 393224 | tf_op jit(solution)/shard_map/ppermute | solution.py:17
  233.5 2.1 collective-permute-done.9
  235.6 1.7 fusion.37
  237.3 15.4 %all-to-all-done.4 = bf16[16,2,128,128]{3,2,1,0:T(8,128)(2,1)S(1)} async-done(((bf16[16,2,128,128]{3,2,1,0:T(8,128)(2,1)}), bf16[16,2,128,128]{3,2,1,0:T(8,128)(2,1)S(1)}, u32[]{:S(2)}, u32[]{:S(2)}) %all-to-all-start.4) | async-done | bytes 1048608 | tf_op jit(solution)/shard_map/all_to_all | solution.py:27
  253.4 1.9 copy.34
  255.3 4.2 %fusion.30 = bf16[1,1,32,128,128]{3,4,2,1,0:T(8,128)(2,1)} fusion(f32[32,128,128]{1,2,0:T(8,128)} %fusion.37, f32[32,128,128]{1,2,0:T(8,128)} %copy.34, bf16[32,128,128]{1,2,0:T(8,128)(2,1)} %add_convert_fusion.1), kind=kLoop, calls=%fused_computation.32 | loop fusion | flops 2097152 | bytes 6291456 | tf_op jit(solution)/shard_map/broadcast_in_dim | solution.py:84
  259.5 2.3 copy.35
  (65 shorter events, 30.7 us)
Async XLA Ops:
  0.0 159.3 %copy-start = (bf16[1,1,32,3,128,128]{5,4,3,2,1,0:T(8,128)(2,1)S(1)}, bf16[1,1,32,3,128,128]{5,4,3,2,1,0:T(8,128)(2,1)}, u32[]{:S(2)}) copy-start(bf16[1,1,32,3,128,128]{5,4,3,2,1,0:T(8,128)(2,1)} %param.22) | copy-start | bytes 9437188
  1.0 104.0 %copy-start.9 = (s32[32]{0:T(128)}, s32[32]{0:T(128)S(1)}, u32[]{:S(2)}) copy-start(s32[32]{0:T(128)S(1)} %reshape_squeeze.3) | copy-start | bytes 388
  1.0 116.7 %copy-start.11 = (pred[32]{0:T(512)(128)(4,1)}, pred[32]{0:T(512)(128)(4,1)S(1)}, u32[]{:S(2)}) copy-start(pred[32]{0:T(512)(128)(4,1)S(1)} %compare_and_fusion.1) | copy-start | bytes 100
  7.0 18.6 %copy-start.7 = (s32[1,1,72,3]{2,1,3,0:T(1,128)S(1)}, s32[1,1,72,3]{2,1,3,0:T(1,128)}, u32[]{:S(2)}) copy-start(s32[1,1,72,3]{2,1,3,0:T(1,128)} %param.21) | copy-start | bytes 2596
  9.4 38.0 %all-to-all-start = ((bf16[16,2,128,128]{2,3,1,0:T(8,128)(2,1)}), bf16[16,2,128,128]{2,3,1,0:T(8,128)(2,1)}, u32[]{:S(2)}, u32[]{:S(2)}) async-start(bf16[16,2,128,128]{2,3,1,0:T(8,128)(2,1)} %bitcast.108), calls=%async_computation | async-start | bytes 2097152 | tf_op jit(solution)/shard_map/all_to_all | solution.py:27
  21.1 6.2 %collective-permute-start = (bf16[4,128,128]{1,2,0:T(8,128)(2,1)}, bf16[4,128,128]{1,2,0:T(8,128)(2,1)S(1)}, u32[]{:S(2)}, u32[]{:S(2)}) collective-permute-start(bf16[4,128,128]{1,2,0:T(8,128)(2,1)} %get-tuple-element.67), channel_id=1, source_target_pairs={{0,16},{16,32},{32,48},{48,64},{64,80},{80,96},{96,112},{112,128},... | collective-permute-start | bytes 393224 | tf_op jit(solution)/shard_map/ppermute | solution.py:17
  24.3 6.8 %collective-permute-start.1 = (bf16[4,128,128]{1,2,0:T(8,128)(2,1)}, bf16[4,128,128]{1,2,0:T(8,128)(2,1)S(1)}, u32[]{:S(2)}, u32[]{:S(2)}) collective-permute-start(bf16[4,128,128]{1,2,0:T(8,128)(2,1)} %get-tuple-element.68), channel_id=1, source_target_pairs={{16,0},{32,16},{48,32},{64,48},{80,64},{96,80},{112,96},{128,112},... | collective-permute-start | bytes 393224 | tf_op jit(solution)/shard_map/ppermute | solution.py:19
  26.0 34.7 %copy-start.5 = (pred[72,3]{1,0:T(8,128)(4,1)}, pred[72,3]{1,0:T(8,128)(4,1)S(1)}, u32[]{:S(2)}) copy-start(pred[72,3]{1,0:T(8,128)(4,1)S(1)} %copy.19) | copy-start | bytes 652
  68.8 2.4 copy-start.4
  73.4 31.6 %all-to-all-start.1 = ((bf16[16,2,128,128]{3,2,1,0:T(8,128)(2,1)}), bf16[16,2,128,128]{3,2,1,0:T(8,128)(2,1)}, u32[]{:S(2)}, u32[]{:S(2)}) async-start(bf16[16,2,128,128]{3,2,1,0:T(8,128)(2,1)} %copy.25), calls=%async_computation.1 | async-start | bytes 2097152 | tf_op jit(solution)/shard_map/all_to_all | solution.py:27
  78.7 6.5 %collective-permute-start.2 = (bf16[4,128,128]{1,2,0:T(8,128)(2,1)S(1)}, bf16[4,128,128]{1,2,0:T(8,128)(2,1)S(1)}, u32[]{:S(2)}, u32[]{:S(2)}) collective-permute-start(bf16[4,128,128]{1,2,0:T(8,128)(2,1)S(1)} %get-tuple-element.62), channel_id=1, source_target_pairs={{0,16},{16,32},{32,48},{48,64},{64,80},{80,96},{96,112},{112,128},... | collective-permute-start | bytes 393224 | tf_op jit(solution)/shard_map/ppermute | solution.py:17
  81.9 7.4 %collective-permute-start.3 = (bf16[4,128,128]{1,2,0:T(8,128)(2,1)S(1)}, bf16[4,128,128]{1,2,0:T(8,128)(2,1)S(1)}, u32[]{:S(2)}, u32[]{:S(2)}) collective-permute-start(bf16[4,128,128]{1,2,0:T(8,128)(2,1)S(1)} %get-tuple-element.61), channel_id=1, source_target_pairs={{16,0},{32,16},{48,32},{64,48},{80,64},{96,80},{112,96},{128,112},... | collective-permute-start | bytes 393224 | tf_op jit(solution)/shard_map/ppermute | solution.py:19
  117.8 6.7 %copy-start.8 = (s32[1,1,32,3]{2,1,3,0:T(1,128)S(1)}, s32[1,1,32,3]{2,1,3,0:T(1,128)}, u32[]{:S(2)}) copy-start(s32[1,1,32,3]{2,1,3,0:T(1,128)} %param.23) | copy-start | bytes 1156
  120.2 31.6 %all-to-all-start.2 = ((bf16[16,2,128,128]{2,3,1,0:T(8,128)(2,1)}), bf16[16,2,128,128]{2,3,1,0:T(8,128)(2,1)}, u32[]{:S(2)}, u32[]{:S(2)}) async-start(bf16[16,2,128,128]{2,3,1,0:T(8,128)(2,1)} %bitcast.109), calls=%async_computation.2 | async-start | bytes 2097152 | tf_op jit(solution)/shard_map/all_to_all | solution.py:27
  126.7 10.0 %collective-permute-start.4 = (bf16[4,128,128]{1,2,0:T(8,128)(2,1)}, bf16[4,128,128]{1,2,0:T(8,128)(2,1)S(1)}, u32[]{:S(2)}, u32[]{:S(2)}) collective-permute-start(bf16[4,128,128]{1,2,0:T(8,128)(2,1)} %get-tuple-element.65), channel_id=1, source_target_pairs={{0,16},{16,32},{32,48},{48,64},{64,80},{80,96},{96,112},{112,128},... | collective-permute-start | bytes 393224 | tf_op jit(solution)/shard_map/ppermute | solution.py:17
  129.9 7.4 %collective-permute-start.5 = (bf16[4,128,128]{1,2,0:T(8,128)(2,1)S(1)}, bf16[4,128,128]{1,2,0:T(8,128)(2,1)S(1)}, u32[]{:S(2)}, u32[]{:S(2)}) collective-permute-start(bf16[4,128,128]{1,2,0:T(8,128)(2,1)S(1)} %get-tuple-element.66), channel_id=1, source_target_pairs={{16,0},{32,16},{48,32},{64,48},{80,64},{96,80},{112,96},{128,112},... | collective-permute-start | bytes 393224 | tf_op jit(solution)/shard_map/ppermute | solution.py:19
  155.0 4.4 %copy-start.13 = (pred[32,3]{1,0:T(8,128)(4,1)S(1)}, pred[32,3]{1,0:T(8,128)(4,1)}, u32[]{:S(2)}) copy-start(pred[32,3]{1,0:T(8,128)(4,1)} %copy.29) | copy-start | bytes 292
  159.3 6.6 %copy-start.12 = (pred[32]{0:T(512)(128)(4,1)S(1)}, pred[32]{0:T(512)(128)(4,1)}, u32[]{:S(2)}) copy-start(pred[32]{0:T(512)(128)(4,1)} %copy-done.11) | copy-start | bytes 100
  167.1 31.5 %all-to-all-start.3 = ((bf16[16,2,128,128]{2,3,1,0:T(8,128)(2,1)}), bf16[16,2,128,128]{2,3,1,0:T(8,128)(2,1)S(1)}, u32[]{:S(2)}, u32[]{:S(2)}) async-start(bf16[16,2,128,128]{2,3,1,0:T(8,128)(2,1)} %bitcast.22), calls=%async_computation.3 | async-start | bytes 2097152 | tf_op jit(solution)/shard_map/all_to_all | solution.py:27
  171.7 6.0 %collective-permute-start.6 = (bf16[4,128,128]{1,2,0:T(8,128)(2,1)S(1)}, bf16[4,128,128]{1,2,0:T(8,128)(2,1)S(1)}, u32[]{:S(2)}, u32[]{:S(2)}) collective-permute-start(bf16[4,128,128]{1,2,0:T(8,128)(2,1)S(1)} %get-tuple-element.63), channel_id=1, source_target_pairs={{0,16},{16,32},{32,48},{48,64},{64,80},{80,96},{96,112},{112,128},... | collective-permute-start | bytes 393224 | tf_op jit(solution)/shard_map/ppermute | solution.py:17
  174.9 6.6 %collective-permute-start.7 = (bf16[4,128,128]{1,2,0:T(8,128)(2,1)S(1)}, bf16[4,128,128]{1,2,0:T(8,128)(2,1)S(1)}, u32[]{:S(2)}, u32[]{:S(2)}) collective-permute-start(bf16[4,128,128]{1,2,0:T(8,128)(2,1)S(1)} %get-tuple-element.64), channel_id=1, source_target_pairs={{16,0},{32,16},{48,32},{64,48},{80,64},{96,80},{112,96},{128,112},... | collective-permute-start | bytes 393224 | tf_op jit(solution)/shard_map/ppermute | solution.py:19
  198.6 1.0 copy-start.2
  201.4 8.3 %copy-start.6 = (pred[72,3]{1,0:T(8,128)(4,1)S(1)}, pred[72,3]{1,0:T(8,128)(4,1)}, u32[]{:S(2)}) copy-start(pred[72,3]{1,0:T(8,128)(4,1)} %copy-done.5) | copy-start | bytes 652
  217.8 2.0 copy-start.3
  221.1 31.6 %copy-start.10 = (s32[32]{0:T(128)S(1)}, s32[32]{0:T(128)}, u32[]{:S(2)}) copy-start(s32[32]{0:T(128)} %copy-done.9) | copy-start | bytes 388
  221.1 31.6 %all-to-all-start.4 = ((bf16[16,2,128,128]{3,2,1,0:T(8,128)(2,1)}), bf16[16,2,128,128]{3,2,1,0:T(8,128)(2,1)S(1)}, u32[]{:S(2)}, u32[]{:S(2)}) async-start(bf16[16,2,128,128]{3,2,1,0:T(8,128)(2,1)} %copy.32), calls=%async_computation.4 | async-start | bytes 2097152 | tf_op jit(solution)/shard_map/all_to_all | solution.py:27
  225.8 6.0 %collective-permute-start.8 = (bf16[4,128,128]{1,2,0:T(8,128)(2,1)S(1)}, bf16[4,128,128]{1,2,0:T(8,128)(2,1)S(1)}, u32[]{:S(2)}, u32[]{:S(2)}) collective-permute-start(bf16[4,128,128]{1,2,0:T(8,128)(2,1)S(1)} %get-tuple-element.58), channel_id=1, source_target_pairs={{0,16},{16,32},{32,48},{48,64},{64,80},{80,96},{96,112},{112,128},... | collective-permute-start | bytes 393224 | tf_op jit(solution)/shard_map/ppermute | solution.py:17
  229.0 6.6 %collective-permute-start.9 = (bf16[4,128,128]{1,2,0:T(8,128)(2,1)S(1)}, bf16[4,128,128]{1,2,0:T(8,128)(2,1)S(1)}, u32[]{:S(2)}, u32[]{:S(2)}) collective-permute-start(bf16[4,128,128]{1,2,0:T(8,128)(2,1)S(1)} %get-tuple-element.57), channel_id=1, source_target_pairs={{16,0},{32,16},{48,32},{64,48},{80,64},{96,80},{112,96},{128,112},... | collective-permute-start | bytes 393224 | tf_op jit(solution)/shard_map/ppermute | solution.py:19
  255.3 6.5 %copy-start.1 = (bf16[1,1,32,3,128,128]{5,4,3,2,1,0:T(8,128)(2,1)S(1)}, bf16[1,1,32,3,128,128]{5,4,3,2,1,0:T(8,128)(2,1)}, u32[]{:S(2)}) copy-start(bf16[1,1,32,3,128,128]{5,4,3,2,1,0:T(8,128)(2,1)} %param.22) | copy-start | bytes 9437188
where the time goes:
time: 263 us; the launch traced here: 262 us
  waiting for transfers between devices  96.4 us (37%)
  local copies, waits for them, and re-layouts  56.5 us (21%)
  starting transfers between devices  48.4 us (18%)
  other arithmetic  35.4 us (13%)
  matrix products  24.8 us (9%)
    all_to_all x5, waiting for transfers between devices, route(): lax.all_to_all(buffer, 'cross', split_axis=0, concat_axis=0, tiled=True)  77.3 us
    all_to_all x5, starting transfers between devices, route(): lax.all_to_all(buffer, 'cross', split_axis=0, concat_axis=0, tiled=True)  25.7 us
    gather x3, local copies, waits for them, and re-layouts, apply_set(): picked = jnp.take(extended, columns, axis=0)  22.5 us
    dot_general x3, matrix products, apply_set(): lax.dot_general(blocks, picked, (((1, 3), (1, 2)), ((0,), (0,))), preferr...  20.8 us
    ppermute x5, starting transfers between devices, extended_2(): lax.ppermute(tail, axis, [(i, (i + 1) % count) for i in range(ends)])  16 us
    ppermute x5, waiting for transfers between devices, extended_2(): lax.ppermute(head, axis, [((i + 1) % count, i) for i in range(ends)])  12.7 us
    concatenate x3, other arithmetic, extend(): jnp.concatenate([field, padded[:OVL], padded[owned + OVL:], incoming.resh...  8.35 us
    gather x3, local copies, waits for them, and re-layouts, extend(): outgoing = jnp.take(field, flat_targets, axis=0)  7.73 us
  transfers between devices with their start and end apart: 15, of which 14 were waited for; matrix products, arithmetic and copies ran while one was open for 7% of the time, Pallas kernels for 0%

commit v1 on v0

v1 whole, which is shorter than its diff:
```python
import functools

import jax
import jax.numpy as jnp
from jax import lax
from jax.experimental import pallas as pl
from jax.experimental.pallas import tpu as pltpu
from jax.sharding import PartitionSpec as P

OVL = 4
BF = jnp.bfloat16
F32 = jnp.float32
VM = pl.BlockSpec(memory_space=pltpu.VMEM)
SM = pl.BlockSpec(memory_space=pltpu.SMEM)
HB = pl.BlockSpec(memory_space=pl.ANY)


def in_vmem(x):
    return pltpu.with_memory_space_constraint(x, pltpu.VMEM)


def params():
    return pltpu.CompilerParams(vmem_limit_bytes=12 * 1024 * 1024)


def cost(flops, nbytes):
    return pl.CostEstimate(flops=flops, bytes_accessed=nbytes, transcendentals=0)


def slot_target(list_ref, count_ref, slot, slots):
    peer, turn = slot // slots, slot % slots
    return list_ref[0, 0, peer, turn], turn < count_ref[0, 0, peer]


def pack_rows(field_ref, list_ref, count_ref, out_ref, slots):
    for slot in range(out_ref.shape[0] * slots):
        row, used = slot_target(list_ref, count_ref, slot, slots)
        out_ref[slot // slots, slot % slots] = jnp.where(used, field_ref[row], jnp.zeros((), BF))


def pack_rhs_kernel(list_ref, count_ref, rhs_ref, out_ref, head_ref, tail_ref):
    rows = rhs_ref.shape[2]
    field = rhs_ref.at[0, 0]
    pack_rows(field, list_ref, count_ref, out_ref, out_ref.shape[1])
    head_ref[...] = field[:OVL]
    tail_ref[...] = field[rows - OVL :]


def fill_extended(ext_ref, own, upper_ref, lower_ref, incoming_ref):
    rows = own.shape[0]
    ext_ref[:rows] = own[...]
    ext_ref[rows : rows + OVL] = upper_ref[...]
    ext_ref[rows + OVL : rows + 2 * OVL] = lower_ref[...]
    peers, slots = incoming_ref.shape[:2]
    for peer in range(peers):
        base = rows + 2 * OVL + peer * slots
        ext_ref[base : base + slots] = incoming_ref[peer]


def row_product(blocks_ref, cols_ref, ext_ref, row):
    terms = blocks_ref.shape[3]
    left = jnp.concatenate([blocks_ref[0, 0, row, k] for k in range(terms)], axis=1)
    right = jnp.concatenate([ext_ref[cols_ref[0, 0, row, k]] for k in range(terms)], axis=0)
    return jnp.dot(left, right, preferred_element_type=F32)


def margin_kernel(cols_ref, own_ref, upper_ref, lower_ref, incoming_ref, blocks_ref, prev_ref, next_ref, cross_ref, ext_ref):
    own = own_ref.at[0, 0]
    rows = own.shape[0]
    fill_extended(ext_ref, own, upper_ref, lower_ref, incoming_ref)
    peers, slots = cross_ref.shape[:2]

    @pl.loop(0, peers)
    def _(peer):
        for turn in range(slots):
            row = rows + 2 * OVL + peer * slots + turn
            cross_ref[peer, turn] = row_product(blocks_ref, cols_ref, ext_ref, row).astype(BF)

    @pl.loop(0, OVL)
    def _(i):
        prev_ref[i] = row_product(blocks_ref, cols_ref, ext_ref, rows + i).astype(BF)
        next_ref[i] = row_product(blocks_ref, cols_ref, ext_ref, rows + OVL + i).astype(BF)


def own_kernel(cols_ref, own_ref, upper_ref, lower_ref, incoming_ref, blocks_ref, out_ref, ext_ref):
    own = own_ref.at[0, 0]
    rows = own.shape[0]
    fill_extended(ext_ref, own, upper_ref, lower_ref, incoming_ref)

    @pl.loop(0, rows // 2)
    def _(i):
        for j in range(2):
            out_ref[2 * i + j] = row_product(blocks_ref, cols_ref, ext_ref, 2 * i + j).astype(BF)


def add_returns(total_ref, list_ref, count_ref, partial_ref, from_prev_ref, from_next_ref, returned_ref):
    rows = partial_ref.shape[0]
    peers, slots = returned_ref.shape[:2]
    total_ref[...] = partial_ref[...].astype(F32)
    total_ref[:OVL] += from_prev_ref[...].astype(F32)
    total_ref[rows - OVL :] += from_next_ref[...].astype(F32)
    for slot in range(peers * slots):
        row, used = slot_target(list_ref, count_ref, slot, slots)
        value = jnp.where(used, returned_ref[slot // slots, slot % slots].astype(F32), 0.0)
        total_ref[row] += value


def first_kernel(list_ref, count_ref, partial_ref, from_prev_ref, from_next_ref, returned_ref, first_ref, out_ref, head_ref, tail_ref, total_ref):
    add_returns(total_ref, list_ref, count_ref, partial_ref, from_prev_ref, from_next_ref, returned_ref)
    first = first_ref.at[0, 0]
    rows = first.shape[0]
    first[...] = total_ref[...].astype(BF)
    pack_rows(first, list_ref, count_ref, out_ref, out_ref.shape[1])
    head_ref[...] = first[:OVL]
    tail_ref[...] = first[rows - OVL :]


def residual_kernel(cols_ref, list_ref, count_ref, rhs_ref, own_ref, upper_ref, lower_ref, incoming_ref, blocks_ref, res_ref, out_ref, head_ref, tail_ref, ext_ref):
    own = own_ref.at[0, 0]
    rows = own.shape[0]
    fill_extended(ext_ref, own, upper_ref, lower_ref, incoming_ref)
    res = res_ref.at[0, 0]

    @pl.loop(0, rows // 2)
    def _(i):
        for j in range(2):
            row = 2 * i + j
            image = row_product(blocks_ref, cols_ref, ext_ref, row)
            res[row] = (rhs_ref[0, 0, row].astype(F32) - image).astype(BF)

    pack_rows(res, list_ref, count_ref, out_ref, out_ref.shape[1])
    head_ref[...] = res[:OVL]
    tail_ref[...] = res[rows - OVL :]


def second_kernel(list_ref, count_ref, first_ref, partial_ref, from_prev_ref, from_next_ref, returned_ref, second_ref, total_ref):
    add_returns(total_ref, list_ref, count_ref, partial_ref, from_prev_ref, from_next_ref, returned_ref)
    second_ref[0, 0] = (first_ref[0, 0].astype(F32) + total_ref[...]).astype(BF)


def to_next(x):
    count = lax.axis_size("slab")
    return lax.ppermute(x, "slab", [(i, i + 1) for i in range(count - 1)])


def to_prev(x):
    count = lax.axis_size("slab")
    return lax.ppermute(x, "slab", [(i + 1, i) for i in range(count - 1)])


def route(buffer):
    return lax.all_to_all(buffer, "cross", split_axis=0, concat_axis=0, tiled=True)


def per_device(rhs, m_blocks, m_cols, j_blocks, j_cols, send_list, send_count):
    _, _, rows, block, vectors = rhs.shape
    peers, slots = send_list.shape[2:]
    extended_rows = m_blocks.shape[2]
    terms = m_blocks.shape[3]
    tile = block * vectors
    field_t = pltpu.VMEM(rhs.shape, BF)
    packed_t = pltpu.VMEM((peers, slots, block, vectors), BF)
    edge_t = pltpu.VMEM((OVL, block, vectors), BF)
    partial_t = pltpu.VMEM((rows, block, vectors), BF)
    ext_s = pltpu.VMEM((extended_rows, block, vectors), BF)
    total_s = pltpu.VMEM((rows, block, vectors), F32)

    rhs_v = in_vmem(rhs)
    m_v = in_vmem(m_blocks)
    j_v = in_vmem(j_blocks)

    packed, head, tail = pl.pallas_call(
        pack_rhs_kernel,
        out_shape=(packed_t, edge_t, edge_t),
        in_specs=[SM, SM, VM],
        out_specs=(VM, VM, VM),
        compiler_params=params(),
        cost_estimate=cost(0, 4 * rows * tile),
        name="pack_rhs",
    )(send_list, send_count, rhs_v)

    def extension(packed, head, tail):
        incoming = in_vmem(route(packed))
        upper = in_vmem(to_next(tail))
        lower = in_vmem(to_prev(head))
        return upper, lower, incoming

    def precondition(field, upper, lower, incoming):
        to_p, to_n, cross = pl.pallas_call(
            margin_kernel,
            out_shape=(edge_t, edge_t, packed_t),
            in_specs=[SM, VM, VM, VM, VM, VM],
            out_specs=(VM, VM, VM),
            scratch_shapes=[ext_s],
            compiler_params=params(),
            cost_estimate=cost(2 * (extended_rows - rows) * terms * block * tile, 6 * extended_rows * tile),
            name="margin_partial",
        )(m_cols, field, upper, lower, incoming, m_v)
        returned = in_vmem(route(cross))
        from_next = in_vmem(to_prev(to_p))
        from_prev = in_vmem(to_next(to_n))
        own = pl.pallas_call(
            own_kernel,
            out_shape=partial_t,
            in_specs=[SM, VM, VM, VM, VM, VM],
            out_specs=VM,
            scratch_shapes=[ext_s],
            compiler_params=params(),
            cost_estimate=cost(2 * rows * terms * block * tile, 6 * extended_rows * tile),
            name="own_partial",
        )(m_cols, field, upper, lower, incoming, m_v)
        return own, from_prev, from_next, returned

    upper, lower, incoming = extension(packed, head, tail)
    own, from_prev, from_next, returned = precondition(rhs_v, upper, lower, incoming)
    first, packed, head, tail = pl.pallas_call(
        first_kernel,
        out_shape=(field_t, packed_t, edge_t, edge_t),
        in_specs=[SM, SM, VM, VM, VM, VM],
        out_specs=(VM, VM, VM, VM),
        scratch_shapes=[total_s],
        compiler_params=params(),
        cost_estimate=cost(0, 10 * rows * tile),
        name="assemble_first",
    )(send_list, send_count, own, from_prev, from_next, returned)
    upper, lower, incoming = extension(packed, head, tail)
    residual, packed, head, tail = pl.pallas_call(
        residual_kernel,
        out_shape=(field_t, packed_t, edge_t, edge_t),
        in_specs=[SM, SM, SM, VM, VM, VM, VM, VM, VM],
        out_specs=(VM, VM, VM, VM),
        scratch_shapes=[ext_s],
        compiler_params=params(),
        cost_estimate=cost(2 * rows * terms * block * tile, 6 * extended_rows * tile),
        name="residual",
    )(j_cols, send_list, send_count, rhs_v, first, upper, lower, incoming, j_v)
    upper, lower, incoming = extension(packed, head, tail)
    own, from_prev, from_next, returned = precondition(residual, upper, lower, incoming)
    return pl.pallas_call(
        second_kernel,
        out_shape=jax.ShapeDtypeStruct(rhs.shape, BF),
        in_specs=[SM, SM, VM, VM, VM, VM, VM],
        out_specs=VM,
        scratch_shapes=[total_s],
        compiler_params=params(),
        cost_estimate=cost(0, 10 * rows * tile),
        name="assemble_second",
    )(send_list, send_count, first, own, from_prev, from_next, returned)


def solution(mesh):
    return jax.shard_map(
        per_device,
        mesh=mesh,
        in_specs=(
            P("slab", "cross", None, None, None),
            P("slab", "cross", None, None, None, None),
            P("slab", "cross", None, None),
            P("slab", "cross", None, None, None, None),
            P("slab", "cross", None, None),
            P("slab", "cross", None, None),
            P("slab", "cross", None),
        ),
        out_specs=P("slab", "cross", None, None, None),
        check_vma=False,
    )
```

time: 263 us -> 212 us (0.81)
  other arithmetic: 35.4 us -> 0 us
  Pallas kernels: 0 us -> 34.4 us
  local copies, waits for them, and re-layouts: 56.5 us -> 30.5 us
  matrix products: 24.8 us -> 0 us
    pallas_call x0 -> x8, Pallas kernels: none -> 34.4 us  [the longest x2 12.9 us: precondition(): pl.pallas_call(margin_kernel, out_shape=(edge_t, edge_t, packed_t), in_sp...]
    gather x6 -> x0, local copies, waits for them, and re-layouts: 30.3 us -> none  [the longest x3 22.5 us: apply_set(): picked = jnp.take(extended, columns, axis=0)]
    unnamed x30 -> x53, local copies, waits for them, and re-layouts: 4.69 us -> 30.5 us
    dot_general x5 -> x0, matrix products: 24.8 us -> none  [the longest x3 20.8 us: apply_set(): lax.dot_general(blocks, picked, (((1, 3), (1, 2)), ((0,), (0,))), preferr...]
    concatenate x3 -> x0, other arithmetic: 8.35 us -> none  [extend(): jnp.concatenate([field, padded[:OVL], padded[owned + OVL:], incoming.resh...]
    scatter-add x4 -> x0, other arithmetic: 6.77 us -> none  [the longest x2 3.39 us: precondition(): total.at[owned - OVL:].add(returned_slab[3 * OVL:].astype(jnp.float32))]
    select_n x6 -> x0, other arithmetic: 6.6 us -> none  [the longest x3 6.01 us: extend(): jnp.where(flat_valid[:, None, None], outgoing, jnp.zeros((), jnp.bfloat16))]
    slice x5 -> x0, local copies, waits for them, and re-layouts: 6.3 us -> none  [the longest x3 4.32 us: extended_2(): lax.slice_in_dim(cells, cells.shape[dim] - width, cells.shape[dim], axis=...]
  transfers between devices with their start and end apart: 15 -> 15, of which waited for: 14 -> 11; matrix products, arithmetic and copies ran while one was open for 7% -> 0% of each run, Pallas kernels for 0% -> 4%
where the time goes in v1:
time: 212 us; the launch traced here: 211 us
  waiting for transfers between devices  97.2 us (46%)
  starting transfers between devices  48.3 us (23%)
  Pallas kernels  34.4 us (16%)
  local copies, waits for them, and re-layouts  30.5 us (14%)
    all_to_all x5, waiting for transfers between devices, route(): lax.all_to_all(buffer, 'cross', split_axis=0, concat_axis=0, tiled=True)  81.9 us
    unnamed x53, local copies, waits for them, and re-layouts  30.5 us
    all_to_all x5, starting transfers between devices, route(): lax.all_to_all(buffer, 'cross', split_axis=0, concat_axis=0, tiled=True)  25.8 us
    ppermute x5, starting transfers between devices, to_next(): return lax.ppermute(x, 'slab', [(i, i + 1) for i in range(count - 1)])  16.1 us
    pallas_call x2, Pallas kernels, precondition(): pl.pallas_call(margin_kernel, out_shape=(edge_t, edge_t, packed_t), in_sp...  12.9 us
    ppermute x5, waiting for transfers between devices, to_prev(): return lax.ppermute(x, 'slab', [(i + 1, i) for i in range(count - 1)])  11.3 us
    pallas_call x2, Pallas kernels, precondition(): pl.pallas_call(own_kernel, out_shape=partial_t, in_specs=[SM, VM, VM, VM,...  9.04 us
    ppermute x5, starting transfers between devices, to_prev(): return lax.ppermute(x, 'slab', [(i + 1, i) for i in range(count - 1)])  6.46 us
  transfers between devices with their start and end apart: 15, of which 11 were waited for; matrix products, arithmetic and copies ran while one was open for 0% of the time, Pallas kernels for 4%

profile of v1, /device:TPU:1, one launch (start us, length us, event | category | flops | bytes accessed | tf_op | source)
XLA Modules:
  0.0 210.7 jit_solution(16717085797948468714)
XLA Ops:
  0.8 1.2 copy-done.4
  2.6 1.9 pack_rhs.1
  4.5 10.1 %all-to-all-start = ((bf16[16,2,128,128]{3,2,1,0:T(8,128)(2,1)}), bf16[16,2,128,128]{3,2,1,0:T(8,128)(2,1)S(1)}, u32[]{:S(2)}, u32[]{:S(2)}) async-start(bf16[16,2,128,128]{3,2,1,0:T(8,128)(2,1)} %get-tuple-element.24), calls=%async_computation | async-start | bytes 2097152 | tf_op jit(solution)/shard_map/all_to_all | solution.py:152
  14.7 3.2 %collective-permute-start = (bf16[4,128,128]{2,1,0:T(8,128)(2,1)S(1)}, bf16[4,128,128]{2,1,0:T(8,128)(2,1)S(1)}, u32[]{:S(2)}, u32[]{:S(2)}) collective-permute-start(bf16[4,128,128]{2,1,0:T(8,128)(2,1)S(1)} %get-tuple-element.22), channel_id=1, source_target_pairs={{0,16},{16,32},{32,48},{48,64},{64,80},{80,96},{96,112},{112,128},... | collective-permute-start | bytes 393224 | tf_op jit(solution)/shard_map/ppermute | solution.py:143
  17.9 1.3 collective-permute-start.1
  20.7 3.8 %collective-permute-done.1.lower_ref = bf16[4,128,128]{2,1,0:T(8,128)(2,1)S(1)} collective-permute-done((bf16[4,128,128]{2,1,0:T(8,128)(2,1)S(1)}, bf16[4,128,128]{2,1,0:T(8,128)(2,1)S(1)}, u32[]{:S(2)}, u32[]{:S(2)}) %collective-permute-start.1) | collective-permute-done | bytes 131104 | tf_op jit(solution)/shard_map/ppermute | solution.py:148
  24.5 18.1 %all-to-all-done.incoming_ref = bf16[16,2,128,128]{3,2,1,0:T(8,128)(2,1)S(1)} async-done(((bf16[16,2,128,128]{3,2,1,0:T(8,128)(2,1)}), bf16[16,2,128,128]{3,2,1,0:T(8,128)(2,1)S(1)}, u32[]{:S(2)}, u32[]{:S(2)}) %all-to-all-start) | async-done | bytes 1048608 | tf_op jit(solution)/shard_map/all_to_all | solution.py:152
  42.6 3.0 %copy-done = bf16[1,1,72,3,128,128]{5,4,3,2,1,0:T(8,128)(2,1)S(1)} copy-done((bf16[1,1,72,3,128,128]{5,4,3,2,1,0:T(8,128)(2,1)S(1)}, bf16[1,1,72,3,128,128]{5,4,3,2,1,0:T(8,128)(2,1)}, u32[]{:S(2)}) %copy-start) | copy-done | bytes 7077912
  45.6 1.2 copy-done.5
  46.8 6.5 %margin_partial.2 = (bf16[4,128,128]{2,1,0:T(8,128)(2,1)}, bf16[4,128,128]{2,1,0:T(8,128)(2,1)}, bf16[16,2,128,128]{3,2,1,0:T(8,128)(2,1)}) custom-call(s32[1,1,72,3]{3,2,1,0:T(8,128)S(1)} %copy.9.cols_ref, bf16[1,1,32,128,128]{4,3,2,1,0:T(8,128)(2,1)S(1)} %copy-done.5, bf16[4,128,128]{2,1,0:T(8,128)(2,1)S(1)} %collective-permute-done.upper_ref, ...), custom_call_target="tpu_custom_call" | custom-call | flops 503316480 | bytes 7077888 | tf_op jit(solution)/shard_map/margin_partial/pallas_call | solution.py:189
  53.3 4.4 %all-to-all-start.1 = ((bf16[16,2,128,128]{3,2,1,0:T(8,128)(2,1)}), bf16[16,2,128,128]{3,2,1,0:T(8,128)(2,1)}, u32[]{:S(2)}, u32[]{:S(2)}) async-start(bf16[16,2,128,128]{3,2,1,0:T(8,128)(2,1)} %get-tuple-element.27), calls=%async_computation.1 | async-start | bytes 2097152 | tf_op jit(solution)/shard_map/all_to_all | solution.py:152
  57.7 3.2 %collective-permute-start.2 = (bf16[4,128,128]{2,1,0:T(8,128)(2,1)}, bf16[4,128,128]{2,1,0:T(8,128)(2,1)S(1)}, u32[]{:S(2)}, u32[]{:S(2)}) collective-permute-start(bf16[4,128,128]{2,1,0:T(8,128)(2,1)} %get-tuple-element.25), channel_id=1, source_target_pairs={{0,16},{16,32},{32,48},{48,64},{64,80},{80,96},{96,112},{112,128},... | collective-permute-start | bytes 393224 | tf_op jit(solution)/shard_map/ppermute | solution.py:143
  60.9 1.3 collective-permute-start.3
  62.2 3.0 %copy-done.1 = bf16[1,1,72,3,128,128]{5,4,3,2,1,0:T(8,128)(2,1)S(1)} copy-done((bf16[1,1,72,3,128,128]{5,4,3,2,1,0:T(8,128)(2,1)S(1)}, bf16[1,1,72,3,128,128]{5,4,3,2,1,0:T(8,128)(2,1)}, u32[]{:S(2)}) %copy-start.1) | copy-done | bytes 7077912
  65.2 4.5 %own_partial.2.partial_ref = bf16[32,128,128]{2,1,0:T(8,128)(2,1)S(1)} custom-call(s32[1,1,72,3]{3,2,1,0:T(8,128)S(1)} %copy.9.cols_ref, bf16[1,1,32,128,128]{4,3,2,1,0:T(8,128)(2,1)S(1)} %copy-done.6, bf16[4,128,128]{2,1,0:T(8,128)(2,1)S(1)} %collective-permute-done.upper_ref, bf16[4,128,128]{2,1,0:T(8,128)(2,1)S(1)} %collective-permute-done.1.lower_ref, ...), custom_call_target="tpu_custom_call" | custom-call | flops 402653184 | bytes 7077888 | tf_op jit(solution)/shard_map/own_partial/pallas_call | solution.py:202
  71.0 13.9 %all-to-all-done.1.returned_ref = bf16[16,2,128,128]{3,2,1,0:T(8,128)(2,1)} async-done(((bf16[16,2,128,128]{3,2,1,0:T(8,128)(2,1)}), bf16[16,2,128,128]{3,2,1,0:T(8,128)(2,1)}, u32[]{:S(2)}, u32[]{:S(2)}) %all-to-all-start.1) | async-done | bytes 1048608 | tf_op jit(solution)/shard_map/all_to_all | solution.py:152
  85.0 0.9 copy-done.17
  85.9 0.9 copy-done.19
  86.8 3.0 %assemble_first.1 = (bf16[1,1,32,128,128]{4,3,2,1,0:T(8,128)(2,1)S(1)}, bf16[16,2,128,128]{3,2,1,0:T(8,128)(2,1)}, bf16[4,128,128]{2,1,0:T(8,128)(2,1)S(1)}, bf16[4,128,128]{2,1,0:T(8,128)(2,1)S(1)}) custom-call(s32[1,1,16,2]{3,2,1,0:T(8,128)S(1)} %copy.16.list_ref, s32[1,1,16]{2,1,0:T(1,128)S(1)} %copy-done.21, ...), custom_call_target="tpu_custom_call" | custom-call | bytes 5242880 | tf_op jit(solution)/shard_map/assemble_first/pallas_call | solution.py:216
  89.8 1.0 copy-done.7
  90.8 3.6 %all-to-all-start.2 = ((bf16[16,2,128,128]{3,2,1,0:T(8,128)(2,1)}), bf16[16,2,128,128]{3,2,1,0:T(8,128)(2,1)S(1)}, u32[]{:S(2)}, u32[]{:S(2)}) async-start(bf16[16,2,128,128]{3,2,1,0:T(8,128)(2,1)} %get-tuple-element.31), calls=%async_computation.2 | async-start | bytes 2097152 | tf_op jit(solution)/shard_map/all_to_all | solution.py:152
  94.4 3.2 %collective-permute-start.4 = (bf16[4,128,128]{2,1,0:T(8,128)(2,1)S(1)}, bf16[4,128,128]{2,1,0:T(8,128)(2,1)S(1)}, u32[]{:S(2)}, u32[]{:S(2)}) collective-permute-start(bf16[4,128,128]{2,1,0:T(8,128)(2,1)S(1)} %get-tuple-element.29), channel_id=1, source_target_pairs={{0,16},{16,32},{32,48},{48,64},{64,80},{80,96},{96,112},{112,128},... | collective-permute-start | bytes 393224 | tf_op jit(solution)/shard_map/ppermute | solution.py:143
  97.6 1.3 collective-permute-start.5
  99.0 1.4 collective-permute-done.4.upper_ref
  100.4 3.8 %collective-permute-done.5.lower_ref = bf16[4,128,128]{2,1,0:T(8,128)(2,1)S(1)} collective-permute-done((bf16[4,128,128]{2,1,0:T(8,128)(2,1)S(1)}, bf16[4,128,128]{2,1,0:T(8,128)(2,1)S(1)}, u32[]{:S(2)}, u32[]{:S(2)}) %collective-permute-start.5) | collective-permute-done | bytes 131104 | tf_op jit(solution)/shard_map/ppermute | solution.py:148
  104.2 18.1 %all-to-all-done.2.incoming_ref = bf16[16,2,128,128]{3,2,1,0:T(8,128)(2,1)S(1)} async-done(((bf16[16,2,128,128]{3,2,1,0:T(8,128)(2,1)}), bf16[16,2,128,128]{3,2,1,0:T(8,128)(2,1)S(1)}, u32[]{:S(2)}, u32[]{:S(2)}) %all-to-all-start.2) | async-done | bytes 1048608 | tf_op jit(solution)/shard_map/all_to_all | solution.py:152
  122.3 1.2 copy-done.8
  123.5 1.9 copy-done.10
  125.4 4.6 %residual.1 = (bf16[1,1,32,128,128]{4,3,2,1,0:T(8,128)(2,1)S(1)}, bf16[16,2,128,128]{3,2,1,0:T(8,128)(2,1)S(1)}, bf16[4,128,128]{2,1,0:T(8,128)(2,1)S(1)}, bf16[4,128,128]{2,1,0:T(8,128)(2,1)S(1)}) custom-call(s32[1,1,32,3]{3,2,1,0:T(8,128)S(1)} %copy.12.cols_ref, s32[1,1,16,2]{3,2,1,0:T(8,128)S(1)} %copy.16.list_ref, s32[1,1,16]{2,1,0:T(1,128)S(1)} %copy-done.21, ...), custom_call_target="tpu_custom_call" | custom-call | flops 402653184 | bytes 7077888 | tf_op jit(solution)/shard_map/residual/pallas_call | solution.py:227
  130.0 1.0 copy-done.11
  132.2 3.6 %all-to-all-start.3 = ((bf16[16,2,128,128]{3,2,1,0:T(8,128)(2,1)}), bf16[16,2,128,128]{3,2,1,0:T(8,128)(2,1)S(1)}, u32[]{:S(2)}, u32[]{:S(2)}) async-start(bf16[16,2,128,128]{3,2,1,0:T(8,128)(2,1)} %copy-done.11), calls=%async_computation.3 | async-start | bytes 2097152 | tf_op jit(solution)/shard_map/all_to_all | solution.py:152
  135.8 3.2 %collective-permute-start.6 = (bf16[4,128,128]{2,1,0:T(8,128)(2,1)}, bf16[4,128,128]{2,1,0:T(8,128)(2,1)S(1)}, u32[]{:S(2)}, u32[]{:S(2)}) collective-permute-start(bf16[4,128,128]{2,1,0:T(8,128)(2,1)} %copy-done.23), channel_id=1, source_target_pairs={{0,16},{16,32},{32,48},{48,64},{64,80},{80,96},{96,112},{112,128},... | collective-permute-start | bytes 393224 | tf_op jit(solution)/shard_map/ppermute | solution.py:143
  139.0 1.3 collective-permute-start.7
  140.3 1.8 collective-permute-done.6.upper_ref
  142.1 3.7 %collective-permute-done.7.lower_ref = bf16[4,128,128]{2,1,0:T(8,128)(2,1)S(1)} collective-permute-done((bf16[4,128,128]{2,1,0:T(8,128)(2,1)}, bf16[4,128,128]{2,1,0:T(8,128)(2,1)S(1)}, u32[]{:S(2)}, u32[]{:S(2)}) %collective-permute-start.7) | collective-permute-done | bytes 131104 | tf_op jit(solution)/shard_map/ppermute | solution.py:148
  145.8 17.8 %all-to-all-done.3.incoming_ref = bf16[16,2,128,128]{3,2,1,0:T(8,128)(2,1)S(1)} async-done(((bf16[16,2,128,128]{3,2,1,0:T(8,128)(2,1)}), bf16[16,2,128,128]{3,2,1,0:T(8,128)(2,1)S(1)}, u32[]{:S(2)}, u32[]{:S(2)}) %all-to-all-start.3) | async-done | bytes 1048608 | tf_op jit(solution)/shard_map/all_to_all | solution.py:152
  163.7 3.0 %copy-done.2 = bf16[1,1,72,3,128,128]{5,4,3,2,1,0:T(8,128)(2,1)S(1)} copy-done((bf16[1,1,72,3,128,128]{5,4,3,2,1,0:T(8,128)(2,1)S(1)}, bf16[1,1,72,3,128,128]{5,4,3,2,1,0:T(8,128)(2,1)}, u32[]{:S(2)}) %copy-start.2) | copy-done | bytes 7077912
  166.7 6.5 %margin_partial.3 = (bf16[4,128,128]{2,1,0:T(8,128)(2,1)}, bf16[4,128,128]{2,1,0:T(8,128)(2,1)}, bf16[16,2,128,128]{3,2,1,0:T(8,128)(2,1)}) custom-call(s32[1,1,72,3]{3,2,1,0:T(8,128)S(1)} %copy.9.cols_ref, bf16[1,1,32,128,128]{4,3,2,1,0:T(8,128)(2,1)S(1)} %get-tuple-element.32.own_ref, bf16[4,128,128]{2,1,0:T(8,128)(2,1)S(1)} %collective-permute-done.6.upper_ref, ...), custom_call_target="tpu_custom_call" | custom-call | flops 503316480 | bytes 7077888 | tf_op jit(solution)/shard_map/margin_partial/pallas_call | solution.py:189
  173.1 4.2 %all-to-all-start.4 = ((bf16[16,2,128,128]{3,2,1,0:T(8,128)(2,1)}), bf16[16,2,128,128]{3,2,1,0:T(8,128)(2,1)}, u32[]{:S(2)}, u32[]{:S(2)}) async-start(bf16[16,2,128,128]{3,2,1,0:T(8,128)(2,1)} %get-tuple-element.38), calls=%async_computation.4 | async-start | bytes 2097152 | tf_op jit(solution)/shard_map/all_to_all | solution.py:152
  177.4 3.2 %collective-permute-start.8 = (bf16[4,128,128]{2,1,0:T(8,128)(2,1)}, bf16[4,128,128]{2,1,0:T(8,128)(2,1)S(1)}, u32[]{:S(2)}, u32[]{:S(2)}) collective-permute-start(bf16[4,128,128]{2,1,0:T(8,128)(2,1)} %get-tuple-element.36), channel_id=1, source_target_pairs={{0,16},{16,32},{32,48},{48,64},{64,80},{80,96},{96,112},{112,128},... | collective-permute-start | bytes 393224 | tf_op jit(solution)/shard_map/ppermute | solution.py:143
  180.6 1.3 collective-permute-start.9
  181.9 3.0 %copy-done.3 = bf16[1,1,72,3,128,128]{5,4,3,2,1,0:T(8,128)(2,1)S(1)} copy-done((bf16[1,1,72,3,128,128]{5,4,3,2,1,0:T(8,128)(2,1)S(1)}, bf16[1,1,72,3,128,128]{5,4,3,2,1,0:T(8,128)(2,1)}, u32[]{:S(2)}) %copy-start.3) | copy-done | bytes 7077912
  184.9 4.5 %own_partial.3.partial_ref = bf16[32,128,128]{2,1,0:T(8,128)(2,1)S(1)} custom-call(s32[1,1,72,3]{3,2,1,0:T(8,128)S(1)} %copy.9.cols_ref, bf16[1,1,32,128,128]{4,3,2,1,0:T(8,128)(2,1)S(1)} %get-tuple-element.32.own_ref, bf16[4,128,128]{2,1,0:T(8,128)(2,1)S(1)} %collective-permute-done.6.upper_ref, bf16[4,128,128]{2,1,0:T(8,128)(2,1)S(1)} %collective-permute-done.7.lower_ref, ...), custom_call_target="tpu_custom_call" | custom-call | flops 402653184 | bytes 7077888 | tf_op jit(solution)/shard_map/own_partial/pallas_call | solution.py:202
  190.7 14.0 %all-to-all-done.4.returned_ref = bf16[16,2,128,128]{3,2,1,0:T(8,128)(2,1)} async-done(((bf16[16,2,128,128]{3,2,1,0:T(8,128)(2,1)}), bf16[16,2,128,128]{3,2,1,0:T(8,128)(2,1)}, u32[]{:S(2)}, u32[]{:S(2)}) %all-to-all-start.4) | async-done | bytes 1048608 | tf_op jit(solution)/shard_map/all_to_all | solution.py:152
  204.7 1.2 copy-done.9
  205.9 0.9 copy-done.13
  206.8 0.9 copy-done.15
  207.7 3.0 %assemble_second.1 = bf16[1,1,32,128,128]{4,3,2,1,0:T(8,128)(2,1)} custom-call(s32[1,1,16,2]{3,2,1,0:T(8,128)S(1)} %copy.16.list_ref, s32[1,1,16]{2,1,0:T(1,128)S(1)} %copy-done.21, bf16[1,1,32,128,128]{4,3,2,1,0:T(8,128)(2,1)S(1)} %copy-done.9, bf16[32,128,128]{2,1,0:T(8,128)(2,1)S(1)} %own_partial.3.partial_ref, bf16[4,128,128]{2,1,0:T(8,128)(2,1)S(1)} %copy-done.13, ...), custom_call_target="tpu_custom_call" | custom-call | bytes 5242880 | tf_op jit(solution)/shard_map/assemble_second/pallas_call | solution.py:239
  (43 shorter events, 6.9 us)
Async XLA Ops:
  0.8 1.2 copy-start.4
  2.0 0.7 copy-start.20
  4.5 57.6 %copy-start.6 = (bf16[1,1,32,128,128]{4,3,2,1,0:T(8,128)(2,1)S(1)}, bf16[1,1,32,128,128]{4,3,2,1,0:T(8,128)(2,1)}, u32[]{:S(2)}) copy-start(bf16[1,1,32,128,128]{4,3,2,1,0:T(8,128)(2,1)} %rhs_ref.3) | copy-start | bytes 3145732
  4.5 38.0 %all-to-all-start = ((bf16[16,2,128,128]{3,2,1,0:T(8,128)(2,1)}), bf16[16,2,128,128]{3,2,1,0:T(8,128)(2,1)S(1)}, u32[]{:S(2)}, u32[]{:S(2)}) async-start(bf16[16,2,128,128]{3,2,1,0:T(8,128)(2,1)} %get-tuple-element.24), calls=%async_computation | async-start | bytes 2097152 | tf_op jit(solution)/shard_map/all_to_all | solution.py:152
  14.7 6.0 %collective-permute-start = (bf16[4,128,128]{2,1,0:T(8,128)(2,1)S(1)}, bf16[4,128,128]{2,1,0:T(8,128)(2,1)S(1)}, u32[]{:S(2)}, u32[]{:S(2)}) collective-permute-start(bf16[4,128,128]{2,1,0:T(8,128)(2,1)S(1)} %get-tuple-element.22), channel_id=1, source_target_pairs={{0,16},{16,32},{32,48},{48,64},{64,80},{80,96},{96,112},{112,128},... | collective-permute-start | bytes 393224 | tf_op jit(solution)/shard_map/ppermute | solution.py:143
  17.9 6.6 %collective-permute-start.1 = (bf16[4,128,128]{2,1,0:T(8,128)(2,1)S(1)}, bf16[4,128,128]{2,1,0:T(8,128)(2,1)S(1)}, u32[]{:S(2)}, u32[]{:S(2)}) collective-permute-start(bf16[4,128,128]{2,1,0:T(8,128)(2,1)S(1)} %get-tuple-element.23), channel_id=1, source_target_pairs={{16,0},{32,16},{48,32},{64,48},{80,64},{96,80},{112,96},{128,112},... | collective-permute-start | bytes 393224 | tf_op jit(solution)/shard_map/ppermute | solution.py:148
  42.6 3.0 %copy-start = (bf16[1,1,72,3,128,128]{5,4,3,2,1,0:T(8,128)(2,1)S(1)}, bf16[1,1,72,3,128,128]{5,4,3,2,1,0:T(8,128)(2,1)}, u32[]{:S(2)}) copy-start(bf16[1,1,72,3,128,128]{5,4,3,2,1,0:T(8,128)(2,1)} %blocks_ref.9) | copy-start | bytes 21233668
  45.6 1.2 copy-start.5
  53.3 31.7 %copy-start.21 = (s32[1,1,16]{2,1,0:T(1,128)S(1)}, s32[1,1,16]{2,1,0:T(1,128)}, u32[]{:S(2)}) copy-start(s32[1,1,16]{2,1,0:T(1,128)} %count_ref.7) | copy-start | bytes 196
  53.3 31.7 %all-to-all-start.1 = ((bf16[16,2,128,128]{3,2,1,0:T(8,128)(2,1)}), bf16[16,2,128,128]{3,2,1,0:T(8,128)(2,1)}, u32[]{:S(2)}, u32[]{:S(2)}) async-start(bf16[16,2,128,128]{3,2,1,0:T(8,128)(2,1)} %get-tuple-element.27), calls=%async_computation.1 | async-start | bytes 2097152 | tf_op jit(solution)/shard_map/all_to_all | solution.py:152
  57.7 12.1 %collective-permute-start.2 = (bf16[4,128,128]{2,1,0:T(8,128)(2,1)}, bf16[4,128,128]{2,1,0:T(8,128)(2,1)S(1)}, u32[]{:S(2)}, u32[]{:S(2)}) collective-permute-start(bf16[4,128,128]{2,1,0:T(8,128)(2,1)} %get-tuple-element.25), channel_id=1, source_target_pairs={{0,16},{16,32},{32,48},{48,64},{64,80},{80,96},{96,112},{112,128},... | collective-permute-start | bytes 393224 | tf_op jit(solution)/shard_map/ppermute | solution.py:143
  60.9 9.5 %collective-permute-start.3 = (bf16[4,128,128]{2,1,0:T(8,128)(2,1)}, bf16[4,128,128]{2,1,0:T(8,128)(2,1)S(1)}, u32[]{:S(2)}, u32[]{:S(2)}) collective-permute-start(bf16[4,128,128]{2,1,0:T(8,128)(2,1)} %get-tuple-element.26), channel_id=1, source_target_pairs={{16,0},{32,16},{48,32},{64,48},{80,64},{96,80},{112,96},{128,112},... | collective-permute-start | bytes 393224 | tf_op jit(solution)/shard_map/ppermute | solution.py:148
  62.2 3.0 %copy-start.1 = (bf16[1,1,72,3,128,128]{5,4,3,2,1,0:T(8,128)(2,1)S(1)}, bf16[1,1,72,3,128,128]{5,4,3,2,1,0:T(8,128)(2,1)}, u32[]{:S(2)}) copy-start(bf16[1,1,72,3,128,128]{5,4,3,2,1,0:T(8,128)(2,1)} %blocks_ref.9) | copy-start | bytes 21233668
  65.2 33.7 %copy-start.24 = (s32[1,1,32,3]{2,1,3,0:T(1,128)S(1)}, s32[1,1,32,3]{2,1,3,0:T(1,128)}, u32[]{:S(2)}) copy-start(s32[1,1,32,3]{2,1,3,0:T(1,128)} %param.11) | copy-start | bytes 1156
  69.7 0.6 copy-start.16
  70.4 0.6 copy-start.18
  85.0 0.9 copy-start.17
  85.9 0.9 copy-start.19
  89.8 1.0 copy-start.7
  90.8 31.5 %all-to-all-start.2 = ((bf16[16,2,128,128]{3,2,1,0:T(8,128)(2,1)}), bf16[16,2,128,128]{3,2,1,0:T(8,128)(2,1)S(1)}, u32[]{:S(2)}, u32[]{:S(2)}) async-start(bf16[16,2,128,128]{3,2,1,0:T(8,128)(2,1)} %get-tuple-element.31), calls=%async_computation.2 | async-start | bytes 2097152 | tf_op jit(solution)/shard_map/all_to_all | solution.py:152
  94.4 6.0 %collective-permute-start.4 = (bf16[4,128,128]{2,1,0:T(8,128)(2,1)S(1)}, bf16[4,128,128]{2,1,0:T(8,128)(2,1)S(1)}, u32[]{:S(2)}, u32[]{:S(2)}) collective-permute-start(bf16[4,128,128]{2,1,0:T(8,128)(2,1)S(1)} %get-tuple-element.29), channel_id=1, source_target_pairs={{0,16},{16,32},{32,48},{48,64},{64,80},{80,96},{96,112},{112,128},... | collective-permute-start | bytes 393224 | tf_op jit(solution)/shard_map/ppermute | solution.py:143
  97.6 6.6 %collective-permute-start.5 = (bf16[4,128,128]{2,1,0:T(8,128)(2,1)S(1)}, bf16[4,128,128]{2,1,0:T(8,128)(2,1)S(1)}, u32[]{:S(2)}, u32[]{:S(2)}) collective-permute-start(bf16[4,128,128]{2,1,0:T(8,128)(2,1)S(1)} %get-tuple-element.30), channel_id=1, source_target_pairs={{16,0},{32,16},{48,32},{64,48},{80,64},{96,80},{112,96},{128,112},... | collective-permute-start | bytes 393224 | tf_op jit(solution)/shard_map/ppermute | solution.py:148
  122.3 1.2 copy-start.8
  123.5 1.9 copy-start.10
  129.9 1.0 copy-start.11
  130.9 0.6 copy-start.22
  131.6 0.6 copy-start.23
  132.2 31.5 %all-to-all-start.3 = ((bf16[16,2,128,128]{3,2,1,0:T(8,128)(2,1)}), bf16[16,2,128,128]{3,2,1,0:T(8,128)(2,1)S(1)}, u32[]{:S(2)}, u32[]{:S(2)}) async-start(bf16[16,2,128,128]{3,2,1,0:T(8,128)(2,1)} %copy-done.11), calls=%async_computation.3 | async-start | bytes 2097152 | tf_op jit(solution)/shard_map/all_to_all | solution.py:152
  135.8 6.4 %collective-permute-start.6 = (bf16[4,128,128]{2,1,0:T(8,128)(2,1)}, bf16[4,128,128]{2,1,0:T(8,128)(2,1)S(1)}, u32[]{:S(2)}, u32[]{:S(2)}) collective-permute-start(bf16[4,128,128]{2,1,0:T(8,128)(2,1)} %copy-done.23), channel_id=1, source_target_pairs={{0,16},{16,32},{32,48},{48,64},{64,80},{80,96},{96,112},{112,128},... | collective-permute-start | bytes 393224 | tf_op jit(solution)/shard_map/ppermute | solution.py:143
  139.0 6.8 %collective-permute-start.7 = (bf16[4,128,128]{2,1,0:T(8,128)(2,1)}, bf16[4,128,128]{2,1,0:T(8,128)(2,1)S(1)}, u32[]{:S(2)}, u32[]{:S(2)}) collective-permute-start(bf16[4,128,128]{2,1,0:T(8,128)(2,1)} %copy-done.22), channel_id=1, source_target_pairs={{16,0},{32,16},{48,32},{64,48},{80,64},{96,80},{112,96},{128,112},... | collective-permute-start | bytes 393224 | tf_op jit(solution)/shard_map/ppermute | solution.py:148
  163.7 3.0 %copy-start.2 = (bf16[1,1,72,3,128,128]{5,4,3,2,1,0:T(8,128)(2,1)S(1)}, bf16[1,1,72,3,128,128]{5,4,3,2,1,0:T(8,128)(2,1)}, u32[]{:S(2)}) copy-start(bf16[1,1,72,3,128,128]{5,4,3,2,1,0:T(8,128)(2,1)} %blocks_ref.9) | copy-start | bytes 21233668
  173.1 31.6 %all-to-all-start.4 = ((bf16[16,2,128,128]{3,2,1,0:T(8,128)(2,1)}), bf16[16,2,128,128]{3,2,1,0:T(8,128)(2,1)}, u32[]{:S(2)}, u32[]{:S(2)}) async-start(bf16[16,2,128,128]{3,2,1,0:T(8,128)(2,1)} %get-tuple-element.38), calls=%async_computation.4 | async-start | bytes 2097152 | tf_op jit(solution)/shard_map/all_to_all | solution.py:152
  177.4 12.1 %collective-permute-start.8 = (bf16[4,128,128]{2,1,0:T(8,128)(2,1)}, bf16[4,128,128]{2,1,0:T(8,128)(2,1)S(1)}, u32[]{:S(2)}, u32[]{:S(2)}) collective-permute-start(bf16[4,128,128]{2,1,0:T(8,128)(2,1)} %get-tuple-element.36), channel_id=1, source_target_pairs={{0,16},{16,32},{32,48},{48,64},{64,80},{80,96},{96,112},{112,128},... | collective-permute-start | bytes 393224 | tf_op jit(solution)/shard_map/ppermute | solution.py:143
  180.6 9.5 %collective-permute-start.9 = (bf16[4,128,128]{2,1,0:T(8,128)(2,1)}, bf16[4,128,128]{2,1,0:T(8,128)(2,1)S(1)}, u32[]{:S(2)}, u32[]{:S(2)}) collective-permute-start(bf16[4,128,128]{2,1,0:T(8,128)(2,1)} %get-tuple-element.37), channel_id=1, source_target_pairs={{16,0},{32,16},{48,32},{64,48},{80,64},{96,80},{112,96},{128,112},... | collective-permute-start | bytes 393224 | tf_op jit(solution)/shard_map/ppermute | solution.py:148
  181.9 3.0 %copy-start.3 = (bf16[1,1,72,3,128,128]{5,4,3,2,1,0:T(8,128)(2,1)S(1)}, bf16[1,1,72,3,128,128]{5,4,3,2,1,0:T(8,128)(2,1)}, u32[]{:S(2)}) copy-start(bf16[1,1,72,3,128,128]{5,4,3,2,1,0:T(8,128)(2,1)} %blocks_ref.9) | copy-start | bytes 21233668
  189.4 0.7 copy-start.12
  190.1 0.7 copy-start.14
  204.7 1.2 copy-start.9
  205.9 0.9 copy-start.13
  206.8 0.9 copy-start.15

commit v2 on v0

v2 whole, which is shorter than its diff:
```python
import functools

import jax
import jax.numpy as jnp
from jax import lax
from jax.experimental import pallas as pl
from jax.experimental.pallas import tpu as pltpu
from jax.sharding import PartitionSpec as P

OVL = 4
GROUP = 8
BF = jnp.bfloat16
F32 = jnp.float32
ANY = pl.BlockSpec(memory_space=pl.ANY)
DMA = pltpu.SemaphoreType.DMA


def params():
    return pltpu.CompilerParams(vmem_limit_bytes=63 * 1024 * 1024)


def cost(flops, nbytes):
    return pl.CostEstimate(flops=flops, bytes_accessed=nbytes, transcendentals=0)


def start(source, target, sem):
    copy = pltpu.make_async_copy(source, target, sem)
    copy.start()
    return copy


def wait_all(copies):
    for copy in copies:
        copy.wait()


def slot_target(list_ref, count_ref, slot):
    slots = list_ref.shape[2]
    peer, turn = slot // slots, slot % slots
    return list_ref[0, 0, turn, peer], turn < count_ref[0, 0, peer]


def start_packing(field, zero_ref, out_ref, list_ref, count_ref, sems):
    slots = out_ref.shape[1]
    copies = []
    for slot in range(out_ref.shape[0] * slots):
        row, used = slot_target(list_ref, count_ref, slot)
        target = out_ref.at[slot // slots, slot % slots]

        @pl.when(used)
        def _():
            pltpu.make_async_copy(field.at[row], target, sems.at[slot]).start()

        @pl.when(jnp.logical_not(used))
        def _():
            pltpu.make_async_copy(zero_ref, target, sems.at[slot]).start()

        copies.append(pltpu.make_async_copy(zero_ref, target, sems.at[slot]))
    return copies


def start_lists(list_hbm, count_hbm, list_ref, count_ref, sems):
    return [start(list_hbm, list_ref, sems.at[0]), start(count_hbm, count_ref, sems.at[1])]


def pack_rhs_kernel(list_hbm, count_hbm, rhs_hbm, out_hbm, head_hbm, tail_hbm, list_ref, count_ref, zero_ref, field_ref, in_sem, out_sem, row_sem):
    lists = start_lists(list_hbm, count_hbm, list_ref, count_ref, in_sem)
    field = start(rhs_hbm.at[0, 0], field_ref, in_sem.at[2])
    rows = field_ref.shape[0]
    zero_ref[...] = jnp.zeros_like(zero_ref)
    wait_all(lists)
    field.wait()
    copies = start_packing(field_ref, zero_ref, out_hbm, list_ref, count_ref, row_sem)
    copies.append(start(field_ref.at[pl.ds(0, OVL)], head_hbm, out_sem.at[0]))
    copies.append(start(field_ref.at[pl.ds(rows - OVL, OVL)], tail_hbm, out_sem.at[1]))
    wait_all(copies)


def start_extended(own, upper, lower, incoming, ext_ref, sems):
    rows = own.shape[0]
    copies = [
        start(own, ext_ref.at[pl.ds(0, rows)], sems.at[0]),
        start(incoming, ext_ref.at[pl.ds(rows + 2 * OVL, incoming.shape[0])], sems.at[3]),
        start(upper, ext_ref.at[pl.ds(rows, OVL)], sems.at[1]),
        start(lower, ext_ref.at[pl.ds(rows + OVL, OVL)], sems.at[2]),
    ]
    return copies


def start_blocks(blocks_hbm, first, chunk_ref, sems):
    copies = []
    for g in range(chunk_ref.shape[0] // GROUP):
        source = blocks_hbm.at[0, 0, pl.ds(first + g * GROUP, GROUP)]
        copies.append(start(source, chunk_ref.at[pl.ds(g * GROUP, GROUP)], sems.at[g]))
    return copies


def row_product(chunk_ref, index, cols_ref, row, ext_ref):
    terms = chunk_ref.shape[1]
    left = jnp.concatenate([chunk_ref[index, k] for k in range(terms)], axis=1)
    right = jnp.concatenate([ext_ref[cols_ref[0, k, 0, row]] for k in range(terms)], axis=0)
    return jnp.dot(left, right, preferred_element_type=F32)


def margin_kernel(cols_hbm, own_hbm, upper_hbm, lower_hbm, incoming_hbm, blocks_hbm, prev_hbm, next_hbm, cross_hbm, cols_ref, ext_ref, chunk_ref, part_ref, in_sem, block_sem, out_sem):
    own = own_hbm.at[0, 0]
    rows = own.shape[0]
    cols = start(cols_hbm, cols_ref, in_sem.at[4])
    pieces = start_extended(own, upper_hbm, lower_hbm, incoming_hbm, ext_ref, in_sem)
    blocks = start_blocks(blocks_hbm, rows, chunk_ref, block_sem)
    cols.wait()
    wait_all(pieces)
    copies = []
    for g, block in enumerate(blocks):
        block.wait()
        for j in range(GROUP):
            i = g * GROUP + j
            part_ref[i] = row_product(chunk_ref, i, cols_ref, rows + i, ext_ref).astype(BF)
        if g == 0:
            copies.append(start(part_ref.at[pl.ds(0, OVL)], prev_hbm, out_sem.at[0]))
            copies.append(start(part_ref.at[pl.ds(OVL, OVL)], next_hbm, out_sem.at[1]))
        else:
            source = part_ref.at[pl.ds(g * GROUP, GROUP)]
            target = cross_hbm.at[pl.ds(g * GROUP - 2 * OVL, GROUP)]
            copies.append(start(source, target, out_sem.at[g + 1]))
    wait_all(copies)


def own_kernel(cols_hbm, own_hbm, upper_hbm, lower_hbm, incoming_hbm, blocks_hbm, out_hbm, cols_ref, ext_ref, chunk_ref, part_ref, in_sem, block_sem, out_sem):
    own = own_hbm.at[0, 0]
    cols = start(cols_hbm, cols_ref, in_sem.at[4])
    pieces = start_extended(own, upper_hbm, lower_hbm, incoming_hbm, ext_ref, in_sem)
    blocks = start_blocks(blocks_hbm, 0, chunk_ref, block_sem)
    cols.wait()
    wait_all(pieces)
    copies = []
    for g, block in enumerate(blocks):
        block.wait()
        for j in range(GROUP):
            i = g * GROUP + j
            part_ref[i] = row_product(chunk_ref, i, cols_ref, i, ext_ref).astype(BF)
        rows = pl.ds(g * GROUP, GROUP)
        copies.append(start(part_ref.at[rows], out_hbm.at[rows], out_sem.at[g]))
    wait_all(copies)


def start_returns(partial_hbm, from_prev_hbm, from_next_hbm, returned_hbm, partial_ref, edge_ref, returned_ref, sems):
    return [
        start(partial_hbm, partial_ref, sems.at[2]),
        start(from_prev_hbm, edge_ref.at[0], sems.at[3]),
        start(from_next_hbm, edge_ref.at[1], sems.at[4]),
        start(returned_hbm, returned_ref, sems.at[5]),
    ]


def add_returns(total_ref, list_ref, count_ref, copies, partial_ref, edge_ref, returned_ref):
    rows = partial_ref.shape[0]
    copies[0].wait()
    total_ref[...] = partial_ref[...].astype(F32)
    copies[1].wait()
    total_ref[:OVL] += edge_ref[0].astype(F32)
    copies[2].wait()
    total_ref[rows - OVL :] += edge_ref[1].astype(F32)
    copies[3].wait()
    for slot in range(returned_ref.shape[0]):
        row, used = slot_target(list_ref, count_ref, slot)

        @pl.when(used)
        def _():
            total_ref[row] += returned_ref[slot].astype(F32)


def first_kernel(list_hbm, count_hbm, partial_hbm, from_prev_hbm, from_next_hbm, returned_hbm, first_hbm, out_hbm, head_hbm, tail_hbm, list_ref, count_ref, zero_ref, partial_ref, edge_ref, returned_ref, total_ref, in_sem, out_sem, row_sem):
    lists = start_lists(list_hbm, count_hbm, list_ref, count_ref, in_sem)
    copies = start_returns(partial_hbm, from_prev_hbm, from_next_hbm, returned_hbm, partial_ref, edge_ref, returned_ref, in_sem)
    zero_ref[...] = jnp.zeros_like(zero_ref)
    wait_all(lists)
    add_returns(total_ref, list_ref, count_ref, copies, partial_ref, edge_ref, returned_ref)
    partial_ref[...] = total_ref[...].astype(BF)
    finish_field(partial_ref, zero_ref, first_hbm, out_hbm, head_hbm, tail_hbm, list_ref, count_ref, out_sem, row_sem)


def finish_field(field_ref, zero_ref, field_hbm, out_hbm, head_hbm, tail_hbm, list_ref, count_ref, out_sem, row_sem):
    rows = field_ref.shape[0]
    copies = start_packing(field_ref, zero_ref, out_hbm, list_ref, count_ref, row_sem)
    copies.append(start(field_ref.at[pl.ds(0, OVL)], head_hbm, out_sem.at[0]))
    copies.append(start(field_ref.at[pl.ds(rows - OVL, OVL)], tail_hbm, out_sem.at[1]))
    copies.append(start(field_ref, field_hbm.at[0, 0], out_sem.at[2]))
    wait_all(copies)


def residual_kernel(cols_hbm, list_hbm, count_hbm, rhs_hbm, own_hbm, upper_hbm, lower_hbm, incoming_hbm, blocks_hbm, res_hbm, out_hbm, head_hbm, tail_hbm, cols_ref, list_ref, count_ref, zero_ref, rhs_ref, ext_ref, chunk_ref, in_sem, ext_sem, block_sem, out_sem, row_sem):
    own = own_hbm.at[0, 0]
    cols = start(cols_hbm, cols_ref, ext_sem.at[4])
    lists = start_lists(list_hbm, count_hbm, list_ref, count_ref, in_sem)
    pieces = start_extended(own, upper_hbm, lower_hbm, incoming_hbm, ext_ref, ext_sem)
    pieces.append(start(rhs_hbm.at[0, 0], rhs_ref, in_sem.at[2]))
    blocks = start_blocks(blocks_hbm, 0, chunk_ref, block_sem)
    zero_ref[...] = jnp.zeros_like(zero_ref)
    cols.wait()
    wait_all(lists)
    wait_all(pieces)
    for g, block in enumerate(blocks):
        block.wait()
        for j in range(GROUP):
            i = g * GROUP + j
            image = row_product(chunk_ref, i, cols_ref, i, ext_ref)
            rhs_ref[i] = (rhs_ref[i].astype(F32) - image).astype(BF)
    finish_field(rhs_ref, zero_ref, res_hbm, out_hbm, head_hbm, tail_hbm, list_ref, count_ref, out_sem, row_sem)


def second_kernel(list_hbm, count_hbm, first_hbm, partial_hbm, from_prev_hbm, from_next_hbm, returned_hbm, second_hbm, list_ref, count_ref, first_ref, partial_ref, edge_ref, returned_ref, total_ref, in_sem, out_sem):
    lists = start_lists(list_hbm, count_hbm, list_ref, count_ref, in_sem)
    copies = start_returns(partial_hbm, from_prev_hbm, from_next_hbm, returned_hbm, partial_ref, edge_ref, returned_ref, in_sem)
    base = start(first_hbm.at[0, 0], first_ref, in_sem.at[6])
    wait_all(lists)
    add_returns(total_ref, list_ref, count_ref, copies, partial_ref, edge_ref, returned_ref)
    base.wait()
    stores = []
    rows = first_ref.shape[0]
    for g in range(rows // GROUP):
        part = pl.ds(g * GROUP, GROUP)
        first_ref[part] = (first_ref[part].astype(F32) + total_ref[part]).astype(BF)
        stores.append(start(first_ref.at[part], second_hbm.at[0, 0, part], out_sem.at[g]))
    wait_all(stores)


def to_next(x):
    count = lax.axis_size("slab")
    return lax.ppermute(x, "slab", [(i, i + 1) for i in range(count - 1)])


def to_prev(x):
    count = lax.axis_size("slab")
    return lax.ppermute(x, "slab", [(i + 1, i) for i in range(count - 1)])


def route(buffer):
    return lax.all_to_all(buffer, "cross", split_axis=0, concat_axis=0, tiled=True)


def per_device(rhs, m_blocks, m_cols, j_blocks, j_cols, send_list, send_count):
    _, _, rows, block, vectors = rhs.shape
    peers, slots = send_list.shape[2:]
    listed = peers * slots
    extended_rows, terms = m_blocks.shape[2:4]
    margin_rows = extended_rows - rows
    tile = block * vectors
    out = jax.ShapeDtypeStruct
    field_t = out(rhs.shape, BF)
    packed_t = out((peers, slots, block, vectors), BF)
    edge_t = out((OVL, block, vectors), BF)
    partial_t = out((rows, block, vectors), BF)
    listed_t = out((listed, block, vectors), BF)

    m_cols = jnp.transpose(m_cols, (0, 3, 1, 2))
    j_cols = jnp.transpose(j_cols, (0, 3, 1, 2))
    send_list = jnp.transpose(send_list, (0, 1, 3, 2))

    def smem(x):
        return pltpu.SMEM(x.shape, jnp.int32)

    def tiles(count, dtype=BF):
        return pltpu.VMEM((count, block, vectors), dtype)

    def chunk(count):
        return pltpu.VMEM((count, terms, block, block), BF)

    lists = [smem(send_list), smem(send_count)]
    zero = pltpu.VMEM((block, vectors), BF)
    edges = pltpu.VMEM((2, OVL, block, vectors), BF)

    def call(kernel, name, out_shape, scratch, estimate, *operands):
        return pl.pallas_call(
            kernel,
            out_shape=out_shape,
            in_specs=[ANY] * len(operands),
            out_specs=jax.tree.map(lambda _: ANY, out_shape),
            scratch_shapes=scratch,
            compiler_params=params(),
            cost_estimate=estimate,
            name=name,
        )(*operands)

    packed, head, tail = call(
        pack_rhs_kernel,
        "pack_rhs",
        (packed_t, edge_t, edge_t),
        [*lists, zero, tiles(rows), DMA((3,)), DMA((2,)), DMA((listed,))],
        cost(0, 4 * rows * tile),
        send_list,
        send_count,
        rhs,
    )

    def extension(packed, head, tail):
        incoming = route(packed).reshape(listed, block, vectors)
        return to_next(tail), to_prev(head), incoming

    def precondition(field, upper, lower, incoming):
        to_p, to_n, cross = call(
            margin_kernel,
            "margin_partial",
            (edge_t, edge_t, listed_t),
            [smem(m_cols), tiles(extended_rows), chunk(margin_rows), tiles(margin_rows), DMA((5,)), DMA((margin_rows // GROUP,)), DMA((margin_rows // GROUP + 1,))],
            cost(2 * margin_rows * terms * block * tile, 12 * extended_rows * tile),
            m_cols,
            field,
            upper,
            lower,
            incoming,
            m_blocks,
        )
        returned = route(cross.reshape(peers, slots, block, vectors)).reshape(listed, block, vectors)
        from_next = to_prev(to_p)
        from_prev = to_next(to_n)
        own = call(
            own_kernel,
            "own_partial",
            partial_t,
            [smem(m_cols), tiles(extended_rows), chunk(rows), tiles(rows), DMA((5,)), DMA((rows // GROUP,)), DMA((rows // GROUP,))],
            cost(2 * rows * terms * block * tile, 12 * extended_rows * tile),
            m_cols,
            field,
            upper,
            lower,
            incoming,
            m_blocks,
        )
        return own, from_prev, from_next, returned

    upper, lower, incoming = extension(packed, head, tail)
    own, from_prev, from_next, returned = precondition(rhs, upper, lower, incoming)
    first, packed, head, tail = call(
        first_kernel,
        "assemble_first",
        (field_t, packed_t, edge_t, edge_t),
        [*lists, zero, tiles(rows), edges, tiles(listed), tiles(rows, F32), DMA((6,)), DMA((3,)), DMA((listed,))],
        cost(0, 10 * rows * tile),
        send_list,
        send_count,
        own,
        from_prev,
        from_next,
        returned,
    )
    upper, lower, incoming = extension(packed, head, tail)
    residual, packed, head, tail = call(
        residual_kernel,
        "residual",
        (field_t, packed_t, edge_t, edge_t),
        [smem(j_cols), *lists, zero, tiles(rows), tiles(extended_rows), chunk(rows), DMA((3,)), DMA((5,)), DMA((rows // GROUP,)), DMA((3,)), DMA((listed,))],
        cost(2 * rows * terms * block * tile, 12 * extended_rows * tile),
        j_cols,
        send_list,
        send_count,
        rhs,
        first,
        upper,
        lower,
        incoming,
        j_blocks,
    )
    upper, lower, incoming = extension(packed, head, tail)
    own, from_prev, from_next, returned = precondition(residual, upper, lower, incoming)
    return call(
        second_kernel,
        "assemble_second",
        field_t,
        [*lists, tiles(rows), tiles(rows), edges, tiles(listed), tiles(rows, F32), DMA((7,)), DMA((rows // GROUP,))],
        cost(0, 10 * rows * tile),
        send_list,
        send_count,
        first,
        own,
        from_prev,
        from_next,
        returned,
    )


def solution(mesh):
    return jax.shard_map(
        per_device,
        mesh=mesh,
        in_specs=(
            P("slab", "cross", None, None, None),
            P("slab", "cross", None, None, None, None),
            P("slab", "cross", None, None),
            P("slab", "cross", None, None, None, None),
            P("slab", "cross", None, None),
            P("slab", "cross", None, None),
            P("slab", "cross", None),
        ),
        out_specs=P("slab", "cross", None, None, None),
        check_vma=False,
    )
```

time: 263 us -> 191 us (0.73)
  local copies, waits for them, and re-layouts: 56.5 us -> 0.04 us
  other arithmetic: 35.4 us -> 0 us
  Pallas kernels: 0 us -> 35 us
  matrix products: 24.8 us -> 0 us
  waiting for transfers between devices: 96.4 us -> 105 us
    pallas_call x0 -> x8, Pallas kernels: none -> 35 us  [call(): pl.pallas_call(kernel, out_shape=out_shape, in_specs=[ANY] * len(operands...]
    gather x6 -> x0, local copies, waits for them, and re-layouts: 30.3 us -> none  [the longest x3 22.5 us: apply_set(): picked = jnp.take(extended, columns, axis=0)]
    dot_general x5 -> x0, matrix products: 24.8 us -> none  [the longest x3 20.8 us: apply_set(): lax.dot_general(blocks, picked, (((1, 3), (1, 2)), ((0,), (0,))), preferr...]
    concatenate x3 -> x0, other arithmetic: 8.35 us -> none  [extend(): jnp.concatenate([field, padded[:OVL], padded[owned + OVL:], incoming.resh...]
    all_to_all x5, waiting for transfers between devices: 77.3 us -> 84.2 us  [route(): lax.all_to_all(buffer, 'cross', split_axis=0, concat_axis=0, tiled=True)]
    scatter-add x4 -> x0, other arithmetic: 6.77 us -> none  [the longest x2 3.39 us: precondition(): total.at[owned - OVL:].add(returned_slab[3 * OVL:].astype(jnp.float32))]
    select_n x6 -> x0, other arithmetic: 6.6 us -> none  [the longest x3 6.01 us: extend(): jnp.where(flat_valid[:, None, None], outgoing, jnp.zeros((), jnp.bfloat16))]
    slice x5 -> x0, local copies, waits for them, and re-layouts: 6.3 us -> none  [the longest x3 4.32 us: extended_2(): lax.slice_in_dim(cells, cells.shape[dim] - width, cells.shape[dim], axis=...]
  transfers between devices with their start and end apart: 15 -> 15, of which waited for: 14 -> 13; matrix products, arithmetic and copies ran while one was open for 7% -> 0% of each run, Pallas kernels for 0% -> 5%
where the time goes in v2:
time: 191 us; the launch traced here: 190 us
  waiting for transfers between devices  105 us (55%)
  starting transfers between devices  49.5 us (26%)
  Pallas kernels  35 us (18%)
    all_to_all x5, waiting for transfers between devices, route(): lax.all_to_all(buffer, 'cross', split_axis=0, concat_axis=0, tiled=True)  84.2 us
    pallas_call x8, Pallas kernels, call(): pl.pallas_call(kernel, out_shape=out_shape, in_specs=[ANY] * len(operands...  35 us
    all_to_all x5, starting transfers between devices, route(): lax.all_to_all(buffer, 'cross', split_axis=0, concat_axis=0, tiled=True)  27 us
    ppermute x5, starting transfers between devices, to_next(): return lax.ppermute(x, 'slab', [(i, i + 1) for i in range(count - 1)])  16.1 us
    ppermute x5, waiting for transfers between devices, to_prev(): return lax.ppermute(x, 'slab', [(i + 1, i) for i in range(count - 1)])  15.1 us
    ppermute x5, starting transfers between devices, to_prev(): return lax.ppermute(x, 'slab', [(i + 1, i) for i in range(count - 1)])  6.46 us
    ppermute x5, waiting for transfers between devices, to_next(): return lax.ppermute(x, 'slab', [(i, i + 1) for i in range(count - 1)])  6.16 us
  transfers between devices with their start and end apart: 15, of which 13 were waited for; matrix products, arithmetic and copies ran while one was open for 0% of the time, Pallas kernels for 5%

profile of v2, /device:TPU:1, one launch (start us, length us, event | category | flops | bytes accessed | tf_op | source)
XLA Modules:
  0.0 190.3 jit_solution(443954196395546710)
XLA Ops:
  0.0 2.6 %pack_rhs.1 = (bf16[16,2,128,128]{3,2,1,0:T(8,128)(2,1)}, bf16[4,128,128]{2,1,0:T(8,128)(2,1)}, bf16[4,128,128]{2,1,0:T(8,128)(2,1)}) custom-call(s32[1,1,2,16]{3,2,1,0:T(2,128)} %bitcast.16, s32[1,1,16]{2,1,0:T(1,128)} %count_hbm.7, bf16[1,1,32,128,128]{4,3,2,1,0:T(8,128)(2,1)} %rhs_hbm.3), custom_call_target="tpu_custom_call" | custom-call | bytes 2097152 | tf_op jit(solution)/shard_map/pack_rhs/pallas_call | solution.py:274
  2.6 10.0 %all-to-all-start = ((bf16[16,2,128,128]{3,2,1,0:T(8,128)(2,1)}), bf16[16,2,128,128]{3,2,1,0:T(8,128)(2,1)}, u32[]{:S(2)}, u32[]{:S(2)}) async-start(bf16[16,2,128,128]{3,2,1,0:T(8,128)(2,1)} %get-tuple-element.24), calls=%async_computation | async-start | bytes 2097152 | tf_op jit(solution)/shard_map/all_to_all | solution.py:239
  12.6 3.2 %collective-permute-start = (bf16[4,128,128]{2,1,0:T(8,128)(2,1)}, bf16[4,128,128]{2,1,0:T(8,128)(2,1)S(1)}, u32[]{:S(2)}, u32[]{:S(2)}) collective-permute-start(bf16[4,128,128]{2,1,0:T(8,128)(2,1)} %get-tuple-element.22), channel_id=1, source_target_pairs={{0,16},{16,32},{32,48},{48,64},{64,80},{80,96},{96,112},{112,128},... | collective-permute-start | bytes 393224 | tf_op jit(solution)/shard_map/ppermute | solution.py:230
  15.8 1.3 collective-permute-start.1
  17.1 1.7 collective-permute-done.upper_hbm
  18.8 3.8 %collective-permute-done.1.lower_hbm = bf16[4,128,128]{2,1,0:T(8,128)(2,1)S(1)} collective-permute-done((bf16[4,128,128]{2,1,0:T(8,128)(2,1)}, bf16[4,128,128]{2,1,0:T(8,128)(2,1)S(1)}, u32[]{:S(2)}, u32[]{:S(2)}) %collective-permute-start.1) | collective-permute-done | bytes 131104 | tf_op jit(solution)/shard_map/ppermute | solution.py:235
  22.6 18.0 %all-to-all-done = bf16[16,2,128,128]{3,2,1,0:T(8,128)(2,1)} async-done(((bf16[16,2,128,128]{3,2,1,0:T(8,128)(2,1)}), bf16[16,2,128,128]{3,2,1,0:T(8,128)(2,1)}, u32[]{:S(2)}, u32[]{:S(2)}) %all-to-all-start) | async-done | bytes 1048608 | tf_op jit(solution)/shard_map/all_to_all | solution.py:239
  40.6 0.0 copy-done.1
  40.6 0.0 copy-done.3
  40.6 5.2 %margin_partial.2 = (bf16[4,128,128]{2,1,0:T(8,128)(2,1)}, bf16[4,128,128]{2,1,0:T(8,128)(2,1)}, bf16[32,128,128]{2,1,0:T(8,128)(2,1)}) custom-call(s32[1,3,1,72]{3,2,1,0:T(1,128)} %bitcast.12, bf16[1,1,32,128,128]{4,3,2,1,0:T(8,128)(2,1)} %rhs_hbm.3, bf16[4,128,128]{2,1,0:T(8,128)(2,1)} %copy-done.1, bf16[4,128,128]{2,1,0:T(8,128)(2,1)} %copy-done.3, ...), custom_call_target="tpu_custom_call" | custom-call | flops 503316480 | bytes 14155776 | tf_op jit(solution)/shard_map/margin_partial/pallas_call | solution.py:274
  45.9 4.2 %all-to-all-start.1 = ((bf16[16,2,128,128]{3,2,1,0:T(8,128)(2,1)}), bf16[16,2,128,128]{3,2,1,0:T(8,128)(2,1)}, u32[]{:S(2)}, u32[]{:S(2)}) async-start(bf16[16,2,128,128]{3,2,1,0:T(8,128)(2,1)} %bitcast.11), calls=%async_computation.1 | async-start | bytes 2097152 | tf_op jit(solution)/shard_map/all_to_all | solution.py:239
  50.1 3.2 %collective-permute-start.2 = (bf16[4,128,128]{2,1,0:T(8,128)(2,1)}, bf16[4,128,128]{2,1,0:T(8,128)(2,1)S(1)}, u32[]{:S(2)}, u32[]{:S(2)}) collective-permute-start(bf16[4,128,128]{2,1,0:T(8,128)(2,1)} %get-tuple-element.25), channel_id=1, source_target_pairs={{0,16},{16,32},{32,48},{48,64},{64,80},{80,96},{96,112},{112,128},... | collective-permute-start | bytes 393224 | tf_op jit(solution)/shard_map/ppermute | solution.py:230
  53.3 1.3 collective-permute-start.3
  54.6 4.6 %own_partial.2.partial_hbm = bf16[32,128,128]{2,1,0:T(8,128)(2,1)} custom-call(s32[1,3,1,72]{3,2,1,0:T(1,128)} %bitcast.13, bf16[1,1,32,128,128]{4,3,2,1,0:T(8,128)(2,1)} %rhs_hbm.3, bf16[4,128,128]{2,1,0:T(8,128)(2,1)} %copy-done.1, bf16[4,128,128]{2,1,0:T(8,128)(2,1)} %copy-done.3, bf16[32,128,128]{2,1,0:T(8,128)(2,1)} %bitcast.2.incoming_hbm, ...), custom_call_target="tpu_custom_call" | custom-call | flops 402653184 | bytes 14155776 | tf_op jit(solution)/shard_map/own_partial/pallas_call | solution.py:274
  59.2 0.0 collective-permute-done.2.from_prev_hbm
  59.2 0.0 copy-start.4
  59.3 1.6 collective-permute-done.3.from_next_hbm
  60.9 16.6 %all-to-all-done.1 = bf16[16,2,128,128]{3,2,1,0:T(8,128)(2,1)} async-done(((bf16[16,2,128,128]{3,2,1,0:T(8,128)(2,1)}), bf16[16,2,128,128]{3,2,1,0:T(8,128)(2,1)}, u32[]{:S(2)}, u32[]{:S(2)}) %all-to-all-start.1) | async-done | bytes 1048608 | tf_op jit(solution)/shard_map/all_to_all | solution.py:239
  77.4 0.0 copy-done.4
  77.4 0.0 copy-done.5
  77.5 3.8 %assemble_first.1 = (bf16[1,1,32,128,128]{4,3,2,1,0:T(8,128)(2,1)}, bf16[16,2,128,128]{3,2,1,0:T(8,128)(2,1)}, bf16[4,128,128]{2,1,0:T(8,128)(2,1)}, bf16[4,128,128]{2,1,0:T(8,128)(2,1)}) custom-call(s32[1,1,2,16]{3,2,1,0:T(2,128)} %bitcast.17, s32[1,1,16]{2,1,0:T(1,128)} %count_hbm.7, bf16[32,128,128]{2,1,0:T(8,128)(2,1)} %own_partial.2.partial_hbm, ...), custom_call_target="tpu_custom_call" | custom-call | bytes 5242880 | tf_op jit(solution)/shard_map/assemble_first/pallas_call | solution.py:274
  81.3 4.2 %all-to-all-start.2 = ((bf16[16,2,128,128]{3,2,1,0:T(8,128)(2,1)}), bf16[16,2,128,128]{3,2,1,0:T(8,128)(2,1)}, u32[]{:S(2)}, u32[]{:S(2)}) async-start(bf16[16,2,128,128]{3,2,1,0:T(8,128)(2,1)} %get-tuple-element.31), calls=%async_computation.2 | async-start | bytes 2097152 | tf_op jit(solution)/shard_map/all_to_all | solution.py:239
  85.5 3.2 %collective-permute-start.4 = (bf16[4,128,128]{2,1,0:T(8,128)(2,1)}, bf16[4,128,128]{2,1,0:T(8,128)(2,1)S(1)}, u32[]{:S(2)}, u32[]{:S(2)}) collective-permute-start(bf16[4,128,128]{2,1,0:T(8,128)(2,1)} %get-tuple-element.29), channel_id=1, source_target_pairs={{0,16},{16,32},{32,48},{48,64},{64,80},{80,96},{96,112},{112,128},... | collective-permute-start | bytes 393224 | tf_op jit(solution)/shard_map/ppermute | solution.py:230
  88.8 1.3 collective-permute-start.5
  90.1 2.2 %collective-permute-done.4.upper_hbm = bf16[4,128,128]{2,1,0:T(8,128)(2,1)S(1)} collective-permute-done((bf16[4,128,128]{2,1,0:T(8,128)(2,1)}, bf16[4,128,128]{2,1,0:T(8,128)(2,1)S(1)}, u32[]{:S(2)}, u32[]{:S(2)}) %collective-permute-start.4) | collective-permute-done | bytes 131104 | tf_op jit(solution)/shard_map/ppermute | solution.py:230
  92.3 4.0 %collective-permute-done.5.lower_hbm = bf16[4,128,128]{2,1,0:T(8,128)(2,1)S(1)} collective-permute-done((bf16[4,128,128]{2,1,0:T(8,128)(2,1)}, bf16[4,128,128]{2,1,0:T(8,128)(2,1)S(1)}, u32[]{:S(2)}, u32[]{:S(2)}) %collective-permute-start.5) | collective-permute-done | bytes 131104 | tf_op jit(solution)/shard_map/ppermute | solution.py:235
  96.3 16.6 %all-to-all-done.2 = bf16[16,2,128,128]{3,2,1,0:T(8,128)(2,1)} async-done(((bf16[16,2,128,128]{3,2,1,0:T(8,128)(2,1)}), bf16[16,2,128,128]{3,2,1,0:T(8,128)(2,1)}, u32[]{:S(2)}, u32[]{:S(2)}) %all-to-all-start.2) | async-done | bytes 1048608 | tf_op jit(solution)/shard_map/all_to_all | solution.py:239
  112.9 0.0 copy-done.6
  112.9 0.0 copy-done.7
  112.9 5.9 %residual.1 = (bf16[1,1,32,128,128]{4,3,2,1,0:T(8,128)(2,1)}, bf16[16,2,128,128]{3,2,1,0:T(8,128)(2,1)}, bf16[4,128,128]{2,1,0:T(8,128)(2,1)}, bf16[4,128,128]{2,1,0:T(8,128)(2,1)}) custom-call(s32[1,3,1,32]{3,2,1,0:T(1,128)} %bitcast.20, s32[1,1,2,16]{3,2,1,0:T(2,128)} %bitcast.18, s32[1,1,16]{2,1,0:T(1,128)} %count_hbm.7, ...), custom_call_target="tpu_custom_call" | custom-call | flops 402653184 | bytes 14155776 | tf_op jit(solution)/shard_map/residual/pallas_call | solution.py:274
  118.8 4.2 %all-to-all-start.3 = ((bf16[16,2,128,128]{3,2,1,0:T(8,128)(2,1)}), bf16[16,2,128,128]{3,2,1,0:T(8,128)(2,1)}, u32[]{:S(2)}, u32[]{:S(2)}) async-start(bf16[16,2,128,128]{3,2,1,0:T(8,128)(2,1)} %get-tuple-element.35), calls=%async_computation.3 | async-start | bytes 2097152 | tf_op jit(solution)/shard_map/all_to_all | solution.py:239
  123.1 3.2 %collective-permute-start.6 = (bf16[4,128,128]{2,1,0:T(8,128)(2,1)}, bf16[4,128,128]{2,1,0:T(8,128)(2,1)S(1)}, u32[]{:S(2)}, u32[]{:S(2)}) collective-permute-start(bf16[4,128,128]{2,1,0:T(8,128)(2,1)} %get-tuple-element.33), channel_id=1, source_target_pairs={{0,16},{16,32},{32,48},{48,64},{64,80},{80,96},{96,112},{112,128},... | collective-permute-start | bytes 393224 | tf_op jit(solution)/shard_map/ppermute | solution.py:230
  126.3 1.3 collective-permute-start.7
  127.6 2.2 %collective-permute-done.6.upper_hbm = bf16[4,128,128]{2,1,0:T(8,128)(2,1)S(1)} collective-permute-done((bf16[4,128,128]{2,1,0:T(8,128)(2,1)}, bf16[4,128,128]{2,1,0:T(8,128)(2,1)S(1)}, u32[]{:S(2)}, u32[]{:S(2)}) %collective-permute-start.6) | collective-permute-done | bytes 131104 | tf_op jit(solution)/shard_map/ppermute | solution.py:230
  129.8 4.0 %collective-permute-done.7.lower_hbm = bf16[4,128,128]{2,1,0:T(8,128)(2,1)S(1)} collective-permute-done((bf16[4,128,128]{2,1,0:T(8,128)(2,1)}, bf16[4,128,128]{2,1,0:T(8,128)(2,1)S(1)}, u32[]{:S(2)}, u32[]{:S(2)}) %collective-permute-start.7) | collective-permute-done | bytes 131104 | tf_op jit(solution)/shard_map/ppermute | solution.py:235
  133.9 16.5 %all-to-all-done.3 = bf16[16,2,128,128]{3,2,1,0:T(8,128)(2,1)} async-done(((bf16[16,2,128,128]{3,2,1,0:T(8,128)(2,1)}), bf16[16,2,128,128]{3,2,1,0:T(8,128)(2,1)}, u32[]{:S(2)}, u32[]{:S(2)}) %all-to-all-start.3) | async-done | bytes 1048608 | tf_op jit(solution)/shard_map/all_to_all | solution.py:239
  150.4 0.0 copy-done
  150.4 5.2 %margin_partial.3 = (bf16[4,128,128]{2,1,0:T(8,128)(2,1)}, bf16[4,128,128]{2,1,0:T(8,128)(2,1)}, bf16[32,128,128]{2,1,0:T(8,128)(2,1)}) custom-call(s32[1,3,1,72]{3,2,1,0:T(1,128)} %bitcast.14, bf16[1,1,32,128,128]{4,3,2,1,0:T(8,128)(2,1)} %get-tuple-element.32.own_hbm, bf16[4,128,128]{2,1,0:T(8,128)(2,1)} %copy-done, bf16[4,128,128]{2,1,0:T(8,128)(2,1)} %copy-done.2, ...), custom_call_target="tpu_custom_call" | custom-call | flops 503316480 | bytes 14155776 | tf_op jit(solution)/shard_map/margin_partial/pallas_call | solution.py:274
  155.7 4.2 %all-to-all-start.4 = ((bf16[16,2,128,128]{3,2,1,0:T(8,128)(2,1)}), bf16[16,2,128,128]{3,2,1,0:T(8,128)(2,1)}, u32[]{:S(2)}, u32[]{:S(2)}) async-start(bf16[16,2,128,128]{3,2,1,0:T(8,128)(2,1)} %bitcast.10), calls=%async_computation.4 | async-start | bytes 2097152 | tf_op jit(solution)/shard_map/all_to_all | solution.py:239
  159.9 3.2 %collective-permute-start.8 = (bf16[4,128,128]{2,1,0:T(8,128)(2,1)}, bf16[4,128,128]{2,1,0:T(8,128)(2,1)S(1)}, u32[]{:S(2)}, u32[]{:S(2)}) collective-permute-start(bf16[4,128,128]{2,1,0:T(8,128)(2,1)} %get-tuple-element.36), channel_id=1, source_target_pairs={{0,16},{16,32},{32,48},{48,64},{64,80},{80,96},{96,112},{112,128},... | collective-permute-start | bytes 393224 | tf_op jit(solution)/shard_map/ppermute | solution.py:230
  163.2 1.3 collective-permute-start.9
  164.5 4.6 %own_partial.3.partial_hbm = bf16[32,128,128]{2,1,0:T(8,128)(2,1)} custom-call(s32[1,3,1,72]{3,2,1,0:T(1,128)} %bitcast.15, bf16[1,1,32,128,128]{4,3,2,1,0:T(8,128)(2,1)} %get-tuple-element.32.own_hbm, bf16[4,128,128]{2,1,0:T(8,128)(2,1)} %copy-done, bf16[4,128,128]{2,1,0:T(8,128)(2,1)} %copy-done.2, bf16[32,128,128]{2,1,0:T(8,128)(2,1)} %bitcast.7.incoming_hbm, ...), custom_call_target="tpu_custom_call" | custom-call | flops 402653184 | bytes 14155776 | tf_op jit(solution)/shard_map/own_partial/pallas_call | solution.py:274
  169.1 0.0 collective-permute-done.8.from_prev_hbm
  169.1 0.0 copy-start.8
  169.1 1.6 collective-permute-done.9.from_next_hbm
  170.7 16.5 %all-to-all-done.4 = bf16[16,2,128,128]{3,2,1,0:T(8,128)(2,1)} async-done(((bf16[16,2,128,128]{3,2,1,0:T(8,128)(2,1)}), bf16[16,2,128,128]{3,2,1,0:T(8,128)(2,1)}, u32[]{:S(2)}, u32[]{:S(2)}) %all-to-all-start.4) | async-done | bytes 1048608 | tf_op jit(solution)/shard_map/all_to_all | solution.py:239
  187.2 0.0 copy-done.9
  187.2 3.0 %assemble_second.1 = bf16[1,1,32,128,128]{4,3,2,1,0:T(8,128)(2,1)} custom-call(s32[1,1,2,16]{3,2,1,0:T(2,128)} %bitcast.19, s32[1,1,16]{2,1,0:T(1,128)} %count_hbm.7, bf16[1,1,32,128,128]{4,3,2,1,0:T(8,128)(2,1)} %get-tuple-element.28.own_hbm.first_hbm, bf16[32,128,128]{2,1,0:T(8,128)(2,1)} %own_partial.3.partial_hbm, bf16[4,128,128]{2,1,0:T(8,128)(2,1)} %copy-done.8, ...), custom_call_target="tpu_custom_call" | custom-call | bytes 5242880 | tf_op jit(solution)/shard_map/assemble_second/pallas_call | solution.py:274
  (10 shorter events, 0.0 us)
Async XLA Ops:
  2.6 38.0 %all-to-all-start = ((bf16[16,2,128,128]{3,2,1,0:T(8,128)(2,1)}), bf16[16,2,128,128]{3,2,1,0:T(8,128)(2,1)}, u32[]{:S(2)}, u32[]{:S(2)}) async-start(bf16[16,2,128,128]{3,2,1,0:T(8,128)(2,1)} %get-tuple-element.24), calls=%async_computation | async-start | bytes 2097152 | tf_op jit(solution)/shard_map/all_to_all | solution.py:239
  12.6 6.2 %collective-permute-start = (bf16[4,128,128]{2,1,0:T(8,128)(2,1)}, bf16[4,128,128]{2,1,0:T(8,128)(2,1)S(1)}, u32[]{:S(2)}, u32[]{:S(2)}) collective-permute-start(bf16[4,128,128]{2,1,0:T(8,128)(2,1)} %get-tuple-element.22), channel_id=1, source_target_pairs={{0,16},{16,32},{32,48},{48,64},{64,80},{80,96},{96,112},{112,128},... | collective-permute-start | bytes 393224 | tf_op jit(solution)/shard_map/ppermute | solution.py:230
  15.8 6.8 %collective-permute-start.1 = (bf16[4,128,128]{2,1,0:T(8,128)(2,1)}, bf16[4,128,128]{2,1,0:T(8,128)(2,1)S(1)}, u32[]{:S(2)}, u32[]{:S(2)}) collective-permute-start(bf16[4,128,128]{2,1,0:T(8,128)(2,1)} %get-tuple-element.23), channel_id=1, source_target_pairs={{16,0},{32,16},{48,32},{64,48},{80,64},{96,80},{112,96},{128,112},... | collective-permute-start | bytes 393224 | tf_op jit(solution)/shard_map/ppermute | solution.py:235
  18.8 21.8 %copy-start.1 = (bf16[4,128,128]{2,1,0:T(8,128)(2,1)}, bf16[4,128,128]{2,1,0:T(8,128)(2,1)S(1)}, u32[]{:S(2)}) copy-start(bf16[4,128,128]{2,1,0:T(8,128)(2,1)S(1)} %collective-permute-done.upper_hbm) | copy-start | bytes 393220
  22.6 18.0 %copy-start.3 = (bf16[4,128,128]{2,1,0:T(8,128)(2,1)}, bf16[4,128,128]{2,1,0:T(8,128)(2,1)S(1)}, u32[]{:S(2)}) copy-start(bf16[4,128,128]{2,1,0:T(8,128)(2,1)S(1)} %collective-permute-done.1.lower_hbm) | copy-start | bytes 393220
  45.9 31.6 %all-to-all-start.1 = ((bf16[16,2,128,128]{3,2,1,0:T(8,128)(2,1)}), bf16[16,2,128,128]{3,2,1,0:T(8,128)(2,1)}, u32[]{:S(2)}, u32[]{:S(2)}) async-start(bf16[16,2,128,128]{3,2,1,0:T(8,128)(2,1)} %bitcast.11), calls=%async_computation.1 | async-start | bytes 2097152 | tf_op jit(solution)/shard_map/all_to_all | solution.py:239
  50.1 9.1 %collective-permute-start.2 = (bf16[4,128,128]{2,1,0:T(8,128)(2,1)}, bf16[4,128,128]{2,1,0:T(8,128)(2,1)S(1)}, u32[]{:S(2)}, u32[]{:S(2)}) collective-permute-start(bf16[4,128,128]{2,1,0:T(8,128)(2,1)} %get-tuple-element.25), channel_id=1, source_target_pairs={{0,16},{16,32},{32,48},{48,64},{64,80},{80,96},{96,112},{112,128},... | collective-permute-start | bytes 393224 | tf_op jit(solution)/shard_map/ppermute | solution.py:230
  53.3 7.5 %collective-permute-start.3 = (bf16[4,128,128]{2,1,0:T(8,128)(2,1)}, bf16[4,128,128]{2,1,0:T(8,128)(2,1)S(1)}, u32[]{:S(2)}, u32[]{:S(2)}) collective-permute-start(bf16[4,128,128]{2,1,0:T(8,128)(2,1)} %get-tuple-element.26), channel_id=1, source_target_pairs={{16,0},{32,16},{48,32},{64,48},{80,64},{96,80},{112,96},{128,112},... | collective-permute-start | bytes 393224 | tf_op jit(solution)/shard_map/ppermute | solution.py:235
  59.2 18.2 %copy-start.4 = (bf16[4,128,128]{2,1,0:T(8,128)(2,1)}, bf16[4,128,128]{2,1,0:T(8,128)(2,1)S(1)}, u32[]{:S(2)}) copy-start(bf16[4,128,128]{2,1,0:T(8,128)(2,1)S(1)} %collective-permute-done.2.from_prev_hbm) | copy-start | bytes 393220
  60.9 16.6 %copy-start.5 = (bf16[4,128,128]{2,1,0:T(8,128)(2,1)}, bf16[4,128,128]{2,1,0:T(8,128)(2,1)S(1)}, u32[]{:S(2)}) copy-start(bf16[4,128,128]{2,1,0:T(8,128)(2,1)S(1)} %collective-permute-done.3.from_next_hbm) | copy-start | bytes 393220
  81.3 31.6 %all-to-all-start.2 = ((bf16[16,2,128,128]{3,2,1,0:T(8,128)(2,1)}), bf16[16,2,128,128]{3,2,1,0:T(8,128)(2,1)}, u32[]{:S(2)}, u32[]{:S(2)}) async-start(bf16[16,2,128,128]{3,2,1,0:T(8,128)(2,1)} %get-tuple-element.31), calls=%async_computation.2 | async-start | bytes 2097152 | tf_op jit(solution)/shard_map/all_to_all | solution.py:239
  85.5 6.8 %collective-permute-start.4 = (bf16[4,128,128]{2,1,0:T(8,128)(2,1)}, bf16[4,128,128]{2,1,0:T(8,128)(2,1)S(1)}, u32[]{:S(2)}, u32[]{:S(2)}) collective-permute-start(bf16[4,128,128]{2,1,0:T(8,128)(2,1)} %get-tuple-element.29), channel_id=1, source_target_pairs={{0,16},{16,32},{32,48},{48,64},{64,80},{80,96},{96,112},{112,128},... | collective-permute-start | bytes 393224 | tf_op jit(solution)/shard_map/ppermute | solution.py:230
  88.8 7.5 %collective-permute-start.5 = (bf16[4,128,128]{2,1,0:T(8,128)(2,1)}, bf16[4,128,128]{2,1,0:T(8,128)(2,1)S(1)}, u32[]{:S(2)}, u32[]{:S(2)}) collective-permute-start(bf16[4,128,128]{2,1,0:T(8,128)(2,1)} %get-tuple-element.30), channel_id=1, source_target_pairs={{16,0},{32,16},{48,32},{64,48},{80,64},{96,80},{112,96},{128,112},... | collective-permute-start | bytes 393224 | tf_op jit(solution)/shard_map/ppermute | solution.py:235
  92.3 20.6 %copy-start.6 = (bf16[4,128,128]{2,1,0:T(8,128)(2,1)}, bf16[4,128,128]{2,1,0:T(8,128)(2,1)S(1)}, u32[]{:S(2)}) copy-start(bf16[4,128,128]{2,1,0:T(8,128)(2,1)S(1)} %collective-permute-done.4.upper_hbm) | copy-start | bytes 393220
  96.3 16.6 %copy-start.7 = (bf16[4,128,128]{2,1,0:T(8,128)(2,1)}, bf16[4,128,128]{2,1,0:T(8,128)(2,1)S(1)}, u32[]{:S(2)}) copy-start(bf16[4,128,128]{2,1,0:T(8,128)(2,1)S(1)} %collective-permute-done.5.lower_hbm) | copy-start | bytes 393220
  118.8 31.6 %all-to-all-start.3 = ((bf16[16,2,128,128]{3,2,1,0:T(8,128)(2,1)}), bf16[16,2,128,128]{3,2,1,0:T(8,128)(2,1)}, u32[]{:S(2)}, u32[]{:S(2)}) async-start(bf16[16,2,128,128]{3,2,1,0:T(8,128)(2,1)} %get-tuple-element.35), calls=%async_computation.3 | async-start | bytes 2097152 | tf_op jit(solution)/shard_map/all_to_all | solution.py:239
  123.1 6.7 %collective-permute-start.6 = (bf16[4,128,128]{2,1,0:T(8,128)(2,1)}, bf16[4,128,128]{2,1,0:T(8,128)(2,1)S(1)}, u32[]{:S(2)}, u32[]{:S(2)}) collective-permute-start(bf16[4,128,128]{2,1,0:T(8,128)(2,1)} %get-tuple-element.33), channel_id=1, source_target_pairs={{0,16},{16,32},{32,48},{48,64},{64,80},{80,96},{96,112},{112,128},... | collective-permute-start | bytes 393224 | tf_op jit(solution)/shard_map/ppermute | solution.py:230
  126.3 7.5 %collective-permute-start.7 = (bf16[4,128,128]{2,1,0:T(8,128)(2,1)}, bf16[4,128,128]{2,1,0:T(8,128)(2,1)S(1)}, u32[]{:S(2)}, u32[]{:S(2)}) collective-permute-start(bf16[4,128,128]{2,1,0:T(8,128)(2,1)} %get-tuple-element.34), channel_id=1, source_target_pairs={{16,0},{32,16},{48,32},{64,48},{80,64},{96,80},{112,96},{128,112},... | collective-permute-start | bytes 393224 | tf_op jit(solution)/shard_map/ppermute | solution.py:235
  129.8 20.6 %copy-start = (bf16[4,128,128]{2,1,0:T(8,128)(2,1)}, bf16[4,128,128]{2,1,0:T(8,128)(2,1)S(1)}, u32[]{:S(2)}) copy-start(bf16[4,128,128]{2,1,0:T(8,128)(2,1)S(1)} %collective-permute-done.6.upper_hbm) | copy-start | bytes 393220
  133.9 16.5 %copy-start.2 = (bf16[4,128,128]{2,1,0:T(8,128)(2,1)}, bf16[4,128,128]{2,1,0:T(8,128)(2,1)S(1)}, u32[]{:S(2)}) copy-start(bf16[4,128,128]{2,1,0:T(8,128)(2,1)S(1)} %collective-permute-done.7.lower_hbm) | copy-start | bytes 393220
  155.7 31.6 %all-to-all-start.4 = ((bf16[16,2,128,128]{3,2,1,0:T(8,128)(2,1)}), bf16[16,2,128,128]{3,2,1,0:T(8,128)(2,1)}, u32[]{:S(2)}, u32[]{:S(2)}) async-start(bf16[16,2,128,128]{3,2,1,0:T(8,128)(2,1)} %bitcast.10), calls=%async_computation.4 | async-start | bytes 2097152 | tf_op jit(solution)/shard_map/all_to_all | solution.py:239
  159.9 9.1 %collective-permute-start.8 = (bf16[4,128,128]{2,1,0:T(8,128)(2,1)}, bf16[4,128,128]{2,1,0:T(8,128)(2,1)S(1)}, u32[]{:S(2)}, u32[]{:S(2)}) collective-permute-start(bf16[4,128,128]{2,1,0:T(8,128)(2,1)} %get-tuple-element.36), channel_id=1, source_target_pairs={{0,16},{16,32},{32,48},{48,64},{64,80},{80,96},{96,112},{112,128},... | collective-permute-start | bytes 393224 | tf_op jit(solution)/shard_map/ppermute | solution.py:230
  163.2 7.6 %collective-permute-start.9 = (bf16[4,128,128]{2,1,0:T(8,128)(2,1)}, bf16[4,128,128]{2,1,0:T(8,128)(2,1)S(1)}, u32[]{:S(2)}, u32[]{:S(2)}) collective-permute-start(bf16[4,128,128]{2,1,0:T(8,128)(2,1)} %get-tuple-element.37), channel_id=1, source_target_pairs={{16,0},{32,16},{48,32},{64,48},{80,64},{96,80},{112,96},{128,112},... | collective-permute-start | bytes 393224 | tf_op jit(solution)/shard_map/ppermute | solution.py:235
  169.1 18.2 %copy-start.8 = (bf16[4,128,128]{2,1,0:T(8,128)(2,1)}, bf16[4,128,128]{2,1,0:T(8,128)(2,1)S(1)}, u32[]{:S(2)}) copy-start(bf16[4,128,128]{2,1,0:T(8,128)(2,1)S(1)} %collective-permute-done.8.from_prev_hbm) | copy-start | bytes 393220
  170.7 16.5 %copy-start.9 = (bf16[4,128,128]{2,1,0:T(8,128)(2,1)}, bf16[4,128,128]{2,1,0:T(8,128)(2,1)S(1)}, u32[]{:S(2)}) copy-start(bf16[4,128,128]{2,1,0:T(8,128)(2,1)S(1)} %collective-permute-done.9.from_next_hbm) | copy-start | bytes 393220

commit v3 on v2

v3 whole, which is shorter than its diff:
```python
import functools

import jax
import jax.numpy as jnp
from jax import lax
from jax.experimental import pallas as pl
from jax.experimental.pallas import tpu as pltpu
from jax.sharding import PartitionSpec as P

OVL = 4
GROUP = 8
BF = jnp.bfloat16
F32 = jnp.float32
HBM = pl.BlockSpec(memory_space=pltpu.HBM)
VMEM = pl.BlockSpec(memory_space=pltpu.VMEM)
DMA = pltpu.SemaphoreType.DMA


def params():
    return pltpu.CompilerParams(vmem_limit_bytes=36 * 1024 * 1024)


def cost(flops, nbytes):
    return pl.CostEstimate(flops=flops, bytes_accessed=nbytes, transcendentals=0)


def start(source, target, sem):
    copy = pltpu.make_async_copy(source, target, sem)
    copy.start()
    return copy


def wait_all(copies):
    for copy in copies:
        copy.wait()


def slot_target(list_ref, count_ref, slot):
    slots = list_ref.shape[2]
    peer, turn = slot // slots, slot % slots
    return list_ref[0, 0, turn, peer], turn < count_ref[0, 0, peer]


def start_packing(field_ref, packed_ref, out_hbm, list_ref, count_ref, sems):
    slots = out_hbm.shape[1]
    peers = GROUP // slots
    copies = []
    for g in range(packed_ref.shape[0] // GROUP):
        for slot in range(g * GROUP, (g + 1) * GROUP):
            row, used = slot_target(list_ref, count_ref, slot)
            packed_ref[slot] = jnp.where(used, field_ref[row], jnp.zeros((), BF))
        for peer in range(g * peers, (g + 1) * peers):
            copies.append(start(packed_ref.at[pl.ds(peer * slots, slots)], out_hbm.at[peer], sems.at[peer]))
    return copies


def start_lists(list_hbm, count_hbm, list_ref, count_ref, sems):
    return [start(list_hbm, list_ref, sems.at[0]), start(count_hbm, count_ref, sems.at[1])]


def pack_rhs_kernel(list_hbm, count_hbm, rhs_hbm, out_hbm, head_hbm, tail_hbm, list_ref, count_ref, packed_ref, field_ref, in_sem, out_sem, row_sem):
    lists = start_lists(list_hbm, count_hbm, list_ref, count_ref, in_sem)
    field = start(rhs_hbm.at[0, 0], field_ref, in_sem.at[2])
    rows = field_ref.shape[0]
    wait_all(lists)
    field.wait()
    copies = start_packing(field_ref, packed_ref, out_hbm, list_ref, count_ref, row_sem)
    copies.append(start(field_ref.at[pl.ds(0, OVL)], head_hbm, out_sem.at[0]))
    copies.append(start(field_ref.at[pl.ds(rows - OVL, OVL)], tail_hbm, out_sem.at[1]))
    wait_all(copies)


def start_blocks(blocks_hbm, first, chunk_ref, sems, order):
    copies = []
    for g in order:
        source = blocks_hbm.at[0, 0, pl.ds(first + g * GROUP, GROUP)]
        copies.append(start(source, chunk_ref.at[pl.ds(g * GROUP, GROUP)], sems.at[g]))
    return copies


def picked_product(chunk_ref, index, terms, picks, ext_ref):
    left = jnp.concatenate([chunk_ref[index, k] for k in terms], axis=1)
    right = jnp.concatenate([ext_ref[pick] for pick in picks], axis=0)
    return jnp.dot(left, right, preferred_element_type=F32)


def row_product(chunk_ref, index, cols_ref, row, ext_ref):
    terms = range(chunk_ref.shape[1])
    return picked_product(chunk_ref, index, terms, [cols_ref[0, k, 0, row] for k in terms], ext_ref)


def stage_kernel(own_hbm, upper_hbm, lower_hbm, near_ref, sems):
    rows = own_hbm.shape[2]
    wait_all([
        start(own_hbm.at[0, 0], near_ref.at[pl.ds(0, rows)], sems.at[0]),
        start(upper_hbm, near_ref.at[pl.ds(rows, OVL)], sems.at[1]),
        start(lower_hbm, near_ref.at[pl.ds(rows + OVL, OVL)], sems.at[2]),
    ])


def half_row(low_ref, high_ref, row):
    half = low_ref.shape[0]
    return low_ref.at[row] if row < half else high_ref.at[row - half]


def near_residual_kernel(cols_hbm, blocks_hbm, rhs_hbm, own_hbm, upper_hbm, lower_hbm, low_ref, high_ref, cols_ref, ext_ref, chunk_ref, rhs_ref, in_sem, cols_sem, block_sem):
    rows = rhs_ref.shape[0]
    near = ext_ref.shape[0] - 1
    cols = start(cols_hbm, cols_ref, cols_sem.at[0])
    pieces = start_near(own_hbm, upper_hbm, lower_hbm, ext_ref, in_sem)
    pieces.append(start(rhs_hbm.at[0, 0], rhs_ref, in_sem.at[3]))
    groups = range(rows // GROUP)
    blocks = start_blocks(blocks_hbm, 0, chunk_ref, block_sem, groups)
    ext_ref[near] = jnp.zeros_like(ext_ref[near])
    cols.wait()
    wait_all(pieces)
    terms = chunk_ref.shape[1]
    for g, block in zip(groups, blocks):
        block.wait()
        for j in range(GROUP):
            i = g * GROUP + j
            picks = [jnp.minimum(cols_ref[0, k, 0, i], near) for k in range(terms)]
            half_row(low_ref, high_ref, i)[...] = rhs_ref[i].astype(F32) - picked_product(chunk_ref, i, range(terms), picks, ext_ref)


def fill_extended(near_ref, incoming_ref, ext_ref):
    near = near_ref.shape[0]
    ext_ref[:near] = near_ref[...]
    ext_ref[near:] = incoming_ref[...]


def margin_kernel(cols_hbm, blocks_hbm, near_ref, incoming_ref, cross_hbm, cols_ref, ext_ref, chunk_ref, part_ref, in_sem, block_sem, out_sem):
    cols = start(cols_hbm, cols_ref, in_sem.at[0])
    near = near_ref.shape[0]
    groups = range(chunk_ref.shape[0] // GROUP)
    blocks = start_blocks(blocks_hbm, near, chunk_ref, block_sem, groups)
    fill_extended(near_ref, incoming_ref, ext_ref)
    cols.wait()
    copies = []
    for g, block in zip(groups, blocks):
        block.wait()
        for j in range(GROUP):
            i = g * GROUP + j
            part_ref[i] = row_product(chunk_ref, i, cols_ref, near + i, ext_ref).astype(BF)
        part = pl.ds(g * GROUP, GROUP)
        copies.append(start(part_ref.at[part], cross_hbm.at[part], out_sem.at[g]))
    wait_all(copies)


def start_near(own_hbm, upper_hbm, lower_hbm, ext_ref, sems):
    rows = own_hbm.shape[2]
    return [
        start(own_hbm.at[0, 0], ext_ref.at[pl.ds(0, rows)], sems.at[0]),
        start(upper_hbm, ext_ref.at[pl.ds(rows, OVL)], sems.at[1]),
        start(lower_hbm, ext_ref.at[pl.ds(rows + OVL, OVL)], sems.at[2]),
    ]


def own_kernel(cols_hbm, blocks_hbm, own_hbm, upper_hbm, lower_hbm, incoming_ref, part_ref, prev_hbm, next_hbm, cols_ref, ext_ref, chunk_ref, edge_ref, in_sem, cols_sem, block_sem, out_sem):
    rows = part_ref.shape[0]
    cols = start(cols_hbm, cols_ref, cols_sem.at[0])
    pieces = start_near(own_hbm, upper_hbm, lower_hbm, ext_ref, in_sem)
    last = rows // GROUP
    order = [last, *range(last)]
    blocks = start_blocks(blocks_hbm, 0, chunk_ref, block_sem, order)
    ext_ref[rows + 2 * OVL :] = incoming_ref[...]
    cols.wait()
    wait_all(pieces)
    copies = []
    for g, block in zip(order, blocks):
        block.wait()
        for j in range(GROUP):
            i = g * GROUP + j
            value = row_product(chunk_ref, i, cols_ref, i, ext_ref).astype(BF)
            if g == last:
                edge_ref[j] = value
            else:
                part_ref[i] = value
        if g == last:
            copies.append(start(edge_ref.at[pl.ds(0, OVL)], prev_hbm, out_sem.at[0]))
            copies.append(start(edge_ref.at[pl.ds(OVL, OVL)], next_hbm, out_sem.at[1]))
    wait_all(copies)


def add_returns(sum_ref, list_ref, count_ref, lists, edges, edge_ref, part_ref, returned_ref):
    rows = part_ref.shape[0]
    sum_ref[...] = part_ref[...].astype(F32)
    wait_all(lists)
    for slot in range(returned_ref.shape[0]):
        row, used = slot_target(list_ref, count_ref, slot)
        sum_ref[row] += jnp.where(used, returned_ref[slot].astype(F32), 0.0)

    wait_all(edges)
    sum_ref[:OVL] += edge_ref[0].astype(F32)
    sum_ref[rows - OVL :] += edge_ref[1].astype(F32)


def start_edges(from_prev_hbm, from_next_hbm, edge_ref, sems):
    return [start(from_prev_hbm, edge_ref.at[0], sems.at[0]), start(from_next_hbm, edge_ref.at[1], sems.at[1])]


def first_kernel(list_hbm, count_hbm, from_prev_hbm, from_next_hbm, part_ref, returned_ref, first_hbm, out_hbm, head_hbm, tail_hbm, list_ref, count_ref, edge_ref, packed_ref, field_ref, sum_ref, in_sem, edge_sem, out_sem, row_sem):
    lists = start_lists(list_hbm, count_hbm, list_ref, count_ref, in_sem)
    edges = start_edges(from_prev_hbm, from_next_hbm, edge_ref, edge_sem)
    add_returns(sum_ref, list_ref, count_ref, lists, edges, edge_ref, part_ref, returned_ref)
    field_ref[...] = sum_ref[...].astype(BF)
    finish_field(field_ref, packed_ref, first_hbm, out_hbm, head_hbm, tail_hbm, list_ref, count_ref, out_sem, row_sem)


def finish_field(field_ref, packed_ref, field_hbm, out_hbm, head_hbm, tail_hbm, list_ref, count_ref, out_sem, row_sem):
    rows = field_ref.shape[0]
    copies = [start(field_ref, field_hbm.at[0, 0], out_sem.at[2])]
    copies += start_packing(field_ref, packed_ref, out_hbm, list_ref, count_ref, row_sem)
    copies.append(start(field_ref.at[pl.ds(0, OVL)], head_hbm, out_sem.at[0]))
    copies.append(start(field_ref.at[pl.ds(rows - OVL, OVL)], tail_hbm, out_sem.at[1]))
    wait_all(copies)


def listed_residual_kernel(near, cols_hbm, list_hbm, count_hbm, blocks_hbm, low_ref, high_ref, incoming_ref, out_hbm, cols_ref, list_ref, count_ref, packed_ref, ext_ref, chunk_ref, res_ref, in_sem, cols_sem, block_sem, row_sem):
    cols = start(cols_hbm, cols_ref, cols_sem.at[0])
    groups = range(res_ref.shape[0] // GROUP)
    terms = chunk_ref.shape[1]
    blocks = []
    for g in groups:
        part = pl.ds(g * GROUP, GROUP)
        blocks.append(start(blocks_hbm.at[0, 0, part, pl.ds(1, terms)], chunk_ref.at[part], block_sem.at[g]))
    lists = start_lists(list_hbm, count_hbm, list_ref, count_ref, in_sem)
    listed = incoming_ref.shape[0]
    ext_ref[:listed] = incoming_ref[...]
    ext_ref[listed] = jnp.zeros_like(ext_ref[listed])
    cols.wait()
    for g, block in zip(groups, blocks):
        block.wait()
        for j in range(GROUP):
            i = g * GROUP + j
            named = [cols_ref[0, k + 1, 0, i] for k in range(terms)]
            picks = [jnp.where(col >= near, col - near, listed) for col in named]
            image = picked_product(chunk_ref, i, range(terms), picks, ext_ref)
            res_ref[i] = (half_row(low_ref, high_ref, i)[...] - image).astype(BF)
    wait_all(lists)
    wait_all(start_packing(res_ref, packed_ref, out_hbm, list_ref, count_ref, row_sem))


def own_residual_kernel(cols_hbm, blocks_hbm, rhs_hbm, own_hbm, upper_hbm, lower_hbm, incoming_ref, res_hbm, head_hbm, tail_hbm, cols_ref, ext_ref, chunk_ref, res_ref, in_sem, cols_sem, block_sem, out_sem):
    rows = res_ref.shape[0]
    cols = start(cols_hbm, cols_ref, cols_sem.at[0])
    pieces = start_near(own_hbm, upper_hbm, lower_hbm, ext_ref, in_sem)
    pieces.append(start(rhs_hbm.at[0, 0], res_ref, in_sem.at[3]))
    groups = range(rows // GROUP)
    blocks = start_blocks(blocks_hbm, 0, chunk_ref, block_sem, groups)
    ext_ref[rows + 2 * OVL :] = incoming_ref[...]
    cols.wait()
    wait_all(pieces)
    for g, block in zip(groups, blocks):
        block.wait()
        for j in range(GROUP):
            i = g * GROUP + j
            image = row_product(chunk_ref, i, cols_ref, i, ext_ref)
            res_ref[i] = (res_ref[i].astype(F32) - image).astype(BF)
    wait_all([
        start(res_ref.at[pl.ds(0, OVL)], head_hbm, out_sem.at[0]),
        start(res_ref.at[pl.ds(rows - OVL, OVL)], tail_hbm, out_sem.at[1]),
        start(res_ref, res_hbm.at[0, 0], out_sem.at[2]),
    ])


def second_kernel(list_hbm, count_hbm, from_prev_hbm, from_next_hbm, first_hbm, part_ref, returned_ref, second_hbm, list_ref, count_ref, edge_ref, field_ref, sum_ref, in_sem, edge_sem, out_sem):
    lists = start_lists(list_hbm, count_hbm, list_ref, count_ref, in_sem)
    edges = start_edges(from_prev_hbm, from_next_hbm, edge_ref, edge_sem)
    base = start(first_hbm.at[0, 0], field_ref, in_sem.at[2])
    add_returns(sum_ref, list_ref, count_ref, lists, edges, edge_ref, part_ref, returned_ref)
    base.wait()
    stores = []
    for g in range(field_ref.shape[0] // GROUP):
        part = pl.ds(g * GROUP, GROUP)
        field_ref[part] = (field_ref[part].astype(F32) + sum_ref[part]).astype(BF)
        stores.append(start(field_ref.at[part], second_hbm.at[0, 0, part], out_sem.at[g]))
    wait_all(stores)


def to_next(x):
    count = lax.axis_size("slab")
    return lax.ppermute(x, "slab", [(i, i + 1) for i in range(count - 1)])


def to_prev(x):
    count = lax.axis_size("slab")
    return lax.ppermute(x, "slab", [(i + 1, i) for i in range(count - 1)])


def route(buffer):
    return lax.all_to_all(buffer, "cross", split_axis=0, concat_axis=0, tiled=True)


def per_device(rhs, m_blocks, m_cols, j_blocks, j_cols, send_list, send_count):
    _, _, rows, block, vectors = rhs.shape
    peers, slots = send_list.shape[2:]
    listed = peers * slots
    extended_rows, terms = m_blocks.shape[2:4]
    near_rows = rows + 2 * OVL
    groups = rows // GROUP
    tile = block * vectors
    field_t = pltpu.HBM(rhs.shape, BF)
    packed_t = pltpu.HBM((peers, slots, block, vectors), BF)
    edge_t = pltpu.HBM((OVL, block, vectors), BF)
    listed_t = pltpu.HBM((listed, block, vectors), BF)

    m_cols = jnp.transpose(m_cols, (0, 3, 1, 2))
    j_cols = jnp.transpose(j_cols, (0, 3, 1, 2))
    send_list = jnp.transpose(send_list, (0, 1, 3, 2))

    def smem(x):
        return pltpu.SMEM(x.shape, jnp.int32)

    def tiles(count, dtype=BF):
        return pltpu.VMEM((count, block, vectors), dtype)

    def chunk(count):
        return pltpu.VMEM((count, terms, block, block), BF)

    lists = [smem(send_list), smem(send_count)]
    edges = pltpu.VMEM((2, OVL, block, vectors), BF)

    def call(kernel, name, out_shape, scratch, estimate, *operands, staged=()):
        placed = [pltpu.with_memory_space_constraint(x, pltpu.HBM) for x in operands]
        placed += [pltpu.with_memory_space_constraint(x, pltpu.VMEM) for x in staged]
        spec = lambda t: pl.BlockSpec(memory_space=t.memory_space)
        return pl.pallas_call(
            kernel,
            out_shape=out_shape,
            in_specs=[HBM] * len(operands) + [VMEM] * len(staged),
            out_specs=tuple(map(spec, out_shape)) if isinstance(out_shape, tuple) else spec(out_shape),
            scratch_shapes=scratch,
            compiler_params=params(),
            cost_estimate=estimate,
            name=name,
        )(*placed)

    packed, head, tail = call(
        pack_rhs_kernel,
        "pack_rhs",
        (packed_t, edge_t, edge_t),
        [*lists, tiles(listed), tiles(rows), DMA((3,)), DMA((2,)), DMA((peers,))],
        cost(0, 4 * rows * tile),
        send_list,
        send_count,
        rhs,
    )

    def extension(packed, head, tail):
        incoming = route(packed).reshape(listed, block, vectors)
        return to_next(tail), to_prev(head), incoming

    def precondition(field, upper, lower, incoming):
        near = call(
            stage_kernel,
            "stage_margin",
            tiles(near_rows),
            [DMA((3,))],
            cost(0, 4 * near_rows * tile),
            field,
            upper,
            lower,
        )
        groups = listed // GROUP
        cross = call(
            margin_kernel,
            "slot_partial",
            listed_t,
            [smem(m_cols), tiles(extended_rows), chunk(listed), tiles(listed), DMA((1,)), DMA((groups,)), DMA((groups,))],
            cost(2 * listed * terms * block * tile, 12 * extended_rows * tile),
            m_cols,
            m_blocks,
            staged=(near, incoming),
        )
        returned = route(cross.reshape(peers, slots, block, vectors)).reshape(listed, block, vectors)
        groups = near_rows // GROUP
        part, to_p, to_n = call(
            own_kernel,
            "own_partial",
            (tiles(rows), edge_t, edge_t),
            [smem(m_cols), tiles(extended_rows), chunk(near_rows), tiles(2 * OVL), DMA((3,)), DMA((1,)), DMA((groups,)), DMA((2,))],
            cost(2 * near_rows * terms * block * tile, 12 * extended_rows * tile),
            m_cols,
            m_blocks,
            field,
            upper,
            lower,
            staged=(incoming,),
        )
        from_next = to_prev(to_p)
        from_prev = to_next(to_n)
        return part, from_prev, from_next, returned

    upper, lower, incoming = extension(packed, head, tail)
    part, from_prev, from_next, returned = precondition(rhs, upper, lower, incoming)
    first, packed, head, tail = call(
        first_kernel,
        "assemble_first",
        (field_t, packed_t, edge_t, edge_t),
        [*lists, edges, tiles(listed), tiles(rows), tiles(rows, F32), DMA((2,)), DMA((2,)), DMA((3,)), DMA((peers,))],
        cost(0, 10 * rows * tile),
        send_list,
        send_count,
        from_prev,
        from_next,
        staged=(part, returned),
    )
    upper, lower, incoming = extension(packed, head, tail)
    low, high = call(
        near_residual_kernel,
        "near_residual",
        (tiles(rows // 2, F32), tiles(rows // 2, F32)),
        [smem(j_cols), tiles(near_rows + 1), chunk(rows), tiles(rows), DMA((4,)), DMA((1,)), DMA((groups,))],
        cost(2 * rows * terms * block * tile, 4 * (near_rows + terms * rows) * tile),
        j_cols,
        j_blocks,
        rhs,
        first,
        upper,
        lower,
    )
    packed = call(
        functools.partial(listed_residual_kernel, near_rows),
        "listed_residual",
        packed_t,
        [smem(j_cols), *lists, tiles(listed), tiles(listed + 1), pltpu.VMEM((rows, terms - 1, block, block), BF), tiles(rows), DMA((2,)), DMA((1,)), DMA((groups,)), DMA((peers,))],
        cost(2 * rows * terms * block * tile, 12 * extended_rows * tile),
        j_cols,
        send_list,
        send_count,
        j_blocks,
        staged=(low, high, incoming),
    )
    residual, head, tail = call(
        own_residual_kernel,
        "own_residual",
        (field_t, edge_t, edge_t),
        [smem(j_cols), tiles(extended_rows), chunk(rows), tiles(rows), DMA((4,)), DMA((1,)), DMA((groups,)), DMA((3,))],
        cost(2 * rows * terms * block * tile, 12 * extended_rows * tile),
        j_cols,
        j_blocks,
        rhs,
        first,
        upper,
        lower,
        staged=(incoming,),
    )
    upper, lower, incoming = extension(packed, head, tail)
    part, from_prev, from_next, returned = precondition(residual, upper, lower, incoming)
    return call(
        second_kernel,
        "assemble_second",
        field_t,
        [*lists, edges, tiles(rows), tiles(rows, F32), DMA((3,)), DMA((2,)), DMA((groups,))],
        cost(0, 10 * rows * tile),
        send_list,
        send_count,
        from_prev,
        from_next,
        first,
        staged=(part, returned),
    )


def solution(mesh):
    return jax.shard_map(
        per_device,
        mesh=mesh,
        in_specs=(
            P("slab", "cross", None, None, None),
            P("slab", "cross", None, None, None, None),
            P("slab", "cross", None, None),
            P("slab", "cross", None, None, None, None),
            P("slab", "cross", None, None),
            P("slab", "cross", None, None),
            P("slab", "cross", None),
        ),
        out_specs=P("slab", "cross", None, None, None),
        check_vma=False,
    )
```

time: 191 us -> 183 us (0.958)
  waiting for transfers between devices: 105 us -> 95.6 us
  starting transfers between devices: 49.5 us -> 47 us
  Pallas kernels: 35 us -> 37.4 us
  local copies, waits for them, and re-layouts: 0.04 us -> 1.97 us
    all_to_all x5, waiting for transfers between devices: 84.2 us -> 68 us  [route(): lax.all_to_all(buffer, 'cross', split_axis=0, concat_axis=0, tiled=True)]
    ppermute x5, waiting for transfers between devices: 15.1 us -> 18.5 us  [to_prev(): return lax.ppermute(x, 'slab', [(i + 1, i) for i in range(count - 1)])]
    ppermute x5, waiting for transfers between devices: 6.16 us -> 9.22 us  [to_next(): return lax.ppermute(x, 'slab', [(i, i + 1) for i in range(count - 1)])]
    all_to_all x5, starting transfers between devices: 27 us -> 24.4 us  [route(): lax.all_to_all(buffer, 'cross', split_axis=0, concat_axis=0, tiled=True)]
    pallas_call x8 -> x12, Pallas kernels: 35 us -> 37.4 us  [call(): pl.pallas_call(kernel, out_shape=out_shape, in_specs=[HBM] * len(operands...]
    unnamed x20, local copies, waits for them, and re-layouts: 0.04 us -> 1.97 us
  transfers between devices with their start and end apart: 15 -> 15, of which waited for: 13 -> 15; matrix products, arithmetic and copies ran while one was open for 0% -> 0% of each run, Pallas kernels for 5% -> 11%
where the time goes in v3:
time: 183 us; the launch traced here: 182 us
  waiting for transfers between devices  95.6 us (52%)
  starting transfers between devices  47 us (26%)
  Pallas kernels  37.4 us (20%)
  local copies, waits for them, and re-layouts  1.97 us (1%)
    all_to_all x5, waiting for transfers between devices, route(): lax.all_to_all(buffer, 'cross', split_axis=0, concat_axis=0, tiled=True)  68 us
    pallas_call x12, Pallas kernels, call(): pl.pallas_call(kernel, out_shape=out_shape, in_specs=[HBM] * len(operands...  37.4 us
    all_to_all x5, starting transfers between devices, route(): lax.all_to_all(buffer, 'cross', split_axis=0, concat_axis=0, tiled=True)  24.4 us
    ppermute x5, waiting for transfers between devices, to_prev(): return lax.ppermute(x, 'slab', [(i + 1, i) for i in range(count - 1)])  18.5 us
    ppermute x5, starting transfers between devices, to_next(): return lax.ppermute(x, 'slab', [(i, i + 1) for i in range(count - 1)])  16.1 us
    ppermute x5, waiting for transfers between devices, to_next(): return lax.ppermute(x, 'slab', [(i, i + 1) for i in range(count - 1)])  9.22 us
    ppermute x5, starting transfers between devices, to_prev(): return lax.ppermute(x, 'slab', [(i + 1, i) for i in range(count - 1)])  6.46 us
  transfers between devices with their start and end apart: 15, of which 15 were waited for; matrix products, arithmetic and copies ran while one was open for 0% of the time, Pallas kernels for 11%

profile of v3, /device:TPU:1, one launch (start us, length us, event | category | flops | bytes accessed | tf_op | source)
XLA Modules:
  0.0 182.3 jit_solution(17765789850732106237)
XLA Ops:
  0.0 2.5 %pack_rhs.1 = (bf16[16,2,128,128]{3,2,1,0:T(8,128)(2,1)}, bf16[4,128,128]{2,1,0:T(8,128)(2,1)}, bf16[4,128,128]{2,1,0:T(8,128)(2,1)}) custom-call(s32[1,1,2,16]{3,2,1,0:T(2,128)} %bitcast.24, s32[1,1,16]{2,1,0:T(1,128)} %count_hbm.7, bf16[1,1,32,128,128]{4,3,2,1,0:T(8,128)(2,1)} %rhs_hbm.5), custom_call_target="tpu_custom_call" | custom-call | bytes 2097152 | tf_op jit(solution)/shard_map/pack_rhs/pallas_call | solution.py:328
  2.5 10.0 %all-to-all-start = ((bf16[16,2,128,128]{3,2,1,0:T(8,128)(2,1)}), bf16[16,2,128,128]{3,2,1,0:T(8,128)(2,1)S(1)}, u32[]{:S(2)}, u32[]{:S(2)}) async-start(bf16[16,2,128,128]{3,2,1,0:T(8,128)(2,1)} %get-tuple-element.25), calls=%async_computation | async-start | bytes 2097152 | tf_op jit(solution)/shard_map/all_to_all | solution.py:292
  12.5 3.2 %collective-permute-start = (bf16[4,128,128]{2,1,0:T(8,128)(2,1)}, bf16[4,128,128]{2,1,0:T(8,128)(2,1)S(1)}, u32[]{:S(2)}, u32[]{:S(2)}) collective-permute-start(bf16[4,128,128]{2,1,0:T(8,128)(2,1)} %get-tuple-element.23), channel_id=1, source_target_pairs={{0,16},{16,32},{32,48},{48,64},{64,80},{80,96},{96,112},{112,128},... | collective-permute-start | bytes 393224 | tf_op jit(solution)/shard_map/ppermute | solution.py:283
  15.7 1.3 collective-permute-start.1
  17.0 1.8 %collective-permute-done.upper_hbm = bf16[4,128,128]{2,1,0:T(8,128)(2,1)S(1)} collective-permute-done((bf16[4,128,128]{2,1,0:T(8,128)(2,1)}, bf16[4,128,128]{2,1,0:T(8,128)(2,1)S(1)}, u32[]{:S(2)}, u32[]{:S(2)}) %collective-permute-start) | collective-permute-done | bytes 131104 | tf_op jit(solution)/shard_map/ppermute | solution.py:283
  18.9 3.7 %collective-permute-done.1.lower_hbm = bf16[4,128,128]{2,1,0:T(8,128)(2,1)S(1)} collective-permute-done((bf16[4,128,128]{2,1,0:T(8,128)(2,1)}, bf16[4,128,128]{2,1,0:T(8,128)(2,1)S(1)}, u32[]{:S(2)}, u32[]{:S(2)}) %collective-permute-start.1) | collective-permute-done | bytes 131104 | tf_op jit(solution)/shard_map/ppermute | solution.py:288
  22.6 0.0 copy-done.1
  22.6 0.6 copy-done.3
  23.2 1.3 stage_margin.2.near_ref
  24.5 15.9 %all-to-all-done = bf16[16,2,128,128]{3,2,1,0:T(8,128)(2,1)S(1)} async-done(((bf16[16,2,128,128]{3,2,1,0:T(8,128)(2,1)}), bf16[16,2,128,128]{3,2,1,0:T(8,128)(2,1)S(1)}, u32[]{:S(2)}, u32[]{:S(2)}) %all-to-all-start) | async-done | bytes 1048608 | tf_op jit(solution)/shard_map/all_to_all | solution.py:292
  40.4 3.4 %slot_partial.2 = bf16[32,128,128]{2,1,0:T(8,128)(2,1)} custom-call(s32[1,3,1,72]{3,2,1,0:T(1,128)} %bitcast.20, bf16[1,1,72,3,128,128]{5,4,3,2,1,0:T(8,128)(2,1)} %blocks_hbm.13, bf16[40,128,128]{2,1,0:T(8,128)(2,1)S(1)} %stage_margin.2.near_ref, bf16[32,128,128]{2,1,0:T(8,128)(2,1)S(1)} %bitcast.14), custom_call_target="tpu_custom_call" | custom-call | flops 402653184 | bytes 14155776 | tf_op jit(solution)/shard_map/slot_partial/pallas_call | solution.py:328
  43.8 3.6 %all-to-all-start.1 = ((bf16[16,2,128,128]{3,2,1,0:T(8,128)(2,1)}), bf16[16,2,128,128]{3,2,1,0:T(8,128)(2,1)S(1)}, u32[]{:S(2)}, u32[]{:S(2)}) async-start(bf16[16,2,128,128]{3,2,1,0:T(8,128)(2,1)} %bitcast.19), calls=%async_computation.1 | async-start | bytes 2097152 | tf_op jit(solution)/shard_map/all_to_all | solution.py:292
  47.4 3.9 %own_partial.2 = (bf16[32,128,128]{2,1,0:T(8,128)(2,1)S(1)}, bf16[4,128,128]{2,1,0:T(8,128)(2,1)}, bf16[4,128,128]{2,1,0:T(8,128)(2,1)}) custom-call(s32[1,3,1,72]{3,2,1,0:T(1,128)} %bitcast.21, bf16[1,1,72,3,128,128]{5,4,3,2,1,0:T(8,128)(2,1)} %blocks_hbm.13, bf16[1,1,32,128,128]{4,3,2,1,0:T(8,128)(2,1)} %rhs_hbm.5, bf16[4,128,128]{2,1,0:T(8,128)(2,1)} %copy-done.1, ...), custom_call_target="tpu_custom_call" | custom-call | flops 503316480 | bytes 14155776 | tf_op jit(solution)/shard_map/own_partial/pallas_call | solution.py:328
  51.4 3.2 %collective-permute-start.2 = (bf16[4,128,128]{2,1,0:T(8,128)(2,1)}, bf16[4,128,128]{2,1,0:T(8,128)(2,1)S(1)}, u32[]{:S(2)}, u32[]{:S(2)}) collective-permute-start(bf16[4,128,128]{2,1,0:T(8,128)(2,1)} %get-tuple-element.26), channel_id=1, source_target_pairs={{0,16},{16,32},{32,48},{48,64},{64,80},{80,96},{96,112},{112,128},... | collective-permute-start | bytes 393224 | tf_op jit(solution)/shard_map/ppermute | solution.py:283
  54.6 1.3 collective-permute-start.3
  55.9 1.9 %collective-permute-done.2.from_prev_hbm = bf16[4,128,128]{2,1,0:T(8,128)(2,1)S(1)} collective-permute-done((bf16[4,128,128]{2,1,0:T(8,128)(2,1)}, bf16[4,128,128]{2,1,0:T(8,128)(2,1)S(1)}, u32[]{:S(2)}, u32[]{:S(2)}) %collective-permute-start.2) | collective-permute-done | bytes 131104 | tf_op jit(solution)/shard_map/ppermute | solution.py:283
  57.7 3.7 %collective-permute-done.3.from_next_hbm = bf16[4,128,128]{2,1,0:T(8,128)(2,1)S(1)} collective-permute-done((bf16[4,128,128]{2,1,0:T(8,128)(2,1)}, bf16[4,128,128]{2,1,0:T(8,128)(2,1)S(1)}, u32[]{:S(2)}, u32[]{:S(2)}) %collective-permute-start.3) | collective-permute-done | bytes 131104 | tf_op jit(solution)/shard_map/ppermute | solution.py:288
  61.4 13.9 %all-to-all-done.1 = bf16[16,2,128,128]{3,2,1,0:T(8,128)(2,1)S(1)} async-done(((bf16[16,2,128,128]{3,2,1,0:T(8,128)(2,1)}), bf16[16,2,128,128]{3,2,1,0:T(8,128)(2,1)S(1)}, u32[]{:S(2)}, u32[]{:S(2)}) %all-to-all-start.1) | async-done | bytes 1048608 | tf_op jit(solution)/shard_map/all_to_all | solution.py:292
  75.3 0.0 copy-done.6
  75.3 0.0 copy-done.7
  75.3 2.9 %assemble_first.1 = (bf16[1,1,32,128,128]{4,3,2,1,0:T(8,128)(2,1)}, bf16[16,2,128,128]{3,2,1,0:T(8,128)(2,1)}, bf16[4,128,128]{2,1,0:T(8,128)(2,1)}, bf16[4,128,128]{2,1,0:T(8,128)(2,1)}) custom-call(s32[1,1,2,16]{3,2,1,0:T(2,128)} %bitcast.25, s32[1,1,16]{2,1,0:T(1,128)} %count_hbm.7, bf16[4,128,128]{2,1,0:T(8,128)(2,1)} %copy-done.6, ...), custom_call_target="tpu_custom_call" | custom-call | bytes 5242880 | tf_op jit(solution)/shard_map/assemble_first/pallas_call | solution.py:328
  78.2 3.6 %all-to-all-start.2 = ((bf16[16,2,128,128]{3,2,1,0:T(8,128)(2,1)}), bf16[16,2,128,128]{3,2,1,0:T(8,128)(2,1)S(1)}, u32[]{:S(2)}, u32[]{:S(2)}) async-start(bf16[16,2,128,128]{3,2,1,0:T(8,128)(2,1)} %get-tuple-element.32), calls=%async_computation.2 | async-start | bytes 2097152 | tf_op jit(solution)/shard_map/all_to_all | solution.py:292
  81.8 3.2 %collective-permute-start.4 = (bf16[4,128,128]{2,1,0:T(8,128)(2,1)}, bf16[4,128,128]{2,1,0:T(8,128)(2,1)S(1)}, u32[]{:S(2)}, u32[]{:S(2)}) collective-permute-start(bf16[4,128,128]{2,1,0:T(8,128)(2,1)} %get-tuple-element.30), channel_id=1, source_target_pairs={{0,16},{16,32},{32,48},{48,64},{64,80},{80,96},{96,112},{112,128},... | collective-permute-start | bytes 393224 | tf_op jit(solution)/shard_map/ppermute | solution.py:283
  85.0 1.3 collective-permute-start.5
  86.3 1.9 %collective-permute-done.4.upper_hbm = bf16[4,128,128]{2,1,0:T(8,128)(2,1)S(1)} collective-permute-done((bf16[4,128,128]{2,1,0:T(8,128)(2,1)}, bf16[4,128,128]{2,1,0:T(8,128)(2,1)S(1)}, u32[]{:S(2)}, u32[]{:S(2)}) %collective-permute-start.4) | collective-permute-done | bytes 131104 | tf_op jit(solution)/shard_map/ppermute | solution.py:283
  88.2 3.7 %collective-permute-done.5.lower_hbm = bf16[4,128,128]{2,1,0:T(8,128)(2,1)S(1)} collective-permute-done((bf16[4,128,128]{2,1,0:T(8,128)(2,1)}, bf16[4,128,128]{2,1,0:T(8,128)(2,1)S(1)}, u32[]{:S(2)}, u32[]{:S(2)}) %collective-permute-start.5) | collective-permute-done | bytes 131104 | tf_op jit(solution)/shard_map/ppermute | solution.py:288
  91.9 0.6 copy-done.5
  92.5 3.9 %near_residual.1 = (f32[16,128,128]{2,1,0:T(8,128)S(1)}, f32[16,128,128]{2,1,0:T(8,128)S(1)}) custom-call(s32[1,3,1,32]{3,2,1,0:T(1,128)} %bitcast.28, bf16[1,1,32,3,128,128]{5,4,3,2,1,0:T(8,128)(2,1)} %blocks_hbm.11, bf16[1,1,32,128,128]{4,3,2,1,0:T(8,128)(2,1)} %rhs_hbm.5, bf16[1,1,32,128,128]{4,3,2,1,0:T(8,128)(2,1)} %get-tuple-element.29.own_hbm.first_hbm, ...), custom_call_target="tpu_custom_call" | custom-call | flops 402653184 | bytes 8912896 | tf_op jit(solution)/shard_map/near_residual/pallas_call | solution.py:328
  96.4 13.3 %all-to-all-done.2 = bf16[16,2,128,128]{3,2,1,0:T(8,128)(2,1)S(1)} async-done(((bf16[16,2,128,128]{3,2,1,0:T(8,128)(2,1)}), bf16[16,2,128,128]{3,2,1,0:T(8,128)(2,1)S(1)}, u32[]{:S(2)}, u32[]{:S(2)}) %all-to-all-start.2) | async-done | bytes 1048608 | tf_op jit(solution)/shard_map/all_to_all | solution.py:292
  109.7 3.5 %listed_residual.1 = bf16[16,2,128,128]{3,2,1,0:T(8,128)(2,1)} custom-call(s32[1,3,1,32]{3,2,1,0:T(1,128)} %bitcast.29, s32[1,1,2,16]{3,2,1,0:T(2,128)} %bitcast.26, s32[1,1,16]{2,1,0:T(1,128)} %count_hbm.7, bf16[1,1,32,3,128,128]{5,4,3,2,1,0:T(8,128)(2,1)} %blocks_hbm.11, f32[16,128,128]{2,1,0:T(8,128)S(1)} %get-tuple-element.36.low_ref, ...), custom_call_target="tpu_custom_call" | custom-call | flops 402653184 | bytes 14155776 | tf_op jit(solution)/shard_map/listed_residual/pallas_call | solution.py:328
  113.2 3.6 %all-to-all-start.3 = ((bf16[16,2,128,128]{3,2,1,0:T(8,128)(2,1)}), bf16[16,2,128,128]{3,2,1,0:T(8,128)(2,1)S(1)}, u32[]{:S(2)}, u32[]{:S(2)}) async-start(bf16[16,2,128,128]{3,2,1,0:T(8,128)(2,1)} %listed_residual.1), calls=%async_computation.3 | async-start | bytes 2097152 | tf_op jit(solution)/shard_map/all_to_all | solution.py:292
  116.8 5.0 %own_residual.1 = (bf16[1,1,32,128,128]{4,3,2,1,0:T(8,128)(2,1)}, bf16[4,128,128]{2,1,0:T(8,128)(2,1)}, bf16[4,128,128]{2,1,0:T(8,128)(2,1)}) custom-call(s32[1,3,1,32]{3,2,1,0:T(1,128)} %bitcast.30, bf16[1,1,32,3,128,128]{5,4,3,2,1,0:T(8,128)(2,1)} %blocks_hbm.11, bf16[1,1,32,128,128]{4,3,2,1,0:T(8,128)(2,1)} %rhs_hbm.5, ...), custom_call_target="tpu_custom_call" | custom-call | flops 402653184 | bytes 14155776 | tf_op jit(solution)/shard_map/own_residual/pallas_call | solution.py:328
  121.7 3.2 %collective-permute-start.6 = (bf16[4,128,128]{2,1,0:T(8,128)(2,1)}, bf16[4,128,128]{2,1,0:T(8,128)(2,1)S(1)}, u32[]{:S(2)}, u32[]{:S(2)}) collective-permute-start(bf16[4,128,128]{2,1,0:T(8,128)(2,1)} %get-tuple-element.34), channel_id=1, source_target_pairs={{0,16},{16,32},{32,48},{48,64},{64,80},{80,96},{96,112},{112,128},... | collective-permute-start | bytes 393224 | tf_op jit(solution)/shard_map/ppermute | solution.py:283
  125.0 1.3 collective-permute-start.7
  126.3 1.8 %collective-permute-done.6.upper_hbm = bf16[4,128,128]{2,1,0:T(8,128)(2,1)S(1)} collective-permute-done((bf16[4,128,128]{2,1,0:T(8,128)(2,1)}, bf16[4,128,128]{2,1,0:T(8,128)(2,1)S(1)}, u32[]{:S(2)}, u32[]{:S(2)}) %collective-permute-start.6) | collective-permute-done | bytes 131104 | tf_op jit(solution)/shard_map/ppermute | solution.py:283
  128.1 3.7 %collective-permute-done.7.lower_hbm = bf16[4,128,128]{2,1,0:T(8,128)(2,1)S(1)} collective-permute-done((bf16[4,128,128]{2,1,0:T(8,128)(2,1)}, bf16[4,128,128]{2,1,0:T(8,128)(2,1)S(1)}, u32[]{:S(2)}, u32[]{:S(2)}) %collective-permute-start.7) | collective-permute-done | bytes 131104 | tf_op jit(solution)/shard_map/ppermute | solution.py:288
  131.8 0.6 copy-done.2
  132.4 1.3 stage_margin.3.near_ref
  133.7 10.9 %all-to-all-done.3 = bf16[16,2,128,128]{3,2,1,0:T(8,128)(2,1)S(1)} async-done(((bf16[16,2,128,128]{3,2,1,0:T(8,128)(2,1)}), bf16[16,2,128,128]{3,2,1,0:T(8,128)(2,1)S(1)}, u32[]{:S(2)}, u32[]{:S(2)}) %all-to-all-start.3) | async-done | bytes 1048608 | tf_op jit(solution)/shard_map/all_to_all | solution.py:292
  144.7 3.4 %slot_partial.3 = bf16[32,128,128]{2,1,0:T(8,128)(2,1)} custom-call(s32[1,3,1,72]{3,2,1,0:T(1,128)} %bitcast.22, bf16[1,1,72,3,128,128]{5,4,3,2,1,0:T(8,128)(2,1)} %blocks_hbm.13, bf16[40,128,128]{2,1,0:T(8,128)(2,1)S(1)} %stage_margin.3.near_ref, bf16[32,128,128]{2,1,0:T(8,128)(2,1)S(1)} %bitcast.10), custom_call_target="tpu_custom_call" | custom-call | flops 402653184 | bytes 14155776 | tf_op jit(solution)/shard_map/slot_partial/pallas_call | solution.py:328
  148.1 3.7 %all-to-all-start.4 = ((bf16[16,2,128,128]{3,2,1,0:T(8,128)(2,1)}), bf16[16,2,128,128]{3,2,1,0:T(8,128)(2,1)S(1)}, u32[]{:S(2)}, u32[]{:S(2)}) async-start(bf16[16,2,128,128]{3,2,1,0:T(8,128)(2,1)} %bitcast.18), calls=%async_computation.4 | async-start | bytes 2097152 | tf_op jit(solution)/shard_map/all_to_all | solution.py:292
  151.8 3.9 %own_partial.3 = (bf16[32,128,128]{2,1,0:T(8,128)(2,1)S(1)}, bf16[4,128,128]{2,1,0:T(8,128)(2,1)}, bf16[4,128,128]{2,1,0:T(8,128)(2,1)}) custom-call(s32[1,3,1,72]{3,2,1,0:T(1,128)} %bitcast.23, bf16[1,1,72,3,128,128]{5,4,3,2,1,0:T(8,128)(2,1)} %blocks_hbm.13, bf16[1,1,32,128,128]{4,3,2,1,0:T(8,128)(2,1)} %get-tuple-element.33.own_hbm, ...), custom_call_target="tpu_custom_call" | custom-call | flops 503316480 | bytes 14155776 | tf_op jit(solution)/shard_map/own_partial/pallas_call | solution.py:328
  155.7 3.2 %collective-permute-start.8 = (bf16[4,128,128]{2,1,0:T(8,128)(2,1)}, bf16[4,128,128]{2,1,0:T(8,128)(2,1)S(1)}, u32[]{:S(2)}, u32[]{:S(2)}) collective-permute-start(bf16[4,128,128]{2,1,0:T(8,128)(2,1)} %get-tuple-element.38), channel_id=1, source_target_pairs={{0,16},{16,32},{32,48},{48,64},{64,80},{80,96},{96,112},{112,128},... | collective-permute-start | bytes 393224 | tf_op jit(solution)/shard_map/ppermute | solution.py:283
  159.0 1.3 collective-permute-start.9
  160.3 1.8 %collective-permute-done.8.from_prev_hbm = bf16[4,128,128]{2,1,0:T(8,128)(2,1)S(1)} collective-permute-done((bf16[4,128,128]{2,1,0:T(8,128)(2,1)}, bf16[4,128,128]{2,1,0:T(8,128)(2,1)S(1)}, u32[]{:S(2)}, u32[]{:S(2)}) %collective-permute-start.8) | collective-permute-done | bytes 131104 | tf_op jit(solution)/shard_map/ppermute | solution.py:283
  162.1 3.7 %collective-permute-done.9.from_next_hbm = bf16[4,128,128]{2,1,0:T(8,128)(2,1)S(1)} collective-permute-done((bf16[4,128,128]{2,1,0:T(8,128)(2,1)}, bf16[4,128,128]{2,1,0:T(8,128)(2,1)S(1)}, u32[]{:S(2)}, u32[]{:S(2)}) %collective-permute-start.9) | collective-permute-done | bytes 131104 | tf_op jit(solution)/shard_map/ppermute | solution.py:288
  165.8 13.9 %all-to-all-done.4 = bf16[16,2,128,128]{3,2,1,0:T(8,128)(2,1)S(1)} async-done(((bf16[16,2,128,128]{3,2,1,0:T(8,128)(2,1)}), bf16[16,2,128,128]{3,2,1,0:T(8,128)(2,1)S(1)}, u32[]{:S(2)}, u32[]{:S(2)}) %all-to-all-start.4) | async-done | bytes 1048608 | tf_op jit(solution)/shard_map/all_to_all | solution.py:292
  179.7 2.5 %assemble_second.1 = bf16[1,1,32,128,128]{4,3,2,1,0:T(8,128)(2,1)} custom-call(s32[1,1,2,16]{3,2,1,0:T(2,128)} %bitcast.27, s32[1,1,16]{2,1,0:T(1,128)} %count_hbm.7, bf16[4,128,128]{2,1,0:T(8,128)(2,1)} %copy-done.8, bf16[4,128,128]{2,1,0:T(8,128)(2,1)} %copy-done.9, bf16[1,1,32,128,128]{4,3,2,1,0:T(8,128)(2,1)} %get-tuple-element.29.own_hbm.first_hbm, ...), custom_call_target="tpu_custom_call" | custom-call | bytes 5242880 | tf_op jit(solution)/shard_map/assemble_second/pallas_call | solution.py:328
  (14 shorter events, 0.0 us)
Async XLA Ops:
  2.5 37.9 %all-to-all-start = ((bf16[16,2,128,128]{3,2,1,0:T(8,128)(2,1)}), bf16[16,2,128,128]{3,2,1,0:T(8,128)(2,1)S(1)}, u32[]{:S(2)}, u32[]{:S(2)}) async-start(bf16[16,2,128,128]{3,2,1,0:T(8,128)(2,1)} %get-tuple-element.25), calls=%async_computation | async-start | bytes 2097152 | tf_op jit(solution)/shard_map/all_to_all | solution.py:292
  12.5 6.4 %collective-permute-start = (bf16[4,128,128]{2,1,0:T(8,128)(2,1)}, bf16[4,128,128]{2,1,0:T(8,128)(2,1)S(1)}, u32[]{:S(2)}, u32[]{:S(2)}) collective-permute-start(bf16[4,128,128]{2,1,0:T(8,128)(2,1)} %get-tuple-element.23), channel_id=1, source_target_pairs={{0,16},{16,32},{32,48},{48,64},{64,80},{80,96},{96,112},{112,128},... | collective-permute-start | bytes 393224 | tf_op jit(solution)/shard_map/ppermute | solution.py:283
  15.7 6.8 %collective-permute-start.1 = (bf16[4,128,128]{2,1,0:T(8,128)(2,1)}, bf16[4,128,128]{2,1,0:T(8,128)(2,1)S(1)}, u32[]{:S(2)}, u32[]{:S(2)}) collective-permute-start(bf16[4,128,128]{2,1,0:T(8,128)(2,1)} %get-tuple-element.24), channel_id=1, source_target_pairs={{16,0},{32,16},{48,32},{64,48},{80,64},{96,80},{112,96},{128,112},... | collective-permute-start | bytes 393224 | tf_op jit(solution)/shard_map/ppermute | solution.py:288
  18.9 3.7 %copy-start.1 = (bf16[4,128,128]{2,1,0:T(8,128)(2,1)}, bf16[4,128,128]{2,1,0:T(8,128)(2,1)S(1)}, u32[]{:S(2)}) copy-start(bf16[4,128,128]{2,1,0:T(8,128)(2,1)S(1)} %collective-permute-done.upper_hbm) | copy-start | bytes 393220
  22.6 0.6 copy-start.3
  43.8 31.5 %all-to-all-start.1 = ((bf16[16,2,128,128]{3,2,1,0:T(8,128)(2,1)}), bf16[16,2,128,128]{3,2,1,0:T(8,128)(2,1)S(1)}, u32[]{:S(2)}, u32[]{:S(2)}) async-start(bf16[16,2,128,128]{3,2,1,0:T(8,128)(2,1)} %bitcast.19), calls=%async_computation.1 | async-start | bytes 2097152 | tf_op jit(solution)/shard_map/all_to_all | solution.py:292
  51.4 6.4 %collective-permute-start.2 = (bf16[4,128,128]{2,1,0:T(8,128)(2,1)}, bf16[4,128,128]{2,1,0:T(8,128)(2,1)S(1)}, u32[]{:S(2)}, u32[]{:S(2)}) collective-permute-start(bf16[4,128,128]{2,1,0:T(8,128)(2,1)} %get-tuple-element.26), channel_id=1, source_target_pairs={{0,16},{16,32},{32,48},{48,64},{64,80},{80,96},{96,112},{112,128},... | collective-permute-start | bytes 393224 | tf_op jit(solution)/shard_map/ppermute | solution.py:283
  54.6 6.9 %collective-permute-start.3 = (bf16[4,128,128]{2,1,0:T(8,128)(2,1)}, bf16[4,128,128]{2,1,0:T(8,128)(2,1)S(1)}, u32[]{:S(2)}, u32[]{:S(2)}) collective-permute-start(bf16[4,128,128]{2,1,0:T(8,128)(2,1)} %get-tuple-element.27), channel_id=1, source_target_pairs={{16,0},{32,16},{48,32},{64,48},{80,64},{96,80},{112,96},{128,112},... | collective-permute-start | bytes 393224 | tf_op jit(solution)/shard_map/ppermute | solution.py:288
  57.7 17.6 %copy-start.6 = (bf16[4,128,128]{2,1,0:T(8,128)(2,1)}, bf16[4,128,128]{2,1,0:T(8,128)(2,1)S(1)}, u32[]{:S(2)}) copy-start(bf16[4,128,128]{2,1,0:T(8,128)(2,1)S(1)} %collective-permute-done.2.from_prev_hbm) | copy-start | bytes 393220
  61.4 13.9 %copy-start.7 = (bf16[4,128,128]{2,1,0:T(8,128)(2,1)}, bf16[4,128,128]{2,1,0:T(8,128)(2,1)S(1)}, u32[]{:S(2)}) copy-start(bf16[4,128,128]{2,1,0:T(8,128)(2,1)S(1)} %collective-permute-done.3.from_next_hbm) | copy-start | bytes 393220
  78.2 31.5 %all-to-all-start.2 = ((bf16[16,2,128,128]{3,2,1,0:T(8,128)(2,1)}), bf16[16,2,128,128]{3,2,1,0:T(8,128)(2,1)S(1)}, u32[]{:S(2)}, u32[]{:S(2)}) async-start(bf16[16,2,128,128]{3,2,1,0:T(8,128)(2,1)} %get-tuple-element.32), calls=%async_computation.2 | async-start | bytes 2097152 | tf_op jit(solution)/shard_map/all_to_all | solution.py:292
  81.8 6.4 %collective-permute-start.4 = (bf16[4,128,128]{2,1,0:T(8,128)(2,1)}, bf16[4,128,128]{2,1,0:T(8,128)(2,1)S(1)}, u32[]{:S(2)}, u32[]{:S(2)}) collective-permute-start(bf16[4,128,128]{2,1,0:T(8,128)(2,1)} %get-tuple-element.30), channel_id=1, source_target_pairs={{0,16},{16,32},{32,48},{48,64},{64,80},{80,96},{96,112},{112,128},... | collective-permute-start | bytes 393224 | tf_op jit(solution)/shard_map/ppermute | solution.py:283
  85.0 6.8 %collective-permute-start.5 = (bf16[4,128,128]{2,1,0:T(8,128)(2,1)}, bf16[4,128,128]{2,1,0:T(8,128)(2,1)S(1)}, u32[]{:S(2)}, u32[]{:S(2)}) collective-permute-start(bf16[4,128,128]{2,1,0:T(8,128)(2,1)} %get-tuple-element.31), channel_id=1, source_target_pairs={{16,0},{32,16},{48,32},{64,48},{80,64},{96,80},{112,96},{128,112},... | collective-permute-start | bytes 393224 | tf_op jit(solution)/shard_map/ppermute | solution.py:288
  88.2 3.7 %copy-start.4 = (bf16[4,128,128]{2,1,0:T(8,128)(2,1)}, bf16[4,128,128]{2,1,0:T(8,128)(2,1)S(1)}, u32[]{:S(2)}) copy-start(bf16[4,128,128]{2,1,0:T(8,128)(2,1)S(1)} %collective-permute-done.4.upper_hbm) | copy-start | bytes 393220
  91.9 0.7 copy-start.5
  113.2 31.5 %all-to-all-start.3 = ((bf16[16,2,128,128]{3,2,1,0:T(8,128)(2,1)}), bf16[16,2,128,128]{3,2,1,0:T(8,128)(2,1)S(1)}, u32[]{:S(2)}, u32[]{:S(2)}) async-start(bf16[16,2,128,128]{3,2,1,0:T(8,128)(2,1)} %listed_residual.1), calls=%async_computation.3 | async-start | bytes 2097152 | tf_op jit(solution)/shard_map/all_to_all | solution.py:292
  121.7 6.4 %collective-permute-start.6 = (bf16[4,128,128]{2,1,0:T(8,128)(2,1)}, bf16[4,128,128]{2,1,0:T(8,128)(2,1)S(1)}, u32[]{:S(2)}, u32[]{:S(2)}) collective-permute-start(bf16[4,128,128]{2,1,0:T(8,128)(2,1)} %get-tuple-element.34), channel_id=1, source_target_pairs={{0,16},{16,32},{32,48},{48,64},{64,80},{80,96},{96,112},{112,128},... | collective-permute-start | bytes 393224 | tf_op jit(solution)/shard_map/ppermute | solution.py:283
  125.0 6.8 %collective-permute-start.7 = (bf16[4,128,128]{2,1,0:T(8,128)(2,1)}, bf16[4,128,128]{2,1,0:T(8,128)(2,1)S(1)}, u32[]{:S(2)}, u32[]{:S(2)}) collective-permute-start(bf16[4,128,128]{2,1,0:T(8,128)(2,1)} %get-tuple-element.35), channel_id=1, source_target_pairs={{16,0},{32,16},{48,32},{64,48},{80,64},{96,80},{112,96},{128,112},... | collective-permute-start | bytes 393224 | tf_op jit(solution)/shard_map/ppermute | solution.py:288
  128.1 3.7 %copy-start = (bf16[4,128,128]{2,1,0:T(8,128)(2,1)}, bf16[4,128,128]{2,1,0:T(8,128)(2,1)S(1)}, u32[]{:S(2)}) copy-start(bf16[4,128,128]{2,1,0:T(8,128)(2,1)S(1)} %collective-permute-done.6.upper_hbm) | copy-start | bytes 393220
  131.8 0.7 copy-start.2
  148.1 31.7 %all-to-all-start.4 = ((bf16[16,2,128,128]{3,2,1,0:T(8,128)(2,1)}), bf16[16,2,128,128]{3,2,1,0:T(8,128)(2,1)S(1)}, u32[]{:S(2)}, u32[]{:S(2)}) async-start(bf16[16,2,128,128]{3,2,1,0:T(8,128)(2,1)} %bitcast.18), calls=%async_computation.4 | async-start | bytes 2097152 | tf_op jit(solution)/shard_map/all_to_all | solution.py:292
  155.7 6.4 %collective-permute-start.8 = (bf16[4,128,128]{2,1,0:T(8,128)(2,1)}, bf16[4,128,128]{2,1,0:T(8,128)(2,1)S(1)}, u32[]{:S(2)}, u32[]{:S(2)}) collective-permute-start(bf16[4,128,128]{2,1,0:T(8,128)(2,1)} %get-tuple-element.38), channel_id=1, source_target_pairs={{0,16},{16,32},{32,48},{48,64},{64,80},{80,96},{96,112},{112,128},... | collective-permute-start | bytes 393224 | tf_op jit(solution)/shard_map/ppermute | solution.py:283
  159.0 6.8 %collective-permute-start.9 = (bf16[4,128,128]{2,1,0:T(8,128)(2,1)}, bf16[4,128,128]{2,1,0:T(8,128)(2,1)S(1)}, u32[]{:S(2)}, u32[]{:S(2)}) collective-permute-start(bf16[4,128,128]{2,1,0:T(8,128)(2,1)} %get-tuple-element.39), channel_id=1, source_target_pairs={{16,0},{32,16},{48,32},{64,48},{80,64},{96,80},{112,96},{128,112},... | collective-permute-start | bytes 393224 | tf_op jit(solution)/shard_map/ppermute | solution.py:288
  162.1 17.6 %copy-start.8 = (bf16[4,128,128]{2,1,0:T(8,128)(2,1)}, bf16[4,128,128]{2,1,0:T(8,128)(2,1)S(1)}, u32[]{:S(2)}) copy-start(bf16[4,128,128]{2,1,0:T(8,128)(2,1)S(1)} %collective-permute-done.8.from_prev_hbm) | copy-start | bytes 393220
  165.8 13.9 %copy-start.9 = (bf16[4,128,128]{2,1,0:T(8,128)(2,1)}, bf16[4,128,128]{2,1,0:T(8,128)(2,1)S(1)}, u32[]{:S(2)}) copy-start(bf16[4,128,128]{2,1,0:T(8,128)(2,1)S(1)} %collective-permute-done.9.from_next_hbm) | copy-start | bytes 393220

commit v4 on v3

--- a/solution.py
+++ b/solution.py
@@ -48,7 +48,7 @@
     for g in range(packed_ref.shape[0] // GROUP):
         for slot in range(g * GROUP, (g + 1) * GROUP):
             row, used = slot_target(list_ref, count_ref, slot)
-            packed_ref[slot] = jnp.where(used, field_ref[row], jnp.zeros((), BF))
+            packed_ref[slot] = jnp.where(used, field_ref[row], jnp.zeros((), field_ref.dtype)).astype(BF)
         for peer in range(g * peers, (g + 1) * peers):
             copies.append(start(packed_ref.at[pl.ds(peer * slots, slots)], out_hbm.at[peer], sems.at[peer]))
     return copies
@@ -89,13 +89,13 @@
     return picked_product(chunk_ref, index, terms, [cols_ref[0, k, 0, row] for k in terms], ext_ref)
 
 
-def stage_kernel(own_hbm, upper_hbm, lower_hbm, near_ref, sems):
-    rows = own_hbm.shape[2]
-    wait_all([
-        start(own_hbm.at[0, 0], near_ref.at[pl.ds(0, rows)], sems.at[0]),
-        start(upper_hbm, near_ref.at[pl.ds(rows, OVL)], sems.at[1]),
-        start(lower_hbm, near_ref.at[pl.ds(rows + OVL, OVL)], sems.at[2]),
-    ])
+def stage_kernel(own_hbm, upper_hbm, lower_hbm, blocks_hbm, near_ref, *refs):
+    *chunk_refs, sems, block_sem = refs
+    near = near_ref.shape[0]
+    copies = start_near(own_hbm, upper_hbm, lower_hbm, near_ref, sems)
+    for g, chunk_ref in enumerate(chunk_refs):
+        copies.append(start(blocks_hbm.at[0, 0, pl.ds(near + g * GROUP, GROUP)], chunk_ref, block_sem.at[g]))
+    wait_all(copies)
 
 
 def half_row(low_ref, high_ref, row):
@@ -129,19 +129,23 @@
     ext_ref[near:] = incoming_ref[...]
 
 
-def margin_kernel(cols_hbm, blocks_hbm, near_ref, incoming_ref, cross_hbm, cols_ref, ext_ref, chunk_ref, part_ref, in_sem, block_sem, out_sem):
+def margin_kernel(cols_hbm, blocks_hbm, near_ref, incoming_ref, *refs):
+    *staged, cross_hbm, cols_ref, ext_ref, chunk_ref, part_ref, in_sem, block_sem, out_sem = refs
     cols = start(cols_hbm, cols_ref, in_sem.at[0])
     near = near_ref.shape[0]
-    groups = range(chunk_ref.shape[0] // GROUP)
-    blocks = start_blocks(blocks_hbm, near, chunk_ref, block_sem, groups)
+    ready = len(staged)
+    later = range(chunk_ref.shape[0] // GROUP)
+    blocks = start_blocks(blocks_hbm, near + ready * GROUP, chunk_ref, block_sem, later)
     fill_extended(near_ref, incoming_ref, ext_ref)
     cols.wait()
     copies = []
-    for g, block in zip(groups, blocks):
-        block.wait()
+    for g in range(ready + len(later)):
+        if g >= ready:
+            blocks[g - ready].wait()
         for j in range(GROUP):
             i = g * GROUP + j
-            part_ref[i] = row_product(chunk_ref, i, cols_ref, near + i, ext_ref).astype(BF)
+            source, index = (staged[g], j) if g < ready else (chunk_ref, i - ready * GROUP)
+            part_ref[i] = row_product(source, index, cols_ref, near + i, ext_ref).astype(BF)
         part = pl.ds(g * GROUP, GROUP)
         copies.append(start(part_ref.at[part], cross_hbm.at[part], out_sem.at[g]))
     wait_all(copies)
@@ -203,14 +207,10 @@
     lists = start_lists(list_hbm, count_hbm, list_ref, count_ref, in_sem)
     edges = start_edges(from_prev_hbm, from_next_hbm, edge_ref, edge_sem)
     add_returns(sum_ref, list_ref, count_ref, lists, edges, edge_ref, part_ref, returned_ref)
+    rows = field_ref.shape[0]
+    copies = start_packing(sum_ref, packed_ref, out_hbm, list_ref, count_ref, row_sem)
     field_ref[...] = sum_ref[...].astype(BF)
-    finish_field(field_ref, packed_ref, first_hbm, out_hbm, head_hbm, tail_hbm, list_ref, count_ref, out_sem, row_sem)
-
-
-def finish_field(field_ref, packed_ref, field_hbm, out_hbm, head_hbm, tail_hbm, list_ref, count_ref, out_sem, row_sem):
-    rows = field_ref.shape[0]
-    copies = [start(field_ref, field_hbm.at[0, 0], out_sem.at[2])]
-    copies += start_packing(field_ref, packed_ref, out_hbm, list_ref, count_ref, row_sem)
+    copies.append(start(field_ref, first_hbm.at[0, 0], out_sem.at[2]))
     copies.append(start(field_ref.at[pl.ds(0, OVL)], head_hbm, out_sem.at[0]))
     copies.append(start(field_ref.at[pl.ds(rows - OVL, OVL)], tail_hbm, out_sem.at[1]))
     wait_all(copies)
@@ -352,26 +352,28 @@
         return to_next(tail), to_prev(head), incoming
 
     def precondition(field, upper, lower, incoming):
-        near = call(
+        groups = listed // GROUP
+        ready = 1
+        near, *chunks = call(
             stage_kernel,
-            "stage_margin",
-            tiles(near_rows),
-            [DMA((3,))],
-            cost(0, 4 * near_rows * tile),
+            "stage_slots",
+            (tiles(near_rows), *[chunk(GROUP)] * ready),
+            [DMA((3,)), DMA((ready,))],
+            cost(0, 4 * (near_rows + terms * ready * GROUP) * tile),
             field,
             upper,
             lower,
+            m_blocks,
         )
-        groups = listed // GROUP
         cross = call(
             margin_kernel,
             "slot_partial",
             listed_t,
-            [smem(m_cols), tiles(extended_rows), chunk(listed), tiles(listed), DMA((1,)), DMA((groups,)), DMA((groups,))],
+            [smem(m_cols), tiles(extended_rows), chunk(listed - ready * GROUP), tiles(listed), DMA((1,)), DMA((groups - ready,)), DMA((groups,))],
             cost(2 * listed * terms * block * tile, 12 * extended_rows * tile),
             m_cols,
             m_blocks,
-            staged=(near, incoming),
+            staged=(near, incoming, *chunks),
         )
         returned = route(cross.reshape(peers, slots, block, vectors)).reshape(listed, block, vectors)
         groups = near_rows // GROUP

time: 183 us -> 182 us (level)
  no operation moved by 1% of the time
where the time goes in v4:
time: 182 us; the launch traced here: 181 us
  waiting for transfers between devices  94.9 us (52%)
  starting transfers between devices  47 us (26%)
  Pallas kernels  37.2 us (20%)
  local copies, waits for them, and re-layouts  1.95 us (1%)
    all_to_all x5, waiting for transfers between devices, route(): lax.all_to_all(buffer, 'cross', split_axis=0, concat_axis=0, tiled=True)  67 us
    pallas_call x12, Pallas kernels, call(): pl.pallas_call(kernel, out_shape=out_shape, in_specs=[HBM] * len(operands...  37.2 us
    all_to_all x5, starting transfers between devices, route(): lax.all_to_all(buffer, 'cross', split_axis=0, concat_axis=0, tiled=True)  24.4 us
    ppermute x5, waiting for transfers between devices, to_prev(): return lax.ppermute(x, 'slab', [(i + 1, i) for i in range(count - 1)])  18.5 us
    ppermute x5, starting transfers between devices, to_next(): return lax.ppermute(x, 'slab', [(i, i + 1) for i in range(count - 1)])  16.1 us
    ppermute x5, waiting for transfers between devices, to_next(): return lax.ppermute(x, 'slab', [(i, i + 1) for i in range(count - 1)])  9.42 us
    ppermute x5, starting transfers between devices, to_prev(): return lax.ppermute(x, 'slab', [(i + 1, i) for i in range(count - 1)])  6.46 us
  transfers between devices with their start and end apart: 15, of which 15 were waited for; matrix products, arithmetic and copies ran while one was open for 0% of the time, Pallas kernels for 11%

profile of v4, /device:TPU:1, one launch (start us, length us, event | category | flops | bytes accessed | tf_op | source)
XLA Modules:
  0.0 181.4 jit_solution(8276022965993789119)
XLA Ops:
  0.0 2.5 %pack_rhs.1 = (bf16[16,2,128,128]{3,2,1,0:T(8,128)(2,1)}, bf16[4,128,128]{2,1,0:T(8,128)(2,1)}, bf16[4,128,128]{2,1,0:T(8,128)(2,1)}) custom-call(s32[1,1,2,16]{3,2,1,0:T(2,128)} %bitcast.24, s32[1,1,16]{2,1,0:T(1,128)} %count_hbm.7, bf16[1,1,32,128,128]{4,3,2,1,0:T(8,128)(2,1)} %rhs_hbm.5), custom_call_target="tpu_custom_call" | custom-call | bytes 2097152 | tf_op jit(solution)/shard_map/pack_rhs/pallas_call | solution.py:328
  2.5 10.0 %all-to-all-start = ((bf16[16,2,128,128]{3,2,1,0:T(8,128)(2,1)}), bf16[16,2,128,128]{3,2,1,0:T(8,128)(2,1)S(1)}, u32[]{:S(2)}, u32[]{:S(2)}) async-start(bf16[16,2,128,128]{3,2,1,0:T(8,128)(2,1)} %get-tuple-element.29), calls=%async_computation | async-start | bytes 2097152 | tf_op jit(solution)/shard_map/all_to_all | solution.py:292
  12.5 3.2 %collective-permute-start = (bf16[4,128,128]{2,1,0:T(8,128)(2,1)}, bf16[4,128,128]{2,1,0:T(8,128)(2,1)S(1)}, u32[]{:S(2)}, u32[]{:S(2)}) collective-permute-start(bf16[4,128,128]{2,1,0:T(8,128)(2,1)} %get-tuple-element.27), channel_id=1, source_target_pairs={{0,16},{16,32},{32,48},{48,64},{64,80},{80,96},{96,112},{112,128},... | collective-permute-start | bytes 393224 | tf_op jit(solution)/shard_map/ppermute | solution.py:283
  15.7 1.3 collective-permute-start.1
  17.0 1.8 %collective-permute-done.upper_hbm = bf16[4,128,128]{2,1,0:T(8,128)(2,1)S(1)} collective-permute-done((bf16[4,128,128]{2,1,0:T(8,128)(2,1)}, bf16[4,128,128]{2,1,0:T(8,128)(2,1)S(1)}, u32[]{:S(2)}, u32[]{:S(2)}) %collective-permute-start) | collective-permute-done | bytes 131104 | tf_op jit(solution)/shard_map/ppermute | solution.py:283
  18.9 3.7 %collective-permute-done.1.lower_hbm = bf16[4,128,128]{2,1,0:T(8,128)(2,1)S(1)} collective-permute-done((bf16[4,128,128]{2,1,0:T(8,128)(2,1)}, bf16[4,128,128]{2,1,0:T(8,128)(2,1)S(1)}, u32[]{:S(2)}, u32[]{:S(2)}) %collective-permute-start.1) | collective-permute-done | bytes 131104 | tf_op jit(solution)/shard_map/ppermute | solution.py:288
  22.6 0.0 copy-done.1
  22.6 0.7 copy-done.3
  23.2 1.6 stage_slots.2
  24.8 15.6 %all-to-all-done = bf16[16,2,128,128]{3,2,1,0:T(8,128)(2,1)S(1)} async-done(((bf16[16,2,128,128]{3,2,1,0:T(8,128)(2,1)}), bf16[16,2,128,128]{3,2,1,0:T(8,128)(2,1)S(1)}, u32[]{:S(2)}, u32[]{:S(2)}) %all-to-all-start) | async-done | bytes 1048608 | tf_op jit(solution)/shard_map/all_to_all | solution.py:292
  40.4 3.1 %slot_partial.2 = bf16[32,128,128]{2,1,0:T(8,128)(2,1)} custom-call(s32[1,3,1,72]{3,2,1,0:T(1,128)} %bitcast.20, bf16[1,1,72,3,128,128]{5,4,3,2,1,0:T(8,128)(2,1)} %blocks_hbm.17, bf16[40,128,128]{2,1,0:T(8,128)(2,1)S(1)} %get-tuple-element.33.near_ref, bf16[32,128,128]{2,1,0:T(8,128)(2,1)S(1)} %bitcast.12, ...), custom_call_target="tpu_custom_call" | custom-call | flops 402653184 | bytes 14155776 | tf_op jit(solution)/shard_map/slot_partial/pallas_call | solution.py:328
  43.5 3.6 %all-to-all-start.1 = ((bf16[16,2,128,128]{3,2,1,0:T(8,128)(2,1)}), bf16[16,2,128,128]{3,2,1,0:T(8,128)(2,1)S(1)}, u32[]{:S(2)}, u32[]{:S(2)}) async-start(bf16[16,2,128,128]{3,2,1,0:T(8,128)(2,1)} %bitcast.19), calls=%async_computation.1 | async-start | bytes 2097152 | tf_op jit(solution)/shard_map/all_to_all | solution.py:292
  47.1 3.9 %own_partial.2 = (bf16[32,128,128]{2,1,0:T(8,128)(2,1)S(1)}, bf16[4,128,128]{2,1,0:T(8,128)(2,1)}, bf16[4,128,128]{2,1,0:T(8,128)(2,1)}) custom-call(s32[1,3,1,72]{3,2,1,0:T(1,128)} %bitcast.21, bf16[1,1,72,3,128,128]{5,4,3,2,1,0:T(8,128)(2,1)} %blocks_hbm.17, bf16[1,1,32,128,128]{4,3,2,1,0:T(8,128)(2,1)} %rhs_hbm.5, bf16[4,128,128]{2,1,0:T(8,128)(2,1)} %copy-done.1, ...), custom_call_target="tpu_custom_call" | custom-call | flops 503316480 | bytes 14155776 | tf_op jit(solution)/shard_map/own_partial/pallas_call | solution.py:328
  51.0 3.2 %collective-permute-start.2 = (bf16[4,128,128]{2,1,0:T(8,128)(2,1)}, bf16[4,128,128]{2,1,0:T(8,128)(2,1)S(1)}, u32[]{:S(2)}, u32[]{:S(2)}) collective-permute-start(bf16[4,128,128]{2,1,0:T(8,128)(2,1)} %get-tuple-element.30), channel_id=1, source_target_pairs={{0,16},{16,32},{32,48},{48,64},{64,80},{80,96},{96,112},{112,128},... | collective-permute-start | bytes 393224 | tf_op jit(solution)/shard_map/ppermute | solution.py:283
  54.3 1.3 collective-permute-start.3
  55.6 1.9 %collective-permute-done.2.from_prev_hbm = bf16[4,128,128]{2,1,0:T(8,128)(2,1)S(1)} collective-permute-done((bf16[4,128,128]{2,1,0:T(8,128)(2,1)}, bf16[4,128,128]{2,1,0:T(8,128)(2,1)S(1)}, u32[]{:S(2)}, u32[]{:S(2)}) %collective-permute-start.2) | collective-permute-done | bytes 131104 | tf_op jit(solution)/shard_map/ppermute | solution.py:283
  57.4 3.7 %collective-permute-done.3.from_next_hbm = bf16[4,128,128]{2,1,0:T(8,128)(2,1)S(1)} collective-permute-done((bf16[4,128,128]{2,1,0:T(8,128)(2,1)}, bf16[4,128,128]{2,1,0:T(8,128)(2,1)S(1)}, u32[]{:S(2)}, u32[]{:S(2)}) %collective-permute-start.3) | collective-permute-done | bytes 131104 | tf_op jit(solution)/shard_map/ppermute | solution.py:288
  61.1 13.9 %all-to-all-done.1 = bf16[16,2,128,128]{3,2,1,0:T(8,128)(2,1)S(1)} async-done(((bf16[16,2,128,128]{3,2,1,0:T(8,128)(2,1)}), bf16[16,2,128,128]{3,2,1,0:T(8,128)(2,1)S(1)}, u32[]{:S(2)}, u32[]{:S(2)}) %all-to-all-start.1) | async-done | bytes 1048608 | tf_op jit(solution)/shard_map/all_to_all | solution.py:292
  75.0 0.0 copy-done.6
  75.0 2.8 %assemble_first.1 = (bf16[1,1,32,128,128]{4,3,2,1,0:T(8,128)(2,1)}, bf16[16,2,128,128]{3,2,1,0:T(8,128)(2,1)}, bf16[4,128,128]{2,1,0:T(8,128)(2,1)}, bf16[4,128,128]{2,1,0:T(8,128)(2,1)}) custom-call(s32[1,1,2,16]{3,2,1,0:T(2,128)} %bitcast.25, s32[1,1,16]{2,1,0:T(1,128)} %count_hbm.7, bf16[4,128,128]{2,1,0:T(8,128)(2,1)} %copy-done.6, ...), custom_call_target="tpu_custom_call" | custom-call | bytes 5242880 | tf_op jit(solution)/shard_map/assemble_first/pallas_call | solution.py:328
  77.8 3.6 %all-to-all-start.2 = ((bf16[16,2,128,128]{3,2,1,0:T(8,128)(2,1)}), bf16[16,2,128,128]{3,2,1,0:T(8,128)(2,1)S(1)}, u32[]{:S(2)}, u32[]{:S(2)}) async-start(bf16[16,2,128,128]{3,2,1,0:T(8,128)(2,1)} %get-tuple-element.38), calls=%async_computation.2 | async-start | bytes 2097152 | tf_op jit(solution)/shard_map/all_to_all | solution.py:292
  81.3 3.2 %collective-permute-start.4 = (bf16[4,128,128]{2,1,0:T(8,128)(2,1)}, bf16[4,128,128]{2,1,0:T(8,128)(2,1)S(1)}, u32[]{:S(2)}, u32[]{:S(2)}) collective-permute-start(bf16[4,128,128]{2,1,0:T(8,128)(2,1)} %get-tuple-element.36), channel_id=1, source_target_pairs={{0,16},{16,32},{32,48},{48,64},{64,80},{80,96},{96,112},{112,128},... | collective-permute-start | bytes 393224 | tf_op jit(solution)/shard_map/ppermute | solution.py:283
  84.6 1.3 collective-permute-start.5
  85.9 1.9 %collective-permute-done.4.upper_hbm = bf16[4,128,128]{2,1,0:T(8,128)(2,1)S(1)} collective-permute-done((bf16[4,128,128]{2,1,0:T(8,128)(2,1)}, bf16[4,128,128]{2,1,0:T(8,128)(2,1)S(1)}, u32[]{:S(2)}, u32[]{:S(2)}) %collective-permute-start.4) | collective-permute-done | bytes 131104 | tf_op jit(solution)/shard_map/ppermute | solution.py:283
  87.7 3.7 %collective-permute-done.5.lower_hbm = bf16[4,128,128]{2,1,0:T(8,128)(2,1)S(1)} collective-permute-done((bf16[4,128,128]{2,1,0:T(8,128)(2,1)}, bf16[4,128,128]{2,1,0:T(8,128)(2,1)S(1)}, u32[]{:S(2)}, u32[]{:S(2)}) %collective-permute-start.5) | collective-permute-done | bytes 131104 | tf_op jit(solution)/shard_map/ppermute | solution.py:288
  91.4 0.6 copy-done.5
  92.0 3.9 %near_residual.1 = (f32[16,128,128]{2,1,0:T(8,128)S(1)}, f32[16,128,128]{2,1,0:T(8,128)S(1)}) custom-call(s32[1,3,1,32]{3,2,1,0:T(1,128)} %bitcast.28, bf16[1,1,32,3,128,128]{5,4,3,2,1,0:T(8,128)(2,1)} %blocks_hbm.14, bf16[1,1,32,128,128]{4,3,2,1,0:T(8,128)(2,1)} %rhs_hbm.5, bf16[1,1,32,128,128]{4,3,2,1,0:T(8,128)(2,1)} %get-tuple-element.35.own_hbm.first_hbm, ...), custom_call_target="tpu_custom_call" | custom-call | flops 402653184 | bytes 8912896 | tf_op jit(solution)/shard_map/near_residual/pallas_call | solution.py:328
  95.9 13.3 %all-to-all-done.2 = bf16[16,2,128,128]{3,2,1,0:T(8,128)(2,1)S(1)} async-done(((bf16[16,2,128,128]{3,2,1,0:T(8,128)(2,1)}), bf16[16,2,128,128]{3,2,1,0:T(8,128)(2,1)S(1)}, u32[]{:S(2)}, u32[]{:S(2)}) %all-to-all-start.2) | async-done | bytes 1048608 | tf_op jit(solution)/shard_map/all_to_all | solution.py:292
  109.2 3.5 %listed_residual.1 = bf16[16,2,128,128]{3,2,1,0:T(8,128)(2,1)} custom-call(s32[1,3,1,32]{3,2,1,0:T(1,128)} %bitcast.29, s32[1,1,2,16]{3,2,1,0:T(2,128)} %bitcast.26, s32[1,1,16]{2,1,0:T(1,128)} %count_hbm.7, bf16[1,1,32,3,128,128]{5,4,3,2,1,0:T(8,128)(2,1)} %blocks_hbm.14, f32[16,128,128]{2,1,0:T(8,128)S(1)} %get-tuple-element.42.low_ref, ...), custom_call_target="tpu_custom_call" | custom-call | flops 402653184 | bytes 14155776 | tf_op jit(solution)/shard_map/listed_residual/pallas_call | solution.py:328
  112.7 3.6 %all-to-all-start.3 = ((bf16[16,2,128,128]{3,2,1,0:T(8,128)(2,1)}), bf16[16,2,128,128]{3,2,1,0:T(8,128)(2,1)S(1)}, u32[]{:S(2)}, u32[]{:S(2)}) async-start(bf16[16,2,128,128]{3,2,1,0:T(8,128)(2,1)} %listed_residual.1), calls=%async_computation.3 | async-start | bytes 2097152 | tf_op jit(solution)/shard_map/all_to_all | solution.py:292
  116.3 5.0 %own_residual.1 = (bf16[1,1,32,128,128]{4,3,2,1,0:T(8,128)(2,1)}, bf16[4,128,128]{2,1,0:T(8,128)(2,1)}, bf16[4,128,128]{2,1,0:T(8,128)(2,1)}) custom-call(s32[1,3,1,32]{3,2,1,0:T(1,128)} %bitcast.30, bf16[1,1,32,3,128,128]{5,4,3,2,1,0:T(8,128)(2,1)} %blocks_hbm.14, bf16[1,1,32,128,128]{4,3,2,1,0:T(8,128)(2,1)} %rhs_hbm.5, ...), custom_call_target="tpu_custom_call" | custom-call | flops 402653184 | bytes 14155776 | tf_op jit(solution)/shard_map/own_residual/pallas_call | solution.py:328
  121.3 3.2 %collective-permute-start.6 = (bf16[4,128,128]{2,1,0:T(8,128)(2,1)}, bf16[4,128,128]{2,1,0:T(8,128)(2,1)S(1)}, u32[]{:S(2)}, u32[]{:S(2)}) collective-permute-start(bf16[4,128,128]{2,1,0:T(8,128)(2,1)} %get-tuple-element.40), channel_id=1, source_target_pairs={{0,16},{16,32},{32,48},{48,64},{64,80},{80,96},{96,112},{112,128},... | collective-permute-start | bytes 393224 | tf_op jit(solution)/shard_map/ppermute | solution.py:283
  124.5 1.3 collective-permute-start.7
  125.8 1.8 %collective-permute-done.6.upper_hbm = bf16[4,128,128]{2,1,0:T(8,128)(2,1)S(1)} collective-permute-done((bf16[4,128,128]{2,1,0:T(8,128)(2,1)}, bf16[4,128,128]{2,1,0:T(8,128)(2,1)S(1)}, u32[]{:S(2)}, u32[]{:S(2)}) %collective-permute-start.6) | collective-permute-done | bytes 131104 | tf_op jit(solution)/shard_map/ppermute | solution.py:283
  127.6 3.7 %collective-permute-done.7.lower_hbm = bf16[4,128,128]{2,1,0:T(8,128)(2,1)S(1)} collective-permute-done((bf16[4,128,128]{2,1,0:T(8,128)(2,1)}, bf16[4,128,128]{2,1,0:T(8,128)(2,1)S(1)}, u32[]{:S(2)}, u32[]{:S(2)}) %collective-permute-start.7) | collective-permute-done | bytes 131104 | tf_op jit(solution)/shard_map/ppermute | solution.py:288
  131.3 0.6 copy-done.2
  132.0 1.6 stage_slots.3
  133.5 10.6 %all-to-all-done.3 = bf16[16,2,128,128]{3,2,1,0:T(8,128)(2,1)S(1)} async-done(((bf16[16,2,128,128]{3,2,1,0:T(8,128)(2,1)}), bf16[16,2,128,128]{3,2,1,0:T(8,128)(2,1)S(1)}, u32[]{:S(2)}, u32[]{:S(2)}) %all-to-all-start.3) | async-done | bytes 1048608 | tf_op jit(solution)/shard_map/all_to_all | solution.py:292
  144.2 3.1 %slot_partial.3 = bf16[32,128,128]{2,1,0:T(8,128)(2,1)} custom-call(s32[1,3,1,72]{3,2,1,0:T(1,128)} %bitcast.22, bf16[1,1,72,3,128,128]{5,4,3,2,1,0:T(8,128)(2,1)} %blocks_hbm.17, bf16[40,128,128]{2,1,0:T(8,128)(2,1)S(1)} %get-tuple-element.47.near_ref, bf16[32,128,128]{2,1,0:T(8,128)(2,1)S(1)} %bitcast.10, ...), custom_call_target="tpu_custom_call" | custom-call | flops 402653184 | bytes 14155776 | tf_op jit(solution)/shard_map/slot_partial/pallas_call | solution.py:328
  147.3 3.7 %all-to-all-start.4 = ((bf16[16,2,128,128]{3,2,1,0:T(8,128)(2,1)}), bf16[16,2,128,128]{3,2,1,0:T(8,128)(2,1)S(1)}, u32[]{:S(2)}, u32[]{:S(2)}) async-start(bf16[16,2,128,128]{3,2,1,0:T(8,128)(2,1)} %bitcast.18), calls=%async_computation.4 | async-start | bytes 2097152 | tf_op jit(solution)/shard_map/all_to_all | solution.py:292
  151.0 3.9 %own_partial.3 = (bf16[32,128,128]{2,1,0:T(8,128)(2,1)S(1)}, bf16[4,128,128]{2,1,0:T(8,128)(2,1)}, bf16[4,128,128]{2,1,0:T(8,128)(2,1)}) custom-call(s32[1,3,1,72]{3,2,1,0:T(1,128)} %bitcast.23, bf16[1,1,72,3,128,128]{5,4,3,2,1,0:T(8,128)(2,1)} %blocks_hbm.17, bf16[1,1,32,128,128]{4,3,2,1,0:T(8,128)(2,1)} %get-tuple-element.39.own_hbm, ...), custom_call_target="tpu_custom_call" | custom-call | flops 503316480 | bytes 14155776 | tf_op jit(solution)/shard_map/own_partial/pallas_call | solution.py:328
  155.0 3.2 %collective-permute-start.8 = (bf16[4,128,128]{2,1,0:T(8,128)(2,1)}, bf16[4,128,128]{2,1,0:T(8,128)(2,1)S(1)}, u32[]{:S(2)}, u32[]{:S(2)}) collective-permute-start(bf16[4,128,128]{2,1,0:T(8,128)(2,1)} %get-tuple-element.44), channel_id=1, source_target_pairs={{0,16},{16,32},{32,48},{48,64},{64,80},{80,96},{96,112},{112,128},... | collective-permute-start | bytes 393224 | tf_op jit(solution)/shard_map/ppermute | solution.py:283
  158.2 1.3 collective-permute-start.9
  159.5 2.0 %collective-permute-done.8.from_prev_hbm = bf16[4,128,128]{2,1,0:T(8,128)(2,1)S(1)} collective-permute-done((bf16[4,128,128]{2,1,0:T(8,128)(2,1)}, bf16[4,128,128]{2,1,0:T(8,128)(2,1)S(1)}, u32[]{:S(2)}, u32[]{:S(2)}) %collective-permute-start.8) | collective-permute-done | bytes 131104 | tf_op jit(solution)/shard_map/ppermute | solution.py:283
  161.5 3.7 %collective-permute-done.9.from_next_hbm = bf16[4,128,128]{2,1,0:T(8,128)(2,1)S(1)} collective-permute-done((bf16[4,128,128]{2,1,0:T(8,128)(2,1)}, bf16[4,128,128]{2,1,0:T(8,128)(2,1)S(1)}, u32[]{:S(2)}, u32[]{:S(2)}) %collective-permute-start.9) | collective-permute-done | bytes 131104 | tf_op jit(solution)/shard_map/ppermute | solution.py:288
  165.2 13.5 %all-to-all-done.4 = bf16[16,2,128,128]{3,2,1,0:T(8,128)(2,1)S(1)} async-done(((bf16[16,2,128,128]{3,2,1,0:T(8,128)(2,1)}), bf16[16,2,128,128]{3,2,1,0:T(8,128)(2,1)S(1)}, u32[]{:S(2)}, u32[]{:S(2)}) %all-to-all-start.4) | async-done | bytes 1048608 | tf_op jit(solution)/shard_map/all_to_all | solution.py:292
  178.8 0.0 copy-done.8
  178.8 2.5 %assemble_second.1 = bf16[1,1,32,128,128]{4,3,2,1,0:T(8,128)(2,1)} custom-call(s32[1,1,2,16]{3,2,1,0:T(2,128)} %bitcast.27, s32[1,1,16]{2,1,0:T(1,128)} %count_hbm.7, bf16[4,128,128]{2,1,0:T(8,128)(2,1)} %copy-done.8, bf16[4,128,128]{2,1,0:T(8,128)(2,1)} %copy-done.9, bf16[1,1,32,128,128]{4,3,2,1,0:T(8,128)(2,1)} %get-tuple-element.35.own_hbm.first_hbm, ...), custom_call_target="tpu_custom_call" | custom-call | bytes 5242880 | tf_op jit(solution)/shard_map/assemble_second/pallas_call | solution.py:328
  (14 shorter events, 0.0 us)
Async XLA Ops:
  2.5 37.9 %all-to-all-start = ((bf16[16,2,128,128]{3,2,1,0:T(8,128)(2,1)}), bf16[16,2,128,128]{3,2,1,0:T(8,128)(2,1)S(1)}, u32[]{:S(2)}, u32[]{:S(2)}) async-start(bf16[16,2,128,128]{3,2,1,0:T(8,128)(2,1)} %get-tuple-element.29), calls=%async_computation | async-start | bytes 2097152 | tf_op jit(solution)/shard_map/all_to_all | solution.py:292
  12.5 6.4 %collective-permute-start = (bf16[4,128,128]{2,1,0:T(8,128)(2,1)}, bf16[4,128,128]{2,1,0:T(8,128)(2,1)S(1)}, u32[]{:S(2)}, u32[]{:S(2)}) collective-permute-start(bf16[4,128,128]{2,1,0:T(8,128)(2,1)} %get-tuple-element.27), channel_id=1, source_target_pairs={{0,16},{16,32},{32,48},{48,64},{64,80},{80,96},{96,112},{112,128},... | collective-permute-start | bytes 393224 | tf_op jit(solution)/shard_map/ppermute | solution.py:283
  15.7 6.8 %collective-permute-start.1 = (bf16[4,128,128]{2,1,0:T(8,128)(2,1)}, bf16[4,128,128]{2,1,0:T(8,128)(2,1)S(1)}, u32[]{:S(2)}, u32[]{:S(2)}) collective-permute-start(bf16[4,128,128]{2,1,0:T(8,128)(2,1)} %get-tuple-element.28), channel_id=1, source_target_pairs={{16,0},{32,16},{48,32},{64,48},{80,64},{96,80},{112,96},{128,112},... | collective-permute-start | bytes 393224 | tf_op jit(solution)/shard_map/ppermute | solution.py:288
  18.9 3.7 %copy-start.1 = (bf16[4,128,128]{2,1,0:T(8,128)(2,1)}, bf16[4,128,128]{2,1,0:T(8,128)(2,1)S(1)}, u32[]{:S(2)}) copy-start(bf16[4,128,128]{2,1,0:T(8,128)(2,1)S(1)} %collective-permute-done.upper_hbm) | copy-start | bytes 393220
  22.6 0.7 copy-start.3
  43.5 31.5 %all-to-all-start.1 = ((bf16[16,2,128,128]{3,2,1,0:T(8,128)(2,1)}), bf16[16,2,128,128]{3,2,1,0:T(8,128)(2,1)S(1)}, u32[]{:S(2)}, u32[]{:S(2)}) async-start(bf16[16,2,128,128]{3,2,1,0:T(8,128)(2,1)} %bitcast.19), calls=%async_computation.1 | async-start | bytes 2097152 | tf_op jit(solution)/shard_map/all_to_all | solution.py:292
  51.0 6.4 %collective-permute-start.2 = (bf16[4,128,128]{2,1,0:T(8,128)(2,1)}, bf16[4,128,128]{2,1,0:T(8,128)(2,1)S(1)}, u32[]{:S(2)}, u32[]{:S(2)}) collective-permute-start(bf16[4,128,128]{2,1,0:T(8,128)(2,1)} %get-tuple-element.30), channel_id=1, source_target_pairs={{0,16},{16,32},{32,48},{48,64},{64,80},{80,96},{96,112},{112,128},... | collective-permute-start | bytes 393224 | tf_op jit(solution)/shard_map/ppermute | solution.py:283
  54.3 6.8 %collective-permute-start.3 = (bf16[4,128,128]{2,1,0:T(8,128)(2,1)}, bf16[4,128,128]{2,1,0:T(8,128)(2,1)S(1)}, u32[]{:S(2)}, u32[]{:S(2)}) collective-permute-start(bf16[4,128,128]{2,1,0:T(8,128)(2,1)} %get-tuple-element.31), channel_id=1, source_target_pairs={{16,0},{32,16},{48,32},{64,48},{80,64},{96,80},{112,96},{128,112},... | collective-permute-start | bytes 393224 | tf_op jit(solution)/shard_map/ppermute | solution.py:288
  57.4 17.6 %copy-start.6 = (bf16[4,128,128]{2,1,0:T(8,128)(2,1)}, bf16[4,128,128]{2,1,0:T(8,128)(2,1)S(1)}, u32[]{:S(2)}) copy-start(bf16[4,128,128]{2,1,0:T(8,128)(2,1)S(1)} %collective-permute-done.2.from_prev_hbm) | copy-start | bytes 393220
  61.1 13.9 %copy-start.7 = (bf16[4,128,128]{2,1,0:T(8,128)(2,1)}, bf16[4,128,128]{2,1,0:T(8,128)(2,1)S(1)}, u32[]{:S(2)}) copy-start(bf16[4,128,128]{2,1,0:T(8,128)(2,1)S(1)} %collective-permute-done.3.from_next_hbm) | copy-start | bytes 393220
  77.8 31.5 %all-to-all-start.2 = ((bf16[16,2,128,128]{3,2,1,0:T(8,128)(2,1)}), bf16[16,2,128,128]{3,2,1,0:T(8,128)(2,1)S(1)}, u32[]{:S(2)}, u32[]{:S(2)}) async-start(bf16[16,2,128,128]{3,2,1,0:T(8,128)(2,1)} %get-tuple-element.38), calls=%async_computation.2 | async-start | bytes 2097152 | tf_op jit(solution)/shard_map/all_to_all | solution.py:292
  81.3 6.4 %collective-permute-start.4 = (bf16[4,128,128]{2,1,0:T(8,128)(2,1)}, bf16[4,128,128]{2,1,0:T(8,128)(2,1)S(1)}, u32[]{:S(2)}, u32[]{:S(2)}) collective-permute-start(bf16[4,128,128]{2,1,0:T(8,128)(2,1)} %get-tuple-element.36), channel_id=1, source_target_pairs={{0,16},{16,32},{32,48},{48,64},{64,80},{80,96},{96,112},{112,128},... | collective-permute-start | bytes 393224 | tf_op jit(solution)/shard_map/ppermute | solution.py:283
  84.6 6.8 %collective-permute-start.5 = (bf16[4,128,128]{2,1,0:T(8,128)(2,1)}, bf16[4,128,128]{2,1,0:T(8,128)(2,1)S(1)}, u32[]{:S(2)}, u32[]{:S(2)}) collective-permute-start(bf16[4,128,128]{2,1,0:T(8,128)(2,1)} %get-tuple-element.37), channel_id=1, source_target_pairs={{16,0},{32,16},{48,32},{64,48},{80,64},{96,80},{112,96},{128,112},... | collective-permute-start | bytes 393224 | tf_op jit(solution)/shard_map/ppermute | solution.py:288
  87.7 3.7 %copy-start.4 = (bf16[4,128,128]{2,1,0:T(8,128)(2,1)}, bf16[4,128,128]{2,1,0:T(8,128)(2,1)S(1)}, u32[]{:S(2)}) copy-start(bf16[4,128,128]{2,1,0:T(8,128)(2,1)S(1)} %collective-permute-done.4.upper_hbm) | copy-start | bytes 393220
  91.4 0.6 copy-start.5
  112.7 31.5 %all-to-all-start.3 = ((bf16[16,2,128,128]{3,2,1,0:T(8,128)(2,1)}), bf16[16,2,128,128]{3,2,1,0:T(8,128)(2,1)S(1)}, u32[]{:S(2)}, u32[]{:S(2)}) async-start(bf16[16,2,128,128]{3,2,1,0:T(8,128)(2,1)} %listed_residual.1), calls=%async_computation.3 | async-start | bytes 2097152 | tf_op jit(solution)/shard_map/all_to_all | solution.py:292
  121.3 6.4 %collective-permute-start.6 = (bf16[4,128,128]{2,1,0:T(8,128)(2,1)}, bf16[4,128,128]{2,1,0:T(8,128)(2,1)S(1)}, u32[]{:S(2)}, u32[]{:S(2)}) collective-permute-start(bf16[4,128,128]{2,1,0:T(8,128)(2,1)} %get-tuple-element.40), channel_id=1, source_target_pairs={{0,16},{16,32},{32,48},{48,64},{64,80},{80,96},{96,112},{112,128},... | collective-permute-start | bytes 393224 | tf_op jit(solution)/shard_map/ppermute | solution.py:283
  124.5 6.8 %collective-permute-start.7 = (bf16[4,128,128]{2,1,0:T(8,128)(2,1)}, bf16[4,128,128]{2,1,0:T(8,128)(2,1)S(1)}, u32[]{:S(2)}, u32[]{:S(2)}) collective-permute-start(bf16[4,128,128]{2,1,0:T(8,128)(2,1)} %get-tuple-element.41), channel_id=1, source_target_pairs={{16,0},{32,16},{48,32},{64,48},{80,64},{96,80},{112,96},{128,112},... | collective-permute-start | bytes 393224 | tf_op jit(solution)/shard_map/ppermute | solution.py:288
  127.6 3.7 %copy-start = (bf16[4,128,128]{2,1,0:T(8,128)(2,1)}, bf16[4,128,128]{2,1,0:T(8,128)(2,1)S(1)}, u32[]{:S(2)}) copy-start(bf16[4,128,128]{2,1,0:T(8,128)(2,1)S(1)} %collective-permute-done.6.upper_hbm) | copy-start | bytes 393220
  131.3 0.6 copy-start.2
  147.3 31.5 %all-to-all-start.4 = ((bf16[16,2,128,128]{3,2,1,0:T(8,128)(2,1)}), bf16[16,2,128,128]{3,2,1,0:T(8,128)(2,1)S(1)}, u32[]{:S(2)}, u32[]{:S(2)}) async-start(bf16[16,2,128,128]{3,2,1,0:T(8,128)(2,1)} %bitcast.18), calls=%async_computation.4 | async-start | bytes 2097152 | tf_op jit(solution)/shard_map/all_to_all | solution.py:292
  155.0 6.6 %collective-permute-start.8 = (bf16[4,128,128]{2,1,0:T(8,128)(2,1)}, bf16[4,128,128]{2,1,0:T(8,128)(2,1)S(1)}, u32[]{:S(2)}, u32[]{:S(2)}) collective-permute-start(bf16[4,128,128]{2,1,0:T(8,128)(2,1)} %get-tuple-element.44), channel_id=1, source_target_pairs={{0,16},{16,32},{32,48},{48,64},{64,80},{80,96},{96,112},{112,128},... | collective-permute-start | bytes 393224 | tf_op jit(solution)/shard_map/ppermute | solution.py:283
  158.2 7.0 %collective-permute-start.9 = (bf16[4,128,128]{2,1,0:T(8,128)(2,1)}, bf16[4,128,128]{2,1,0:T(8,128)(2,1)S(1)}, u32[]{:S(2)}, u32[]{:S(2)}) collective-permute-start(bf16[4,128,128]{2,1,0:T(8,128)(2,1)} %get-tuple-element.45), channel_id=1, source_target_pairs={{16,0},{32,16},{48,32},{64,48},{80,64},{96,80},{112,96},{128,112},... | collective-permute-start | bytes 393224 | tf_op jit(solution)/shard_map/ppermute | solution.py:288
  161.5 17.2 %copy-start.8 = (bf16[4,128,128]{2,1,0:T(8,128)(2,1)}, bf16[4,128,128]{2,1,0:T(8,128)(2,1)S(1)}, u32[]{:S(2)}) copy-start(bf16[4,128,128]{2,1,0:T(8,128)(2,1)S(1)} %collective-permute-done.8.from_prev_hbm) | copy-start | bytes 393220
  165.2 13.5 %copy-start.9 = (bf16[4,128,128]{2,1,0:T(8,128)(2,1)}, bf16[4,128,128]{2,1,0:T(8,128)(2,1)S(1)}, u32[]{:S(2)}) copy-start(bf16[4,128,128]{2,1,0:T(8,128)(2,1)S(1)} %collective-permute-done.9.from_next_hbm) | copy-start | bytes 393220

commit v5 on v4

--- a/solution.py
+++ b/solution.py
@@ -103,7 +103,7 @@
     return low_ref.at[row] if row < half else high_ref.at[row - half]
 
 
-def near_residual_kernel(cols_hbm, blocks_hbm, rhs_hbm, own_hbm, upper_hbm, lower_hbm, low_ref, high_ref, cols_ref, ext_ref, chunk_ref, rhs_ref, in_sem, cols_sem, block_sem):
+def near_residual_kernel(cols_hbm, blocks_hbm, rhs_hbm, own_hbm, upper_hbm, lower_hbm, low_ref, high_ref, ready_ref, cols_ref, ext_ref, chunk_ref, rhs_ref, in_sem, cols_sem, ready_sem, block_sem):
     rows = rhs_ref.shape[0]
     near = ext_ref.shape[0] - 1
     cols = start(cols_hbm, cols_ref, cols_sem.at[0])
@@ -111,6 +111,7 @@
     pieces.append(start(rhs_hbm.at[0, 0], rhs_ref, in_sem.at[3]))
     groups = range(rows // GROUP)
     blocks = start_blocks(blocks_hbm, 0, chunk_ref, block_sem, groups)
+    ready = start(blocks_hbm.at[0, 0, pl.ds(0, GROUP), pl.ds(1, ready_ref.shape[1])], ready_ref, ready_sem.at[0])
     ext_ref[near] = jnp.zeros_like(ext_ref[near])
     cols.wait()
     wait_all(pieces)
@@ -121,6 +122,7 @@
             i = g * GROUP + j
             picks = [jnp.minimum(cols_ref[0, k, 0, i], near) for k in range(terms)]
             half_row(low_ref, high_ref, i)[...] = rhs_ref[i].astype(F32) - picked_product(chunk_ref, i, range(terms), picks, ext_ref)
+    ready.wait()
 
 
 def fill_extended(near_ref, incoming_ref, ext_ref):
@@ -216,26 +218,28 @@
     wait_all(copies)
 
 
-def listed_residual_kernel(near, cols_hbm, list_hbm, count_hbm, blocks_hbm, low_ref, high_ref, incoming_ref, out_hbm, cols_ref, list_ref, count_ref, packed_ref, ext_ref, chunk_ref, res_ref, in_sem, cols_sem, block_sem, row_sem):
+def listed_residual_kernel(near, cols_hbm, list_hbm, count_hbm, blocks_hbm, low_ref, high_ref, ready_ref, incoming_ref, out_hbm, cols_ref, list_ref, count_ref, packed_ref, ext_ref, chunk_ref, res_ref, in_sem, cols_sem, block_sem, row_sem):
     cols = start(cols_hbm, cols_ref, cols_sem.at[0])
     groups = range(res_ref.shape[0] // GROUP)
     terms = chunk_ref.shape[1]
-    blocks = []
-    for g in groups:
-        part = pl.ds(g * GROUP, GROUP)
-        blocks.append(start(blocks_hbm.at[0, 0, part, pl.ds(1, terms)], chunk_ref.at[part], block_sem.at[g]))
+    blocks = [None]
+    for g in groups[1:]:
+        source = blocks_hbm.at[0, 0, pl.ds(g * GROUP, GROUP), pl.ds(1, terms)]
+        blocks.append(start(source, chunk_ref.at[pl.ds((g - 1) * GROUP, GROUP)], block_sem.at[g - 1]))
     lists = start_lists(list_hbm, count_hbm, list_ref, count_ref, in_sem)
     listed = incoming_ref.shape[0]
     ext_ref[:listed] = incoming_ref[...]
     ext_ref[listed] = jnp.zeros_like(ext_ref[listed])
     cols.wait()
     for g, block in zip(groups, blocks):
-        block.wait()
+        if g > 0:
+            block.wait()
         for j in range(GROUP):
             i = g * GROUP + j
             named = [cols_ref[0, k + 1, 0, i] for k in range(terms)]
             picks = [jnp.where(col >= near, col - near, listed) for col in named]
-            image = picked_product(chunk_ref, i, range(terms), picks, ext_ref)
+            source, index = (chunk_ref, i - GROUP) if g > 0 else (ready_ref, j)
+            image = picked_product(source, index, range(terms), picks, ext_ref)
             res_ref[i] = (half_row(low_ref, high_ref, i)[...] - image).astype(BF)
     wait_all(lists)
     wait_all(start_packing(res_ref, packed_ref, out_hbm, list_ref, count_ref, row_sem))
@@ -317,6 +321,9 @@
 
     def chunk(count):
         return pltpu.VMEM((count, terms, block, block), BF)
+
+    def later_blocks(count):
+        return pltpu.VMEM((count, terms - 1, block, block), BF)
 
     lists = [smem(send_list), smem(send_count)]
     edges = pltpu.VMEM((2, OVL, block, vectors), BF)
@@ -409,11 +416,11 @@
         staged=(part, returned),
     )
     upper, lower, incoming = extension(packed, head, tail)
-    low, high = call(
+    low, high, ready = call(
         near_residual_kernel,
         "near_residual",
-        (tiles(rows // 2, F32), tiles(rows // 2, F32)),
-        [smem(j_cols), tiles(near_rows + 1), chunk(rows), tiles(rows), DMA((4,)), DMA((1,)), DMA((groups,))],
+        (tiles(rows // 2, F32), tiles(rows // 2, F32), later_blocks(GROUP)),
+        [smem(j_cols), tiles(near_rows + 1), chunk(rows), tiles(rows), DMA((4,)), DMA((1,)), DMA((1,)), DMA((groups,))],
         cost(2 * rows * terms * block * tile, 4 * (near_rows + terms * rows) * tile),
         j_cols,
         j_blocks,
@@ -426,13 +433,13 @@
         functools.partial(listed_residual_kernel, near_rows),
         "listed_residual",
         packed_t,
-        [smem(j_cols), *lists, tiles(listed), tiles(listed + 1), pltpu.VMEM((rows, terms - 1, block, block), BF), tiles(rows), DMA((2,)), DMA((1,)), DMA((groups,)), DMA((peers,))],
+        [smem(j_cols), *lists, tiles(listed), tiles(listed + 1), later_blocks(rows - GROUP), tiles(rows), DMA((2,)), DMA((1,)), DMA((groups - 1,)), DMA((peers,))],
         cost(2 * rows * terms * block * tile, 12 * extended_rows * tile),
         j_cols,
         send_list,
         send_count,
         j_blocks,
-        staged=(low, high, incoming),
+        staged=(low, high, ready, incoming),
     )
     residual, head, tail = call(
         own_residual_kernel,

time: 182 us -> 183 us (level)
  local copies, waits for them, and re-layouts: 1.95 us -> 3.8 us
    unnamed x20 -> x24, local copies, waits for them, and re-layouts: 1.95 us -> 3.8 us
where the time goes in v5:
time: 183 us; the launch traced here: 182 us
  waiting for transfers between devices  94.1 us (51%)
  starting transfers between devices  47 us (26%)
  Pallas kernels  37 us (20%)
  local copies, waits for them, and re-layouts  3.8 us (2%)
    all_to_all x5, waiting for transfers between devices, route(): lax.all_to_all(buffer, 'cross', split_axis=0, concat_axis=0, tiled=True)  66.2 us
    pallas_call x12, Pallas kernels, call(): pl.pallas_call(kernel, out_shape=out_shape, in_specs=[HBM] * len(operands...  37 us
    all_to_all x5, starting transfers between devices, route(): lax.all_to_all(buffer, 'cross', split_axis=0, concat_axis=0, tiled=True)  24.4 us
    ppermute x5, waiting for transfers between devices, to_prev(): return lax.ppermute(x, 'slab', [(i + 1, i) for i in range(count - 1)])  18.4 us
    ppermute x5, starting transfers between devices, to_next(): return lax.ppermute(x, 'slab', [(i, i + 1) for i in range(count - 1)])  16.1 us
    ppermute x5, waiting for transfers between devices, to_next(): return lax.ppermute(x, 'slab', [(i, i + 1) for i in range(count - 1)])  9.42 us
    ppermute x5, starting transfers between devices, to_prev(): return lax.ppermute(x, 'slab', [(i + 1, i) for i in range(count - 1)])  6.46 us
    unnamed x24, local copies, waits for them, and re-layouts  3.8 us
  transfers between devices with their start and end apart: 15, of which 15 were waited for; matrix products, arithmetic and copies ran while one was open for 0% of the time, Pallas kernels for 11%

profile of v5, /device:TPU:1, one launch (start us, length us, event | category | flops | bytes accessed | tf_op | source)
XLA Modules:
  0.0 182.2 jit_solution(16206788764493958214)
XLA Ops:
  0.0 2.5 %pack_rhs.1 = (bf16[16,2,128,128]{3,2,1,0:T(8,128)(2,1)}, bf16[4,128,128]{2,1,0:T(8,128)(2,1)}, bf16[4,128,128]{2,1,0:T(8,128)(2,1)}) custom-call(s32[1,1,2,16]{3,2,1,0:T(2,128)} %bitcast.24, s32[1,1,16]{2,1,0:T(1,128)} %count_hbm.7, bf16[1,1,32,128,128]{4,3,2,1,0:T(8,128)(2,1)} %rhs_hbm.5), custom_call_target="tpu_custom_call" | custom-call | bytes 2097152 | tf_op jit(solution)/shard_map/pack_rhs/pallas_call | solution.py:335
  2.5 10.0 %all-to-all-start = ((bf16[16,2,128,128]{3,2,1,0:T(8,128)(2,1)}), bf16[16,2,128,128]{3,2,1,0:T(8,128)(2,1)S(1)}, u32[]{:S(2)}, u32[]{:S(2)}) async-start(bf16[16,2,128,128]{3,2,1,0:T(8,128)(2,1)} %get-tuple-element.30), calls=%async_computation | async-start | bytes 2097152 | tf_op jit(solution)/shard_map/all_to_all | solution.py:296
  12.5 3.2 %collective-permute-start = (bf16[4,128,128]{2,1,0:T(8,128)(2,1)}, bf16[4,128,128]{2,1,0:T(8,128)(2,1)S(1)}, u32[]{:S(2)}, u32[]{:S(2)}) collective-permute-start(bf16[4,128,128]{2,1,0:T(8,128)(2,1)} %get-tuple-element.28), channel_id=1, source_target_pairs={{0,16},{16,32},{32,48},{48,64},{64,80},{80,96},{96,112},{112,128},... | collective-permute-start | bytes 393224 | tf_op jit(solution)/shard_map/ppermute | solution.py:287
  15.7 1.3 collective-permute-start.1
  17.0 1.8 %collective-permute-done.upper_hbm = bf16[4,128,128]{2,1,0:T(8,128)(2,1)S(1)} collective-permute-done((bf16[4,128,128]{2,1,0:T(8,128)(2,1)}, bf16[4,128,128]{2,1,0:T(8,128)(2,1)S(1)}, u32[]{:S(2)}, u32[]{:S(2)}) %collective-permute-start) | collective-permute-done | bytes 131104 | tf_op jit(solution)/shard_map/ppermute | solution.py:287
  18.9 3.7 %collective-permute-done.1.lower_hbm = bf16[4,128,128]{2,1,0:T(8,128)(2,1)S(1)} collective-permute-done((bf16[4,128,128]{2,1,0:T(8,128)(2,1)}, bf16[4,128,128]{2,1,0:T(8,128)(2,1)S(1)}, u32[]{:S(2)}, u32[]{:S(2)}) %collective-permute-start.1) | collective-permute-done | bytes 131104 | tf_op jit(solution)/shard_map/ppermute | solution.py:292
  22.6 0.0 copy-done.3
  22.6 0.7 copy-done.5
  23.2 1.6 stage_slots.2
  24.8 15.6 %all-to-all-done = bf16[16,2,128,128]{3,2,1,0:T(8,128)(2,1)S(1)} async-done(((bf16[16,2,128,128]{3,2,1,0:T(8,128)(2,1)}), bf16[16,2,128,128]{3,2,1,0:T(8,128)(2,1)S(1)}, u32[]{:S(2)}, u32[]{:S(2)}) %all-to-all-start) | async-done | bytes 1048608 | tf_op jit(solution)/shard_map/all_to_all | solution.py:296
  40.4 3.1 %slot_partial.2 = bf16[32,128,128]{2,1,0:T(8,128)(2,1)} custom-call(s32[1,3,1,72]{3,2,1,0:T(1,128)} %bitcast.20, bf16[1,1,72,3,128,128]{5,4,3,2,1,0:T(8,128)(2,1)} %blocks_hbm.17, bf16[40,128,128]{2,1,0:T(8,128)(2,1)S(1)} %get-tuple-element.34.near_ref, bf16[32,128,128]{2,1,0:T(8,128)(2,1)S(1)} %bitcast.12, ...), custom_call_target="tpu_custom_call" | custom-call | flops 402653184 | bytes 14155776 | tf_op jit(solution)/shard_map/slot_partial/pallas_call | solution.py:335
  43.5 3.6 %all-to-all-start.1 = ((bf16[16,2,128,128]{3,2,1,0:T(8,128)(2,1)}), bf16[16,2,128,128]{3,2,1,0:T(8,128)(2,1)S(1)}, u32[]{:S(2)}, u32[]{:S(2)}) async-start(bf16[16,2,128,128]{3,2,1,0:T(8,128)(2,1)} %bitcast.19), calls=%async_computation.1 | async-start | bytes 2097152 | tf_op jit(solution)/shard_map/all_to_all | solution.py:296
  47.1 3.9 %own_partial.2 = (bf16[32,128,128]{2,1,0:T(8,128)(2,1)S(1)}, bf16[4,128,128]{2,1,0:T(8,128)(2,1)}, bf16[4,128,128]{2,1,0:T(8,128)(2,1)}) custom-call(s32[1,3,1,72]{3,2,1,0:T(1,128)} %bitcast.21, bf16[1,1,72,3,128,128]{5,4,3,2,1,0:T(8,128)(2,1)} %blocks_hbm.17, bf16[1,1,32,128,128]{4,3,2,1,0:T(8,128)(2,1)} %rhs_hbm.5, bf16[4,128,128]{2,1,0:T(8,128)(2,1)} %copy-done.3, ...), custom_call_target="tpu_custom_call" | custom-call | flops 503316480 | bytes 14155776 | tf_op jit(solution)/shard_map/own_partial/pallas_call | solution.py:335
  51.0 3.2 %collective-permute-start.2 = (bf16[4,128,128]{2,1,0:T(8,128)(2,1)}, bf16[4,128,128]{2,1,0:T(8,128)(2,1)S(1)}, u32[]{:S(2)}, u32[]{:S(2)}) collective-permute-start(bf16[4,128,128]{2,1,0:T(8,128)(2,1)} %get-tuple-element.31), channel_id=1, source_target_pairs={{0,16},{16,32},{32,48},{48,64},{64,80},{80,96},{96,112},{112,128},... | collective-permute-start | bytes 393224 | tf_op jit(solution)/shard_map/ppermute | solution.py:287
  54.3 1.3 collective-permute-start.3
  55.6 1.9 %collective-permute-done.2.from_prev_hbm = bf16[4,128,128]{2,1,0:T(8,128)(2,1)S(1)} collective-permute-done((bf16[4,128,128]{2,1,0:T(8,128)(2,1)}, bf16[4,128,128]{2,1,0:T(8,128)(2,1)S(1)}, u32[]{:S(2)}, u32[]{:S(2)}) %collective-permute-start.2) | collective-permute-done | bytes 131104 | tf_op jit(solution)/shard_map/ppermute | solution.py:287
  57.4 3.7 %collective-permute-done.3.from_next_hbm = bf16[4,128,128]{2,1,0:T(8,128)(2,1)S(1)} collective-permute-done((bf16[4,128,128]{2,1,0:T(8,128)(2,1)}, bf16[4,128,128]{2,1,0:T(8,128)(2,1)S(1)}, u32[]{:S(2)}, u32[]{:S(2)}) %collective-permute-start.3) | collective-permute-done | bytes 131104 | tf_op jit(solution)/shard_map/ppermute | solution.py:292
  61.1 13.9 %all-to-all-done.1 = bf16[16,2,128,128]{3,2,1,0:T(8,128)(2,1)S(1)} async-done(((bf16[16,2,128,128]{3,2,1,0:T(8,128)(2,1)}), bf16[16,2,128,128]{3,2,1,0:T(8,128)(2,1)S(1)}, u32[]{:S(2)}, u32[]{:S(2)}) %all-to-all-start.1) | async-done | bytes 1048608 | tf_op jit(solution)/shard_map/all_to_all | solution.py:296
  75.0 2.8 %assemble_first.1 = (bf16[1,1,32,128,128]{4,3,2,1,0:T(8,128)(2,1)}, bf16[16,2,128,128]{3,2,1,0:T(8,128)(2,1)}, bf16[4,128,128]{2,1,0:T(8,128)(2,1)}, bf16[4,128,128]{2,1,0:T(8,128)(2,1)}) custom-call(s32[1,1,2,16]{3,2,1,0:T(2,128)} %bitcast.25, s32[1,1,16]{2,1,0:T(1,128)} %count_hbm.7, bf16[4,128,128]{2,1,0:T(8,128)(2,1)} %copy-done.8, ...), custom_call_target="tpu_custom_call" | custom-call | bytes 5242880 | tf_op jit(solution)/shard_map/assemble_first/pallas_call | solution.py:335
  77.8 3.6 %all-to-all-start.2 = ((bf16[16,2,128,128]{3,2,1,0:T(8,128)(2,1)}), bf16[16,2,128,128]{3,2,1,0:T(8,128)(2,1)S(1)}, u32[]{:S(2)}, u32[]{:S(2)}) async-start(bf16[16,2,128,128]{3,2,1,0:T(8,128)(2,1)} %get-tuple-element.39), calls=%async_computation.2 | async-start | bytes 2097152 | tf_op jit(solution)/shard_map/all_to_all | solution.py:296
  81.3 3.2 %collective-permute-start.4 = (bf16[4,128,128]{2,1,0:T(8,128)(2,1)}, bf16[4,128,128]{2,1,0:T(8,128)(2,1)S(1)}, u32[]{:S(2)}, u32[]{:S(2)}) collective-permute-start(bf16[4,128,128]{2,1,0:T(8,128)(2,1)} %get-tuple-element.37), channel_id=1, source_target_pairs={{0,16},{16,32},{32,48},{48,64},{64,80},{80,96},{96,112},{112,128},... | collective-permute-start | bytes 393224 | tf_op jit(solution)/shard_map/ppermute | solution.py:287
  84.6 1.3 collective-permute-start.5
  85.9 1.9 %collective-permute-done.4.upper_hbm = bf16[4,128,128]{2,1,0:T(8,128)(2,1)S(1)} collective-permute-done((bf16[4,128,128]{2,1,0:T(8,128)(2,1)}, bf16[4,128,128]{2,1,0:T(8,128)(2,1)S(1)}, u32[]{:S(2)}, u32[]{:S(2)}) %collective-permute-start.4) | collective-permute-done | bytes 131104 | tf_op jit(solution)/shard_map/ppermute | solution.py:287
  87.7 3.7 %collective-permute-done.5.lower_hbm = bf16[4,128,128]{2,1,0:T(8,128)(2,1)S(1)} collective-permute-done((bf16[4,128,128]{2,1,0:T(8,128)(2,1)}, bf16[4,128,128]{2,1,0:T(8,128)(2,1)S(1)}, u32[]{:S(2)}, u32[]{:S(2)}) %collective-permute-start.5) | collective-permute-done | bytes 131104 | tf_op jit(solution)/shard_map/ppermute | solution.py:292
  91.4 0.6 copy-done.7
  92.1 3.9 %near_residual.1 = (f32[16,128,128]{2,1,0:T(8,128)S(1)}, f32[16,128,128]{2,1,0:T(8,128)S(1)}, bf16[8,2,128,128]{3,2,1,0:T(8,128)(2,1)S(1)}) custom-call(s32[1,3,1,32]{3,2,1,0:T(1,128)} %bitcast.28, bf16[1,1,32,3,128,128]{5,4,3,2,1,0:T(8,128)(2,1)} %blocks_hbm.14, bf16[1,1,32,128,128]{4,3,2,1,0:T(8,128)(2,1)} %rhs_hbm.5, ...), custom_call_target="tpu_custom_call" | custom-call | flops 402653184 | bytes 8912896 | tf_op jit(solution)/shard_map/near_residual/pallas_call | solution.py:335
  96.0 0.8 copy-done
  96.7 12.5 %all-to-all-done.2 = bf16[16,2,128,128]{3,2,1,0:T(8,128)(2,1)S(1)} async-done(((bf16[16,2,128,128]{3,2,1,0:T(8,128)(2,1)}), bf16[16,2,128,128]{3,2,1,0:T(8,128)(2,1)S(1)}, u32[]{:S(2)}, u32[]{:S(2)}) %all-to-all-start.2) | async-done | bytes 1048608 | tf_op jit(solution)/shard_map/all_to_all | solution.py:296
  109.2 1.0 copy-done.1
  110.3 3.3 %listed_residual.1 = bf16[16,2,128,128]{3,2,1,0:T(8,128)(2,1)} custom-call(s32[1,3,1,32]{3,2,1,0:T(1,128)} %bitcast.29, s32[1,1,2,16]{3,2,1,0:T(2,128)} %bitcast.26, s32[1,1,16]{2,1,0:T(1,128)} %count_hbm.7, bf16[1,1,32,3,128,128]{5,4,3,2,1,0:T(8,128)(2,1)} %blocks_hbm.14, f32[16,128,128]{2,1,0:T(8,128)S(1)} %get-tuple-element.43.low_ref, ...), custom_call_target="tpu_custom_call" | custom-call | flops 402653184 | bytes 14155776 | tf_op jit(solution)/shard_map/listed_residual/pallas_call | solution.py:335
  113.6 3.6 %all-to-all-start.3 = ((bf16[16,2,128,128]{3,2,1,0:T(8,128)(2,1)}), bf16[16,2,128,128]{3,2,1,0:T(8,128)(2,1)S(1)}, u32[]{:S(2)}, u32[]{:S(2)}) async-start(bf16[16,2,128,128]{3,2,1,0:T(8,128)(2,1)} %listed_residual.1), calls=%async_computation.3 | async-start | bytes 2097152 | tf_op jit(solution)/shard_map/all_to_all | solution.py:296
  117.1 5.0 %own_residual.1 = (bf16[1,1,32,128,128]{4,3,2,1,0:T(8,128)(2,1)}, bf16[4,128,128]{2,1,0:T(8,128)(2,1)}, bf16[4,128,128]{2,1,0:T(8,128)(2,1)}) custom-call(s32[1,3,1,32]{3,2,1,0:T(1,128)} %bitcast.30, bf16[1,1,32,3,128,128]{5,4,3,2,1,0:T(8,128)(2,1)} %blocks_hbm.14, bf16[1,1,32,128,128]{4,3,2,1,0:T(8,128)(2,1)} %rhs_hbm.5, ...), custom_call_target="tpu_custom_call" | custom-call | flops 402653184 | bytes 14155776 | tf_op jit(solution)/shard_map/own_residual/pallas_call | solution.py:335
  122.1 3.2 %collective-permute-start.6 = (bf16[4,128,128]{2,1,0:T(8,128)(2,1)}, bf16[4,128,128]{2,1,0:T(8,128)(2,1)S(1)}, u32[]{:S(2)}, u32[]{:S(2)}) collective-permute-start(bf16[4,128,128]{2,1,0:T(8,128)(2,1)} %get-tuple-element.41), channel_id=1, source_target_pairs={{0,16},{16,32},{32,48},{48,64},{64,80},{80,96},{96,112},{112,128},... | collective-permute-start | bytes 393224 | tf_op jit(solution)/shard_map/ppermute | solution.py:287
  125.3 1.3 collective-permute-start.7
  126.6 1.8 %collective-permute-done.6.upper_hbm = bf16[4,128,128]{2,1,0:T(8,128)(2,1)S(1)} collective-permute-done((bf16[4,128,128]{2,1,0:T(8,128)(2,1)}, bf16[4,128,128]{2,1,0:T(8,128)(2,1)S(1)}, u32[]{:S(2)}, u32[]{:S(2)}) %collective-permute-start.6) | collective-permute-done | bytes 131104 | tf_op jit(solution)/shard_map/ppermute | solution.py:287
  128.5 3.7 %collective-permute-done.7.lower_hbm = bf16[4,128,128]{2,1,0:T(8,128)(2,1)S(1)} collective-permute-done((bf16[4,128,128]{2,1,0:T(8,128)(2,1)}, bf16[4,128,128]{2,1,0:T(8,128)(2,1)S(1)}, u32[]{:S(2)}, u32[]{:S(2)}) %collective-permute-start.7) | collective-permute-done | bytes 131104 | tf_op jit(solution)/shard_map/ppermute | solution.py:292
  132.2 0.6 copy-done.4
  132.8 1.6 stage_slots.3
  134.4 10.6 %all-to-all-done.3 = bf16[16,2,128,128]{3,2,1,0:T(8,128)(2,1)S(1)} async-done(((bf16[16,2,128,128]{3,2,1,0:T(8,128)(2,1)}), bf16[16,2,128,128]{3,2,1,0:T(8,128)(2,1)S(1)}, u32[]{:S(2)}, u32[]{:S(2)}) %all-to-all-start.3) | async-done | bytes 1048608 | tf_op jit(solution)/shard_map/all_to_all | solution.py:296
  145.0 3.1 %slot_partial.3 = bf16[32,128,128]{2,1,0:T(8,128)(2,1)} custom-call(s32[1,3,1,72]{3,2,1,0:T(1,128)} %bitcast.22, bf16[1,1,72,3,128,128]{5,4,3,2,1,0:T(8,128)(2,1)} %blocks_hbm.17, bf16[40,128,128]{2,1,0:T(8,128)(2,1)S(1)} %get-tuple-element.49.near_ref, bf16[32,128,128]{2,1,0:T(8,128)(2,1)S(1)} %bitcast.10, ...), custom_call_target="tpu_custom_call" | custom-call | flops 402653184 | bytes 14155776 | tf_op jit(solution)/shard_map/slot_partial/pallas_call | solution.py:335
  148.1 3.7 %all-to-all-start.4 = ((bf16[16,2,128,128]{3,2,1,0:T(8,128)(2,1)}), bf16[16,2,128,128]{3,2,1,0:T(8,128)(2,1)S(1)}, u32[]{:S(2)}, u32[]{:S(2)}) async-start(bf16[16,2,128,128]{3,2,1,0:T(8,128)(2,1)} %bitcast.18), calls=%async_computation.4 | async-start | bytes 2097152 | tf_op jit(solution)/shard_map/all_to_all | solution.py:296
  151.9 3.9 %own_partial.3 = (bf16[32,128,128]{2,1,0:T(8,128)(2,1)S(1)}, bf16[4,128,128]{2,1,0:T(8,128)(2,1)}, bf16[4,128,128]{2,1,0:T(8,128)(2,1)}) custom-call(s32[1,3,1,72]{3,2,1,0:T(1,128)} %bitcast.23, bf16[1,1,72,3,128,128]{5,4,3,2,1,0:T(8,128)(2,1)} %blocks_hbm.17, bf16[1,1,32,128,128]{4,3,2,1,0:T(8,128)(2,1)} %get-tuple-element.40.own_hbm, ...), custom_call_target="tpu_custom_call" | custom-call | flops 503316480 | bytes 14155776 | tf_op jit(solution)/shard_map/own_partial/pallas_call | solution.py:335
  155.8 3.2 %collective-permute-start.8 = (bf16[4,128,128]{2,1,0:T(8,128)(2,1)}, bf16[4,128,128]{2,1,0:T(8,128)(2,1)S(1)}, u32[]{:S(2)}, u32[]{:S(2)}) collective-permute-start(bf16[4,128,128]{2,1,0:T(8,128)(2,1)} %get-tuple-element.46), channel_id=1, source_target_pairs={{0,16},{16,32},{32,48},{48,64},{64,80},{80,96},{96,112},{112,128},... | collective-permute-start | bytes 393224 | tf_op jit(solution)/shard_map/ppermute | solution.py:287
  159.0 1.3 collective-permute-start.9
  160.3 2.0 %collective-permute-done.8.from_prev_hbm = bf16[4,128,128]{2,1,0:T(8,128)(2,1)S(1)} collective-permute-done((bf16[4,128,128]{2,1,0:T(8,128)(2,1)}, bf16[4,128,128]{2,1,0:T(8,128)(2,1)S(1)}, u32[]{:S(2)}, u32[]{:S(2)}) %collective-permute-start.8) | collective-permute-done | bytes 131104 | tf_op jit(solution)/shard_map/ppermute | solution.py:287
  162.4 3.7 %collective-permute-done.9.from_next_hbm = bf16[4,128,128]{2,1,0:T(8,128)(2,1)S(1)} collective-permute-done((bf16[4,128,128]{2,1,0:T(8,128)(2,1)}, bf16[4,128,128]{2,1,0:T(8,128)(2,1)S(1)}, u32[]{:S(2)}, u32[]{:S(2)}) %collective-permute-start.9) | collective-permute-done | bytes 131104 | tf_op jit(solution)/shard_map/ppermute | solution.py:292
  166.1 13.5 %all-to-all-done.4 = bf16[16,2,128,128]{3,2,1,0:T(8,128)(2,1)S(1)} async-done(((bf16[16,2,128,128]{3,2,1,0:T(8,128)(2,1)}), bf16[16,2,128,128]{3,2,1,0:T(8,128)(2,1)S(1)}, u32[]{:S(2)}, u32[]{:S(2)}) %all-to-all-start.4) | async-done | bytes 1048608 | tf_op jit(solution)/shard_map/all_to_all | solution.py:296
  179.6 2.5 %assemble_second.1 = bf16[1,1,32,128,128]{4,3,2,1,0:T(8,128)(2,1)} custom-call(s32[1,1,2,16]{3,2,1,0:T(2,128)} %bitcast.27, s32[1,1,16]{2,1,0:T(1,128)} %count_hbm.7, bf16[4,128,128]{2,1,0:T(8,128)(2,1)} %copy-done.10, bf16[4,128,128]{2,1,0:T(8,128)(2,1)} %copy-done.11, bf16[1,1,32,128,128]{4,3,2,1,0:T(8,128)(2,1)} %get-tuple-element.36.own_hbm.first_hbm, ...), custom_call_target="tpu_custom_call" | custom-call | bytes 5242880 | tf_op jit(solution)/shard_map/assemble_second/pallas_call | solution.py:335
  (18 shorter events, 0.0 us)
Async XLA Ops:
  2.5 37.9 %all-to-all-start = ((bf16[16,2,128,128]{3,2,1,0:T(8,128)(2,1)}), bf16[16,2,128,128]{3,2,1,0:T(8,128)(2,1)S(1)}, u32[]{:S(2)}, u32[]{:S(2)}) async-start(bf16[16,2,128,128]{3,2,1,0:T(8,128)(2,1)} %get-tuple-element.30), calls=%async_computation | async-start | bytes 2097152 | tf_op jit(solution)/shard_map/all_to_all | solution.py:296
  12.5 6.4 %collective-permute-start = (bf16[4,128,128]{2,1,0:T(8,128)(2,1)}, bf16[4,128,128]{2,1,0:T(8,128)(2,1)S(1)}, u32[]{:S(2)}, u32[]{:S(2)}) collective-permute-start(bf16[4,128,128]{2,1,0:T(8,128)(2,1)} %get-tuple-element.28), channel_id=1, source_target_pairs={{0,16},{16,32},{32,48},{48,64},{64,80},{80,96},{96,112},{112,128},... | collective-permute-start | bytes 393224 | tf_op jit(solution)/shard_map/ppermute | solution.py:287
  15.7 6.8 %collective-permute-start.1 = (bf16[4,128,128]{2,1,0:T(8,128)(2,1)}, bf16[4,128,128]{2,1,0:T(8,128)(2,1)S(1)}, u32[]{:S(2)}, u32[]{:S(2)}) collective-permute-start(bf16[4,128,128]{2,1,0:T(8,128)(2,1)} %get-tuple-element.29), channel_id=1, source_target_pairs={{16,0},{32,16},{48,32},{64,48},{80,64},{96,80},{112,96},{128,112},... | collective-permute-start | bytes 393224 | tf_op jit(solution)/shard_map/ppermute | solution.py:292
  18.9 3.7 %copy-start.3 = (bf16[4,128,128]{2,1,0:T(8,128)(2,1)}, bf16[4,128,128]{2,1,0:T(8,128)(2,1)S(1)}, u32[]{:S(2)}) copy-start(bf16[4,128,128]{2,1,0:T(8,128)(2,1)S(1)} %collective-permute-done.upper_hbm) | copy-start | bytes 393220
  22.6 0.7 copy-start.5
  43.5 31.5 %all-to-all-start.1 = ((bf16[16,2,128,128]{3,2,1,0:T(8,128)(2,1)}), bf16[16,2,128,128]{3,2,1,0:T(8,128)(2,1)S(1)}, u32[]{:S(2)}, u32[]{:S(2)}) async-start(bf16[16,2,128,128]{3,2,1,0:T(8,128)(2,1)} %bitcast.19), calls=%async_computation.1 | async-start | bytes 2097152 | tf_op jit(solution)/shard_map/all_to_all | solution.py:296
  51.0 6.4 %collective-permute-start.2 = (bf16[4,128,128]{2,1,0:T(8,128)(2,1)}, bf16[4,128,128]{2,1,0:T(8,128)(2,1)S(1)}, u32[]{:S(2)}, u32[]{:S(2)}) collective-permute-start(bf16[4,128,128]{2,1,0:T(8,128)(2,1)} %get-tuple-element.31), channel_id=1, source_target_pairs={{0,16},{16,32},{32,48},{48,64},{64,80},{80,96},{96,112},{112,128},... | collective-permute-start | bytes 393224 | tf_op jit(solution)/shard_map/ppermute | solution.py:287
  54.3 6.8 %collective-permute-start.3 = (bf16[4,128,128]{2,1,0:T(8,128)(2,1)}, bf16[4,128,128]{2,1,0:T(8,128)(2,1)S(1)}, u32[]{:S(2)}, u32[]{:S(2)}) collective-permute-start(bf16[4,128,128]{2,1,0:T(8,128)(2,1)} %get-tuple-element.32), channel_id=1, source_target_pairs={{16,0},{32,16},{48,32},{64,48},{80,64},{96,80},{112,96},{128,112},... | collective-permute-start | bytes 393224 | tf_op jit(solution)/shard_map/ppermute | solution.py:292
  57.4 17.6 %copy-start.8 = (bf16[4,128,128]{2,1,0:T(8,128)(2,1)}, bf16[4,128,128]{2,1,0:T(8,128)(2,1)S(1)}, u32[]{:S(2)}) copy-start(bf16[4,128,128]{2,1,0:T(8,128)(2,1)S(1)} %collective-permute-done.2.from_prev_hbm) | copy-start | bytes 393220
  61.1 13.9 %copy-start.9 = (bf16[4,128,128]{2,1,0:T(8,128)(2,1)}, bf16[4,128,128]{2,1,0:T(8,128)(2,1)S(1)}, u32[]{:S(2)}) copy-start(bf16[4,128,128]{2,1,0:T(8,128)(2,1)S(1)} %collective-permute-done.3.from_next_hbm) | copy-start | bytes 393220
  77.8 31.5 %all-to-all-start.2 = ((bf16[16,2,128,128]{3,2,1,0:T(8,128)(2,1)}), bf16[16,2,128,128]{3,2,1,0:T(8,128)(2,1)S(1)}, u32[]{:S(2)}, u32[]{:S(2)}) async-start(bf16[16,2,128,128]{3,2,1,0:T(8,128)(2,1)} %get-tuple-element.39), calls=%async_computation.2 | async-start | bytes 2097152 | tf_op jit(solution)/shard_map/all_to_all | solution.py:296
  81.3 6.4 %collective-permute-start.4 = (bf16[4,128,128]{2,1,0:T(8,128)(2,1)}, bf16[4,128,128]{2,1,0:T(8,128)(2,1)S(1)}, u32[]{:S(2)}, u32[]{:S(2)}) collective-permute-start(bf16[4,128,128]{2,1,0:T(8,128)(2,1)} %get-tuple-element.37), channel_id=1, source_target_pairs={{0,16},{16,32},{32,48},{48,64},{64,80},{80,96},{96,112},{112,128},... | collective-permute-start | bytes 393224 | tf_op jit(solution)/shard_map/ppermute | solution.py:287
  84.6 6.8 %collective-permute-start.5 = (bf16[4,128,128]{2,1,0:T(8,128)(2,1)}, bf16[4,128,128]{2,1,0:T(8,128)(2,1)S(1)}, u32[]{:S(2)}, u32[]{:S(2)}) collective-permute-start(bf16[4,128,128]{2,1,0:T(8,128)(2,1)} %get-tuple-element.38), channel_id=1, source_target_pairs={{16,0},{32,16},{48,32},{64,48},{80,64},{96,80},{112,96},{128,112},... | collective-permute-start | bytes 393224 | tf_op jit(solution)/shard_map/ppermute | solution.py:292
  87.7 3.7 %copy-start.6 = (bf16[4,128,128]{2,1,0:T(8,128)(2,1)}, bf16[4,128,128]{2,1,0:T(8,128)(2,1)S(1)}, u32[]{:S(2)}) copy-start(bf16[4,128,128]{2,1,0:T(8,128)(2,1)S(1)} %collective-permute-done.4.upper_hbm) | copy-start | bytes 393220
  91.4 0.6 copy-start.7
  96.0 0.8 copy-start
  109.2 1.0 copy-start.1
  113.6 31.5 %all-to-all-start.3 = ((bf16[16,2,128,128]{3,2,1,0:T(8,128)(2,1)}), bf16[16,2,128,128]{3,2,1,0:T(8,128)(2,1)S(1)}, u32[]{:S(2)}, u32[]{:S(2)}) async-start(bf16[16,2,128,128]{3,2,1,0:T(8,128)(2,1)} %listed_residual.1), calls=%async_computation.3 | async-start | bytes 2097152 | tf_op jit(solution)/shard_map/all_to_all | solution.py:296
  122.1 6.4 %collective-permute-start.6 = (bf16[4,128,128]{2,1,0:T(8,128)(2,1)}, bf16[4,128,128]{2,1,0:T(8,128)(2,1)S(1)}, u32[]{:S(2)}, u32[]{:S(2)}) collective-permute-start(bf16[4,128,128]{2,1,0:T(8,128)(2,1)} %get-tuple-element.41), channel_id=1, source_target_pairs={{0,16},{16,32},{32,48},{48,64},{64,80},{80,96},{96,112},{112,128},... | collective-permute-start | bytes 393224 | tf_op jit(solution)/shard_map/ppermute | solution.py:287
  125.3 6.8 %collective-permute-start.7 = (bf16[4,128,128]{2,1,0:T(8,128)(2,1)}, bf16[4,128,128]{2,1,0:T(8,128)(2,1)S(1)}, u32[]{:S(2)}, u32[]{:S(2)}) collective-permute-start(bf16[4,128,128]{2,1,0:T(8,128)(2,1)} %get-tuple-element.42), channel_id=1, source_target_pairs={{16,0},{32,16},{48,32},{64,48},{80,64},{96,80},{112,96},{128,112},... | collective-permute-start | bytes 393224 | tf_op jit(solution)/shard_map/ppermute | solution.py:292
  128.5 3.7 %copy-start.2 = (bf16[4,128,128]{2,1,0:T(8,128)(2,1)}, bf16[4,128,128]{2,1,0:T(8,128)(2,1)S(1)}, u32[]{:S(2)}) copy-start(bf16[4,128,128]{2,1,0:T(8,128)(2,1)S(1)} %collective-permute-done.6.upper_hbm) | copy-start | bytes 393220
  132.2 0.6 copy-start.4
  148.1 31.5 %all-to-all-start.4 = ((bf16[16,2,128,128]{3,2,1,0:T(8,128)(2,1)}), bf16[16,2,128,128]{3,2,1,0:T(8,128)(2,1)S(1)}, u32[]{:S(2)}, u32[]{:S(2)}) async-start(bf16[16,2,128,128]{3,2,1,0:T(8,128)(2,1)} %bitcast.18), calls=%async_computation.4 | async-start | bytes 2097152 | tf_op jit(solution)/shard_map/all_to_all | solution.py:296
  155.8 6.6 %collective-permute-start.8 = (bf16[4,128,128]{2,1,0:T(8,128)(2,1)}, bf16[4,128,128]{2,1,0:T(8,128)(2,1)S(1)}, u32[]{:S(2)}, u32[]{:S(2)}) collective-permute-start(bf16[4,128,128]{2,1,0:T(8,128)(2,1)} %get-tuple-element.46), channel_id=1, source_target_pairs={{0,16},{16,32},{32,48},{48,64},{64,80},{80,96},{96,112},{112,128},... | collective-permute-start | bytes 393224 | tf_op jit(solution)/shard_map/ppermute | solution.py:287
  159.0 7.0 %collective-permute-start.9 = (bf16[4,128,128]{2,1,0:T(8,128)(2,1)}, bf16[4,128,128]{2,1,0:T(8,128)(2,1)S(1)}, u32[]{:S(2)}, u32[]{:S(2)}) collective-permute-start(bf16[4,128,128]{2,1,0:T(8,128)(2,1)} %get-tuple-element.47), channel_id=1, source_target_pairs={{16,0},{32,16},{48,32},{64,48},{80,64},{96,80},{112,96},{128,112},... | collective-permute-start | bytes 393224 | tf_op jit(solution)/shard_map/ppermute | solution.py:292
  162.4 17.2 %copy-start.10 = (bf16[4,128,128]{2,1,0:T(8,128)(2,1)}, bf16[4,128,128]{2,1,0:T(8,128)(2,1)S(1)}, u32[]{:S(2)}) copy-start(bf16[4,128,128]{2,1,0:T(8,128)(2,1)S(1)} %collective-permute-done.8.from_prev_hbm) | copy-start | bytes 393220
  166.1 13.5 %copy-start.11 = (bf16[4,128,128]{2,1,0:T(8,128)(2,1)}, bf16[4,128,128]{2,1,0:T(8,128)(2,1)S(1)}, u32[]{:S(2)}) copy-start(bf16[4,128,128]{2,1,0:T(8,128)(2,1)S(1)} %collective-permute-done.9.from_next_hbm) | copy-start | bytes 393220
